TPU v7x, 32 devices: a whole 2x2x4 slice. The times are simulated.
32 devices in a mesh: group: 2 (over y), tensor: 4 (over z), seq: 4 (over x, core).
Axes of the slice: x: 2, y: 2, z: 4, core: 2. Of those that a mesh axis runs over, the one named last changes fastest.
Arguments:
- tokens: bfloat16 [768, 8192], P(('group', 'seq'), 'tensor'), parts along dimension 0, may hold values from -6 to 6
- grad_out: bfloat16 [768, 8192], P(('group', 'seq'), 'tensor'), parts along dimension 0, may hold values from -6 to 6
- counts: int32 [8], P(('group', 'seq')), parts along dimension 0, may hold values from 1 to 96, 288 in all
- packing: int32 [768], P('group'), parts along dimension 0, may hold values from 0 to 383, each once
- gate_weight: bfloat16 [8192, 16384], P('seq', 'tensor'), may hold values from -0.0625 to 0.0625
- up_weight: bfloat16 [8192, 16384], P('seq', 'tensor'), may hold values from -0.0625 to 0.0625
- down_weight: bfloat16 [16384, 8192], P('tensor', 'seq'), may hold values from -0.0625 to 0.0625
Outputs:
- input_grad: bfloat16 [768, 8192], P(('group', 'tensor'), 'seq'), parts along dimension 0
There are 2 independent parts, one for each index of `group`. A program takes and returns all parts, laid end to end along the dimension named above; an argument that names none is the same for every part. Nothing has to cross between parts.
Inputs may be any that keep to these rules, and one draw needn't show every extreme that they name: `packing`: every arriving row index appears exactly once.
All inputs are finite; a program needn't handle non-finite values. No bound on the sum of `counts` on one device may be relied on, other than what follows from the above.
Results may differ from a plain program's by a relative error of at most 0.02.
Values may be sent and summed in bfloat16 or wider, within the bound.
No kernel may reach another device: no remote copies, remote signals or barrier semaphores. Data moves between devices by JAX's collectives and lax.ppermute only.
A program may use at most 192 MiB of HBM per device.

v0:
```python
import jax
import jax.numpy as jnp
from jax import lax
from jax.sharding import PartitionSpec as P


def derive(gate, up, hidden_grad):
    sig = jax.nn.sigmoid(gate)
    d_up = (hidden_grad * gate * sig).astype(jnp.bfloat16)
    d_gate = (hidden_grad * up * sig * (1.0 + gate * (1.0 - sig))).astype(jnp.bfloat16)
    return (d_gate, d_up)


def shards(tokens, grad_out, counts, packing, gate_weight, up_weight, down_weight):
    shard_rows = tokens.shape[0]
    alive_rows = jnp.arange(shard_rows, dtype=jnp.int32) < counts[0]
    masked = jnp.where(alive_rows[:, None], grad_out, jnp.zeros_like(grad_out))
    whole_tokens, whole_cotangent = (
        lax.all_gather(tokens, "tensor", axis=1, tiled=True),
        lax.all_gather(masked, "tensor", axis=1, tiled=True),
    )
    owned_tokens, owned_cotangent = (
        lax.all_to_all(whole_tokens, "seq", split_axis=1, concat_axis=0, tiled=True),
        lax.all_to_all(whole_cotangent, "seq", split_axis=1, concat_axis=0, tiled=True),
    )
    packed_tokens = jnp.take(owned_tokens, packing, axis=0)
    packed_cotangent = jnp.take(owned_cotangent, packing, axis=0)
    contract = (((1,), (1,)), ((), ()))
    gate_part = jnp.dot(packed_tokens, gate_weight, preferred_element_type=jnp.float32)
    up_part = jnp.dot(packed_tokens, up_weight, preferred_element_type=jnp.float32)
    hidden_part = lax.dot_general(
        packed_cotangent, down_weight, contract, preferred_element_type=jnp.float32
    )
    gate, up, hidden_grad = (
        lax.psum(gate_part.astype(jnp.bfloat16), "seq").astype(jnp.float32),
        lax.psum(up_part.astype(jnp.bfloat16), "seq").astype(jnp.float32),
        lax.psum(hidden_part.astype(jnp.bfloat16), "seq").astype(jnp.float32),
    )
    d_gate, d_up = derive(gate, up, hidden_grad)
    result = lax.dot_general(d_gate, gate_weight, contract, preferred_element_type=jnp.float32)
    return lax.psum_scatter(
        (
            result + lax.dot_general(d_up, up_weight, contract, preferred_element_type=jnp.float32)
        ).astype(jnp.bfloat16),
        "tensor",
        scatter_dimension=0,
        tiled=True,
    )


def solution(mesh):
    placed = (
        P(("group", "seq"), "tensor"),
        P(("group", "seq"), "tensor"),
        P(("group", "seq")),
        P("group"),
        P("seq", "tensor"),
        P("seq", "tensor"),
        P("tensor", "seq"),
    )
    return jax.shard_map(
        shards, mesh=mesh, in_specs=placed, out_specs=P(("group", "tensor"), "seq"), check_vma=False
    )
```

profile of v0, /device:TPU:0, one launch (start us, length us, event | category | flops | bytes accessed | tf_op | source)
XLA Modules:
  0.0 394.6 jit_solution(3636978745372393139)
XLA Ops:
  6.5 0.0 all-gather.5.cloned.1.call-start
  6.5 0.7 all-gather.5.cloned.1.call-update
  7.3 0.0 all-gather.3.cloned.1.call-start
  8.0 1.8 broadcast_select_fusion.3
  9.8 0.0 all-gather.3.cloned.1.call-update
  9.8 38.9 %all-gather.5.cloned.1.call-done = bf16[96,8192]{1,0:T(8,128)(2,1)} async-done(((bf16[96,2048]{1,0:T(8,128)(2,1)}), bf16[96,8192]{1,0:T(8,128)(2,1)}) %all-gather.5.cloned.1.call-update) | async-done | bytes 1572880 | tf_op jit(solution)/shard_map/all_gather | solution.py:19
  48.8 2.7 copy.14
  51.5 3.6 all-to-all-start.1
  55.1 31.3 %all-gather.3.cloned.1.call-done = bf16[96,8192]{1,0:T(8,128)(2,1)} async-done(((bf16[96,2048]{1,0:T(8,128)(2,1)}), bf16[96,8192]{1,0:T(8,128)(2,1)}) %all-gather.3.cloned.1.call-update) | async-done | bytes 1572880 | tf_op jit(solution)/shard_map/all_gather | solution.py:20
  86.3 0.0 copy-start.2
  86.3 2.8 copy.15
  89.1 0.0 all-to-all-done.1
  89.1 3.6 all-to-all-start
  92.6 0.0 all-reduce.3.cloned.1.call-start
  92.7 0.0 copy-done.2
  92.7 3.1 gather_fusion.1
  95.9 16.8 %all-to-all-done = bf16[96,4,2048]{2,0,1:T(8,128)(2,1)S(1)} async-done(((bf16[96,4,2048]{2,0,1:T(8,128)(2,1)}), bf16[96,4,2048]{2,0,1:T(8,128)(2,1)S(1)}, u32[]{:S(2)}, u32[]{:S(2)}) %all-to-all-start) | async-done | bytes 1572896 | tf_op jit(solution)/shard_map/all_to_all | solution.py:24
  112.7 3.1 gather_fusion
  115.8 0.0 copy-done
  115.8 11.7 %convolution_convert_fusion = bf16[384,4096]{1,0:T(8,128)(2,1)} fusion(bf16[2048,4096]{1,0:T(8,128)(2,1)} %param.13, bf16[384,2048]{1,0:T(8,128)(2,1)S(1)} %copy-done, pred[384]{0:T(512)(128)(4,1)S(1)} %compare_and_fusion), kind=kOutput, calls=%fused_computation.15 | convolution fusion | flops 6444810240 | bytes 21496192 | tf_op jit(solution)/shard_map/dot_general | solution.py:29
  127.5 0.0 copy-start.1
  127.5 11.8 %convolution_convert_fusion.1 = bf16[384,4096]{1,0:T(8,128)(2,1)} fusion(bf16[2048,4096]{1,0:T(8,128)(2,1)} %param.14, bf16[384,2048]{1,0:T(8,128)(2,1)S(1)} %copy-done, pred[384]{0:T(512)(128)(4,1)S(1)} %compare_and_fusion), kind=kOutput, calls=%fused_computation.16 | convolution fusion | flops 6444810240 | bytes 21496192 | tf_op jit(solution)/shard_map/dot_general | solution.py:30
  139.3 0.0 copy-done.1
  139.3 11.6 %convolution_convert_fusion.2 = bf16[384,4096]{1,0:T(8,128)(2,1)} fusion(bf16[4096,2048]{1,0:T(8,128)(2,1)} %param.15, bf16[384,2048]{1,0:T(8,128)(2,1)S(1)} %copy-done.1, pred[384]{0:T(512)(128)(4,1)S(1)} %compare_and_fusion), kind=kOutput, calls=%fused_computation.17 | convolution fusion | flops 6444810240 | bytes 21496192 | tf_op jit(solution)/shard_map/dot_general | solution.py:31
  151.0 0.0 all-reduce.3.cloned.1.call-update
  151.0 0.2 reduce-scatter.2.cloned.1.call-start
  151.2 168.4 %all-reduce.3.cloned.1.call-done = (bf16[384,4096]{1,0:T(8,128)(2,1)}, bf16[384,4096]{1,0:T(8,128)(2,1)}, bf16[384,4096]{1,0:T(8,128)(2,1)}) async-done(((bf16[384,4096]{1,0:T(8,128)(2,1)}, bf16[384,4096]{1,0:T(8,128)(2,1)}, bf16[384,4096]{1,0:T(8,128)(2,1)}), (bf16[384,4096]{1,0:T(8,128)(2,1)}, bf16[384,4096]{1,0:T(8,128)(2,1)}, bf16[384,4096]{1,0:T(8,128)(2,1)})) %all-reduce.3.cloned.1.call-update) | async-done | bytes 9437200 | tf_op jit(solution)/shard_map/psum | solution.py:35
  319.6 16.2 %fusion.9 = f32[384,2048]{1,0:T(8,128)} fusion(bf16[2048,4096]{1,0:T(8,128)(2,1)} %param.14, bf16[384,4096]{1,0:T(8,128)(2,1)} %get-tuple-element.6, bf16[384,4096]{1,0:T(8,128)(2,1)} %get-tuple-element.7), kind=kOutput, calls=%fused_computation.18 | convolution fusion | flops 6455033856 | bytes 26214400 | tf_op jit(solution)/shard_map/dot_general | solution.py:43
  335.9 0.0 copy-done.3
  335.9 16.6 %add_convert_fusion = bf16[384,2048]{1,0:T(8,128)(2,1)} fusion(f32[384,2048]{1,0:T(8,128)} %fusion.9, bf16[2048,4096]{1,0:T(8,128)(2,1)} %param.13, bf16[384,4096]{1,0:T(8,128)(2,1)} %get-tuple-element.7, bf16[384,4096]{1,0:T(8,128)(2,1)S(1)} %copy-done.3, bf16[384,4096]{1,0:T(8,128)(2,1)} %get-tuple-element.8), kind=kOutput, calls=%fused_computation.20 | convolution fusion | flops 6464471040 | bytes 30932992 | tf_op jit(solution)/shard_map/dot_general | solution.py:40
  352.4 0.0 reduce-scatter.2.cloned.1.call-update
  352.5 35.6 %reduce-scatter.2.cloned.1.call-done = bf16[96,2048]{1,0:T(8,128)(2,1)} async-done(((bf16[384,2048]{1,0:T(8,128)(2,1)}), bf16[96,2048]{1,0:T(8,128)(2,1)}) %reduce-scatter.2.cloned.1.call-update) | async-done | bytes 393232 | tf_op jit(solution)/shard_map/reduce_scatter | solution.py:41
  (6 shorter events, 0.0 us)
Async XLA Ops:
  6.5 42.2 %all-gather.5.cloned.1.call-start = ((), (), s32[]{:S(2)}) async-start(), calls=%async_computation.4 | async-start | bytes 1966080 | tf_op jit(solution)/shard_map/all_gather | solution.py:19
  7.3 79.1 %all-gather.3.cloned.1.call-start = ((), (), s32[]{:S(2)}) async-start(), calls=%async_computation.3 | async-start | bytes 1966080 | tf_op jit(solution)/shard_map/all_gather | solution.py:20
  51.5 37.6 %all-to-all-start.1 = ((bf16[96,4,2048]{2,0,1:T(8,128)(2,1)}), bf16[96,4,2048]{2,0,1:T(8,128)(2,1)S(1)}, u32[]{:S(2)}, u32[]{:S(2)}) async-start(bf16[96,4,2048]{2,0,1:T(8,128)(2,1)} %bitcast.18), calls=%async_computation.1 | async-start | bytes 3145728 | tf_op jit(solution)/shard_map/all_to_all | solution.py:23
  86.3 6.4 %copy-start.2 = (s32[384]{0:T(512)S(1)}, s32[384]{0:T(512)}, u32[]{:S(2)}) copy-start(s32[384]{0:T(512)} %param.12) | copy-start | bytes 4612
  89.1 23.6 %all-to-all-start = ((bf16[96,4,2048]{2,0,1:T(8,128)(2,1)}), bf16[96,4,2048]{2,0,1:T(8,128)(2,1)S(1)}, u32[]{:S(2)}, u32[]{:S(2)}) async-start(bf16[96,4,2048]{2,0,1:T(8,128)(2,1)} %bitcast.23), calls=%async_computation | async-start | bytes 3145728 | tf_op jit(solution)/shard_map/all_to_all | solution.py:24
  92.6 227.0 %all-reduce.3.cloned.1.call-start = ((), (), s32[]{:S(2)}) async-start(), calls=%async_computation.6 | async-start | bytes 18874368 | tf_op jit(solution)/shard_map/psum | solution.py:35
  112.7 3.1 copy-start
  127.5 11.8 %copy-start.1 = (bf16[384,2048]{1,0:T(8,128)(2,1)S(1)}, bf16[384,2048]{1,0:T(8,128)(2,1)}, u32[]{:S(2)}) copy-start(bf16[384,2048]{1,0:T(8,128)(2,1)} %gather_fusion) | copy-start | bytes 4718596
  151.0 237.1 %reduce-scatter.2.cloned.1.call-start = ((), (), s32[]{:S(2)}) async-start(), calls=%async_computation.5 | async-start | bytes 1966080 | tf_op jit(solution)/shard_map/reduce_scatter | solution.py:41
  319.6 16.2 %copy-start.3 = (bf16[384,4096]{1,0:T(8,128)(2,1)S(1)}, bf16[384,4096]{1,0:T(8,128)(2,1)}, u32[]{:S(2)}) copy-start(bf16[384,4096]{1,0:T(8,128)(2,1)} %get-tuple-element.6) | copy-start | bytes 9437188
Sparse Core Ops, SparseCore 0:
  8.9 39.7 all-gather.4
  50.3 35.9 all-gather.2
  151.1 168.4 all-reduce.2
  352.6 35.4 reduce-scatter.1
where the time goes:
time: 395 us
  waiting for transfers between devices  292 us (74%)
  matrix products  67.9 us (17%)
  between operations  13.8 us (3%)
  local copies, waits for them, and re-layouts  11.8 us (3%)
  starting transfers between devices  7.43 us (2%)
    psum x1, waiting for transfers between devices, shards(): lax.psum(gate_part.astype(jnp.bfloat16), 'seq').astype(jnp.float32)  168 us
    all_gather x1, waiting for transfers between devices, shards(): lax.all_gather(tokens, 'tensor', axis=1, tiled=True)  38.9 us
    reduce_scatter x1, waiting for transfers between devices, shards(): lax.psum_scatter((result + lax.dot_general(d_up, up_weight, contract, pre...  35.6 us
    all_gather x1, waiting for transfers between devices, shards(): lax.all_gather(masked, 'tensor', axis=1, tiled=True)  31.3 us
    all_to_all x1, waiting for transfers between devices, shards(): lax.all_to_all(whole_cotangent, 'seq', split_axis=1, concat_axis=0, tiled...  16.8 us
    dot_general x1, matrix products, shards(): lax.dot_general(d_gate, gate_weight, contract, preferred_element_type=jnp...  16.6 us
    dot_general x1, matrix products, shards(): lax.dot_general(d_up, up_weight, contract, preferred_element_type=jnp.flo...  16.2 us
    dot_general x1, matrix products, shards(): jnp.dot(packed_tokens, up_weight, preferred_element_type=jnp.float32)  11.8 us
  transfers between devices with their start and end apart: 6, of which 5 were waited for; matrix products, arithmetic and copies ran while one was open for 3% of the time, Pallas kernels for 0%

commit v1 on v0

v1 whole, which is shorter than its diff:
```python
import functools
import jax
import jax.numpy as jnp
from jax import lax
from jax.experimental import pallas as pl
from jax.experimental.pallas import tpu as pltpu
from jax.sharding import PartitionSpec as P

BF, F32 = jnp.bfloat16, jnp.float32
ROW_CONTRACT = (((1,), (1,)), ((), ()))
VMEM = 56 * 1024 * 1024


def derive(gate, up, hidden_grad):
    sig = jax.nn.sigmoid(gate)
    d_up = (hidden_grad * gate * sig).astype(BF)
    d_gate = (hidden_grad * up * sig * (1.0 + gate * (1.0 - sig))).astype(BF)
    return (d_gate, d_up)


def general(tokens, grad_out, counts, packing, gate_weight, up_weight, down_weight):
    shard_rows = tokens.shape[0]
    alive_rows = jnp.arange(shard_rows, dtype=jnp.int32) < counts[0]
    masked = jnp.where(alive_rows[:, None], grad_out, jnp.zeros_like(grad_out))
    whole_tokens, whole_cotangent = (
        lax.all_gather(tokens, "tensor", axis=1, tiled=True),
        lax.all_gather(masked, "tensor", axis=1, tiled=True),
    )
    owned_tokens, owned_cotangent = (
        lax.all_to_all(whole_tokens, "seq", split_axis=1, concat_axis=0, tiled=True),
        lax.all_to_all(whole_cotangent, "seq", split_axis=1, concat_axis=0, tiled=True),
    )
    packed_tokens = jnp.take(owned_tokens, packing, axis=0)
    packed_cotangent = jnp.take(owned_cotangent, packing, axis=0)
    gate_part = jnp.dot(packed_tokens, gate_weight, preferred_element_type=F32)
    up_part = jnp.dot(packed_tokens, up_weight, preferred_element_type=F32)
    hidden_part = lax.dot_general(
        packed_cotangent, down_weight, ROW_CONTRACT, preferred_element_type=F32
    )
    gate, up, hidden_grad = (
        lax.psum(gate_part.astype(BF), "seq").astype(F32),
        lax.psum(up_part.astype(BF), "seq").astype(F32),
        lax.psum(hidden_part.astype(BF), "seq").astype(F32),
    )
    d_gate, d_up = derive(gate, up, hidden_grad)
    result = lax.dot_general(d_gate, gate_weight, ROW_CONTRACT, preferred_element_type=F32)
    return lax.psum_scatter(
        (result + lax.dot_general(d_up, up_weight, ROW_CONTRACT, preferred_element_type=F32)).astype(BF),
        "tensor",
        scatter_dimension=0,
        tiled=True,
    )


def slot_block(slot, half, ids, per_half):
    core, x = ids[0], ids[1]
    which_core = jnp.where(slot % 2 == 0, 1 - core, core)
    which_x = jnp.where(slot // 2 == 0, 1 - x, x)
    return half * per_half + 2 * which_core + which_x


def pick(select_ref, parts, rows_ref):
    width = parts[0].shape[0]
    total = jnp.dot(select_ref[:, :width], parts[0][...], preferred_element_type=F32)
    for k in range(1, len(parts)):
        total += jnp.dot(select_ref[:, k * width:(k + 1) * width], parts[k][...], preferred_element_type=F32)
    rows_ref[...] = total.astype(BF)


def gate_up_kernel(ids, select_ref, p0, p1, p2, p3, gate_ref, up_ref, send_ref, keep_ref, rows_ref):
    slot = pl.program_id(0)

    @pl.when(slot == 0)
    def _():
        pick(select_ref, (p0, p1, p2, p3), rows_ref)

    gate = jnp.dot(rows_ref[...], gate_ref[...], preferred_element_type=F32).astype(BF)
    up = jnp.dot(rows_ref[...], up_ref[...], preferred_element_type=F32).astype(BF)

    @pl.when(slot % 2 == 0)
    def _():
        send_ref[0, 0] = gate
        send_ref[0, 1] = up

    @pl.when(slot % 2 == 1)
    def _():
        keep_ref[0, 0] = gate
        keep_ref[0, 1] = up


def gate_up(half, ids, select, parts, gate_weight, up_weight, block):
    rows, depth = select.shape[0], gate_weight.shape[0]
    whole = lambda a: pl.BlockSpec(a.shape, lambda j, ids: (0,) * a.ndim)
    weight = pl.BlockSpec((depth, block), lambda j, ids: (0, slot_block(j, half, ids, 4)))
    out = pl.BlockSpec((1, 2, rows, block), lambda j, ids: (j // 2, 0, 0, 0))
    return pl.pallas_call(
        gate_up_kernel,
        grid_spec=pltpu.PrefetchScalarGridSpec(
            num_scalar_prefetch=1,
            grid=(4,),
            in_specs=[whole(select)] + [whole(p) for p in parts] + [weight, weight],
            out_specs=[out, out],
            scratch_shapes=[pltpu.VMEM((rows, depth), BF)],
        ),
        out_shape=[jax.ShapeDtypeStruct((2, 2, rows, block), BF)] * 2,
        compiler_params=pltpu.CompilerParams(vmem_limit_bytes=VMEM),
        cost_estimate=pl.CostEstimate(flops=16 * rows * depth * block, bytes_accessed=16 * depth * block, transcendentals=0),
    )(ids, select, *parts, gate_weight, up_weight)


def hidden_kernel(ids, select_ref, p0, p1, p2, p3, down_ref, send_a, send_b, keep_a, keep_b, rows_ref):
    step = pl.program_id(0)
    rows = send_a.shape[2]

    @pl.when(step == 0)
    def _():
        pick(select_ref, (p0, p1, p2, p3), rows_ref)

    hidden = lax.dot_general(rows_ref[...], down_ref[...], ROW_CONTRACT, preferred_element_type=F32).astype(BF)

    @pl.when((step // 2) % 2 == 0)
    def _():
        send_a[0, 0] = hidden[:rows]
        send_b[0, 0] = hidden[rows:]

    @pl.when((step // 2) % 2 == 1)
    def _():
        keep_a[0, 0] = hidden[:rows]
        keep_b[0, 0] = hidden[rows:]


def hidden_grads(ids, select, parts, down_weight, block):
    rows, depth = select.shape[0] // 2, down_weight.shape[1]
    whole = lambda a: pl.BlockSpec(a.shape, lambda j, ids: (0,) * a.ndim)
    weight = pl.BlockSpec((block, depth), lambda j, ids: (slot_block(j // 2, j % 2, ids, 4), 0))

    def sent(j, ids):
        return (j // 4, jnp.where((j // 2) % 2 == 0, j % 2, 1), 0, 0)

    def kept(j, ids):
        slot = j // 2
        return (jnp.where(slot == 3, 1, 0), jnp.where(slot == 0, 0, jnp.where(slot == 2, 1, j % 2)), 0, 0)

    out = lambda place: pl.BlockSpec((1, 1, rows, block), place)
    return pl.pallas_call(
        hidden_kernel,
        grid_spec=pltpu.PrefetchScalarGridSpec(
            num_scalar_prefetch=1,
            grid=(8,),
            in_specs=[whole(select)] + [whole(p) for p in parts] + [weight],
            out_specs=[out(sent), out(sent), out(kept), out(kept)],
            scratch_shapes=[pltpu.VMEM((2 * rows, depth), BF)],
        ),
        out_shape=[jax.ShapeDtypeStruct((2, 2, rows, block), BF)] * 4,
        compiler_params=pltpu.CompilerParams(vmem_limit_bytes=VMEM),
        cost_estimate=pl.CostEstimate(flops=32 * rows * depth * block, bytes_accessed=16 * depth * block, transcendentals=0),
    )(ids, select, *parts, down_weight)


def back_step(mine, other, gate_ref, up_ref, acc, first):
    step = pl.program_id(0)

    def add(source):
        term = lax.dot_general(source[0, step % 2], gate_ref[...], ROW_CONTRACT, preferred_element_type=F32)
        return term + lax.dot_general(source[1, step % 2], up_ref[...], ROW_CONTRACT, preferred_element_type=F32)

    @pl.when(step == 0)
    def _():
        acc[...] = add(mine) if first is None else first[...] + add(mine)

    @pl.when(step == 1)
    def _():
        acc[...] += add(mine)

    @pl.when(step >= 2)
    def _():
        acc[...] += add(other)


def near_kernel(ids, mine, other, gate_ref, up_ref, acc):
    back_step(mine, other, gate_ref, up_ref, acc, None)


def far_kernel(ids, mine, other, gate_ref, up_ref, first, place_ref, o0, o1, o2, o3, acc):
    back_step(mine, other, gate_ref, up_ref, acc, first)

    @pl.when(pl.program_id(0) == 3)
    def _():
        rounded = acc[...].astype(BF)
        for k, out in enumerate((o0, o1, o2, o3)):
            out[...] = jnp.dot(place_ref[k], rounded, preferred_element_type=F32).astype(BF)


def back(far, ids, mine, other, gate_weight, up_weight, block, first=None, place=None):
    rows, depth = mine.shape[2], gate_weight.shape[0]
    whole = lambda a: pl.BlockSpec(a.shape, lambda j, ids: (0,) * a.ndim)

    def spot(j, ids):
        core = jnp.where(j // 2 == 0, ids[0], 1 - ids[0])
        return (0, (j % 2) * 4 + 2 * core + (1 - ids[1] if far else ids[1]))

    weight = pl.BlockSpec((depth, block), spot)
    specs = [whole(mine), whole(other), weight, weight]
    args = (mine, other, gate_weight, up_weight)
    flops = 16 * rows * depth * block
    cost = pl.CostEstimate(flops=flops, bytes_accessed=16 * depth * block, transcendentals=0)
    params = pltpu.CompilerParams(vmem_limit_bytes=VMEM)
    acc = (rows, depth)
    if not far:
        return pl.pallas_call(
            near_kernel,
            grid_spec=pltpu.PrefetchScalarGridSpec(
                num_scalar_prefetch=1, grid=(4,), in_specs=specs,
                out_specs=pl.BlockSpec(acc, lambda j, ids: (0, 0)),
            ),
            out_shape=jax.ShapeDtypeStruct(acc, F32),
            compiler_params=params,
            cost_estimate=cost,
        )(ids, *args)
    piece = (place.shape[1], depth)
    return pl.pallas_call(
        far_kernel,
        grid_spec=pltpu.PrefetchScalarGridSpec(
            num_scalar_prefetch=1, grid=(4,), in_specs=specs + [whole(first), whole(place)],
            out_specs=[pl.BlockSpec(piece, lambda j, ids: (0, 0))] * 4,
            scratch_shapes=[pltpu.VMEM(acc, F32)],
        ),
        out_shape=[jax.ShapeDtypeStruct(piece, BF)] * 4,
        compiler_params=params,
        cost_estimate=cost,
    )(ids, *args, first, place)


def after(value, *others):
    return lax.optimization_barrier((value,) + others)[0]


def tuned(n, tokens, grad_out, counts, packing, gate_weight, up_weight, down_weight):
    shard_rows, depth = tokens.shape
    rows = packing.shape[0]
    live_rows = rows * 3 // 4
    sets, hidden = 2, gate_weight.shape[1]
    block = hidden // 8
    set_rows, piece = live_rows // sets, shard_rows // sets
    t, s = lax.axis_index("tensor"), lax.axis_index("seq")
    core, x = s % 2, s // 2
    ids = jnp.stack([core, x]).astype(jnp.int32)
    sibling = [(i, i ^ 1) for i in range(n)]
    across = [(i, i ^ 2) for i in range(n)]

    def spread(value, k):
        pairs = [(a * n + b, ((b + k) % n) * n + a) for a in range(n) for b in range(n)]
        return lax.ppermute(value, ("tensor", "seq"), pairs)

    token_parts = [spread(tokens, k) for k in range(n)]
    held = after(grad_out, *token_parts)
    grad_parts = [spread(held, k) for k in range(n)]

    all_counts = lax.all_gather(counts, "seq", tiled=True)
    home, place_in = packing // shard_rows, packing % shard_rows
    bound = jnp.sum(jnp.where(home[:, None] == jnp.arange(n)[None, :], all_counts[None, :], 0), axis=1)
    alive = place_in < bound
    order = jnp.arange(rows, dtype=jnp.int32)
    rank = jnp.sum(jnp.where(order[None, :] < order[:, None], alive[None, :].astype(jnp.int32), 0), axis=1)
    index = jnp.where(alive, (rank % sets) * set_rows + rank // sets, -1)
    slot = jnp.arange(rows, dtype=jnp.int32)
    arriving = ((t - slot // shard_rows) % n) * shard_rows + slot % shard_rows
    to_row = (index[None, :] == jnp.arange(live_rows, dtype=jnp.int32)[:, None]).astype(BF)
    from_slot = (packing[:, None] == arriving[None, :]).astype(BF)
    select = jnp.dot(to_row, from_slot, preferred_element_type=F32).astype(BF)
    before = jnp.sum(
        jnp.where(order[None, :] < (jnp.arange(n) * shard_rows)[:, None], alive[None, :].astype(jnp.int32), 0), axis=1
    )
    begin = jnp.stack([(before + sets - 1 - m) // sets for m in range(sets)])
    target = (t + jnp.arange(n)) % n
    target_begin = jnp.sum(
        jnp.where(target[None, :, None] == jnp.arange(n)[None, None, :], begin[:, None, :], 0), axis=2
    )
    place = (
        target_begin[:, :, None, None] + jnp.arange(piece)[None, None, :, None]
        == jnp.arange(set_rows)[None, None, None, :]
    ).astype(BF)
    own = (order // shard_rows == t)
    mine_rank = jnp.sum(jnp.where((order[None, :] == t * shard_rows + jnp.arange(shard_rows)[:, None]),
                                  jnp.where(alive, rank, -1)[None, :], 0), axis=1)
    spot = jnp.where(mine_rank >= 0, (mine_rank % sets) * piece + mine_rank // sets
                     - jnp.where(mine_rank % sets == 0, target_begin[0, 0], target_begin[1, 0]), -1)
    final = (spot[:, None] == jnp.arange(sets * piece)[None, :]).astype(BF)

    gates, ups = [], []
    for half in range(2):
        send, keep = gate_up(half, ids, select, token_parts, gate_weight, up_weight, block)
        got = lax.ppermute(send, "seq", sibling)
        far = (keep[0].astype(F32) + got[0].astype(F32)).astype(BF)
        far_got = lax.ppermute(far, "seq", across)
        near = keep[1].astype(F32) + got[1].astype(F32) + far_got.astype(F32)
        gates.append(near[0])
        ups.append(near[1])

    outs = hidden_grads(ids, select, grad_parts, down_weight, block)
    pieces = []
    for m in range(sets):
        send, keep = outs[m], outs[2 + m]
        got = lax.ppermute(send, "seq", sibling)
        far = (keep[0].astype(F32) + got[0].astype(F32)).astype(BF)
        far_got = lax.ppermute(far, "seq", across)
        hid = keep[1].astype(F32) + got[1].astype(F32) + far_got.astype(F32)
        part = slice(m * set_rows, (m + 1) * set_rows)
        gate = jnp.stack([g[part] for g in gates])
        up = jnp.stack([u[part] for u in ups])
        d = jnp.stack(derive(gate, up, hid))
        d_core = lax.ppermute(d, "seq", sibling)
        d_far = lax.ppermute(d, "seq", across)
        d_both = lax.ppermute(d_far, "seq", sibling)
        first = back(False, ids, d, d_core, gate_weight, up_weight, block)
        parts = back(True, ids, d_far, d_both, gate_weight, up_weight, block, first, place[m])
        total = parts[0].astype(F32)
        for k in range(1, n):
            shift = [(i, (i + k) % n) for i in range(n)]
            total += lax.ppermute(parts[k], "tensor", shift).astype(F32)
        pieces.append(total.astype(BF))
    return jnp.dot(final, jnp.concatenate(pieces), preferred_element_type=F32).astype(BF)


def solution(mesh):
    placed = (
        P(("group", "seq"), "tensor"),
        P(("group", "seq"), "tensor"),
        P(("group", "seq")),
        P("group"),
        P("seq", "tensor"),
        P("seq", "tensor"),
        P("tensor", "seq"),
    )
    if mesh.shape["tensor"] == 4 and mesh.shape["seq"] == 4:
        body = functools.partial(tuned, 4)
    else:
        body = general
    return jax.shard_map(
        body, mesh=mesh, in_specs=placed, out_specs=P(("group", "tensor"), "seq"), check_vma=False
    )
```

time: 395 us -> 248 us (0.63)
  waiting for transfers between devices: 292 us -> 78.6 us
  Pallas kernels: 0 us -> 87.8 us
  matrix products: 67.9 us -> 2.88 us
  starting transfers between devices: 7.43 us -> 55.9 us
  between operations: 13.8 us -> 0.99 us
  blocking collectives: 0 us -> 5.96 us
  other arithmetic: 1.86 us -> 7.09 us
    psum x1 -> x0, waiting for transfers between devices: 168 us -> none  [shards(): lax.psum(gate_part.astype(jnp.bfloat16), 'seq').astype(jnp.float32)]
    pallas_call x0 -> x7, Pallas kernels: none -> 87.8 us  [the longest x2 26.2 us: gate_up(): pl.pallas_call(gate_up_kernel, grid_spec=pltpu.PrefetchScalarGridSpec(num...]
    ppermute x0 -> x28, waiting for transfers between devices: none -> 78.6 us  [the longest x4 34.5 us: tuned(): far_got = lax.ppermute(far, 'seq', across)]
    all_gather x2 -> x0, waiting for transfers between devices: 70.2 us -> none  [the longest x1 38.9 us: shards(): lax.all_gather(tokens, 'tensor', axis=1, tiled=True)]
    dot_general x5 -> x2, matrix products: 67.9 us -> 2.88 us  [the longest x1 1.81 us: tuned(): select = jnp.dot(to_row, from_slot, preferred_element_type=F32).astype(BF)]
    ppermute x0 -> x28, starting transfers between devices: none -> 55.9 us  [the longest x8 33.5 us: spread(): return lax.ppermute(value, ('tensor', 'seq'), pairs)]
    reduce_scatter x1 -> x0, waiting for transfers between devices: 35.6 us -> none  [shards(): lax.psum_scatter((result + lax.dot_general(d_up, up_weight, contract, pre...]
    all_to_all x2 -> x0, waiting for transfers between devices: 16.8 us -> none  [the longest x1 16.8 us: shards(): lax.all_to_all(whole_cotangent, 'seq', split_axis=1, concat_axis=0, tiled...]
  transfers between devices with their start and end apart: 6 -> 28, of which waited for: 5 -> 9; matrix products, arithmetic and copies ran while one was open for 3% -> 5% of each run, Pallas kernels for 0% -> 35%
where the time goes in v1:
time: 248 us
  Pallas kernels  87.8 us (35%)
  waiting for transfers between devices  78.6 us (32%)
  starting transfers between devices  55.9 us (23%)
  local copies, waits for them, and re-layouts  8.42 us (3%)
  other arithmetic  7.09 us (3%)
  blocking collectives  5.96 us (2%)
  matrix products  2.88 us (1%)
    ppermute x4, waiting for transfers between devices, tuned(): far_got = lax.ppermute(far, 'seq', across)  34.5 us
    ppermute x8, starting transfers between devices, spread(): return lax.ppermute(value, ('tensor', 'seq'), pairs)  33.5 us
    pallas_call x2, Pallas kernels, gate_up(): pl.pallas_call(gate_up_kernel, grid_spec=pltpu.PrefetchScalarGridSpec(num...  26.2 us
    pallas_call x2, Pallas kernels, back(): pl.pallas_call(far_kernel, grid_spec=pltpu.PrefetchScalarGridSpec(num_sca...  24 us
    pallas_call x2, Pallas kernels, back(): pl.pallas_call(near_kernel, grid_spec=pltpu.PrefetchScalarGridSpec(num_sc...  22.7 us
    ppermute x2, waiting for transfers between devices, tuned(): d_far = lax.ppermute(d, 'seq', across)  20 us
    ppermute x6, waiting for transfers between devices, tuned(): total += lax.ppermute(parts[k], 'tensor', shift).astype(F32)  17.1 us
    pallas_call x1, Pallas kernels, hidden_grads(): pl.pallas_call(hidden_kernel, grid_spec=pltpu.PrefetchScalarGridSpec(num_...  14.9 us
  transfers between devices with their start and end apart: 28, of which 9 were waited for; matrix products, arithmetic and copies ran while one was open for 5% of the time, Pallas kernels for 35%

profile of v1, /device:TPU:0, one launch (start us, length us, event | category | flops | bytes accessed | tf_op | source)
XLA Modules:
  0.0 247.6 jit_solution(17845768292193766954)
XLA Ops:
  0.0 1.6 collective-permute-start
  1.6 3.4 %collective-permute-start.1 = (bf16[96,2048]{1,0:T(8,128)(2,1)}, bf16[96,2048]{1,0:T(8,128)(2,1)S(1)}, u32[]{:S(2)}, u32[]{:S(2)}) collective-permute-start(bf16[96,2048]{1,0:T(8,128)(2,1)} %param.7), channel_id=1, source_target_pairs={{0,4},{1,8},{2,12},{3,0},{4,5},{5,9},{6,13},{7,1},{8,6},{9,10},{10... | collective-permute-start | bytes 1179656 | tf_op jit(solution)/shard_map/ppermute | solution.py:253
  5.0 3.4 %collective-permute-start.2 = (bf16[96,2048]{1,0:T(8,128)(2,1)}, bf16[96,2048]{1,0:T(8,128)(2,1)S(1)}, u32[]{:S(2)}, u32[]{:S(2)}) collective-permute-start(bf16[96,2048]{1,0:T(8,128)(2,1)} %param.7), channel_id=1, source_target_pairs={{0,8},{1,12},{2,0},{3,4},{4,9},{5,13},{6,1},{7,5},{8,10},{9,14},{1... | collective-permute-start | bytes 1179656 | tf_op jit(solution)/shard_map/ppermute | solution.py:253
  8.4 2.6 %collective-permute-start.3 = (bf16[96,2048]{1,0:T(8,128)(2,1)}, bf16[96,2048]{1,0:T(8,128)(2,1)S(1)}, u32[]{:S(2)}, u32[]{:S(2)}) collective-permute-start(bf16[96,2048]{1,0:T(8,128)(2,1)} %param.7), channel_id=1, source_target_pairs={{0,12},{1,0},{2,4},{3,8},{4,13},{5,1},{6,5},{7,9},{8,14},{9,2},{10... | collective-permute-start | bytes 1179656 | tf_op jit(solution)/shard_map/ppermute | solution.py:253
  11.7 1.2 dynamic-slice
  13.7 6.0 %all-reduce = s32[4]{0:T(128)S(1)} all-reduce(s32[4]{0:T(128)S(1)} %dynamic-update-slice), channel_id=1, replica_groups=mesh['group'=2,'tensor'=4,'seq'=4] {'seq'}, use_global_device_ids=true, to_apply=%add | all-reduce | flops 4 | bytes 32
  22.2 1.8 convolution_convert_fusion.1.select_ref
  24.0 7.0 %collective-permute-done.3.p3 = bf16[96,2048]{1,0:T(8,128)(2,1)S(1)} collective-permute-done((bf16[96,2048]{1,0:T(8,128)(2,1)}, bf16[96,2048]{1,0:T(8,128)(2,1)S(1)}, u32[]{:S(2)}, u32[]{:S(2)}) %collective-permute-start.3) | collective-permute-done | bytes 393248 | tf_op jit(solution)/shard_map/ppermute | solution.py:253
  31.1 1.6 collective-permute-start.4
  32.7 11.5 %collective-permute-start.5 = (bf16[96,2048]{1,0:T(8,128)(2,1)}, bf16[96,2048]{1,0:T(8,128)(2,1)S(1)}, u32[]{:S(2)}, u32[]{:S(2)}) collective-permute-start(bf16[96,2048]{1,0:T(8,128)(2,1)} %param.8), channel_id=1, source_target_pairs={{0,4},{1,8},{2,12},{3,0},{4,5},{5,9},{6,13},{7,1},{8,6},{9,10},{10... | collective-permute-start | bytes 1179656 | tf_op jit(solution)/shard_map/ppermute | solution.py:253
  44.2 8.8 %collective-permute-start.6 = (bf16[96,2048]{1,0:T(8,128)(2,1)}, bf16[96,2048]{1,0:T(8,128)(2,1)S(1)}, u32[]{:S(2)}, u32[]{:S(2)}) collective-permute-start(bf16[96,2048]{1,0:T(8,128)(2,1)} %param.8), channel_id=1, source_target_pairs={{0,8},{1,12},{2,0},{3,4},{4,9},{5,13},{6,1},{7,5},{8,10},{9,14},{1... | collective-permute-start | bytes 1179656 | tf_op jit(solution)/shard_map/ppermute | solution.py:253
  53.5 13.1 %shard_map.75 = (bf16[2,2,288,512]{3,2,1,0:T(8,128)(2,1)}, bf16[2,2,288,512]{3,2,1,0:T(8,128)(2,1)}) custom-call(s32[2]{0:T(128)} %pad_add_fusion.1.ids, bf16[288,384]{1,0:T(8,128)(2,1)} %convolution_convert_fusion.1.select_ref, bf16[96,2048]{1,0:T(8,128)(2,1)} %copy-done.2, bf16[96,2048]{1,0:T(8,128)(2,1)} %copy-done.3, bf16[96,2048]{1,0:T(8,128)(2,1)} %copy-done.4, ...), custom_call_target="tpu_custom_call" | custom-call | flops 4831838208 | bytes 16777216 | tf_op jit(solution)/shard_map/pallas_call | solution.py:96
  66.7 13.1 %shard_map.74 = (bf16[2,2,288,512]{3,2,1,0:T(8,128)(2,1)}, bf16[2,2,288,512]{3,2,1,0:T(8,128)(2,1)}) custom-call(s32[2]{0:T(128)} %pad_add_fusion.1.ids, bf16[288,384]{1,0:T(8,128)(2,1)} %convolution_convert_fusion.1.select_ref, bf16[96,2048]{1,0:T(8,128)(2,1)} %copy-done.2, bf16[96,2048]{1,0:T(8,128)(2,1)} %copy-done.3, bf16[96,2048]{1,0:T(8,128)(2,1)} %copy-done.4, ...), custom_call_target="tpu_custom_call" | custom-call | flops 4831838208 | bytes 16777216 | tf_op jit(solution)/shard_map/pallas_call | solution.py:96
  82.2 14.9 %shard_map.73 = (bf16[2,2,144,512]{3,2,1,0:T(8,128)(2,1)}, bf16[2,2,144,512]{3,2,1,0:T(8,128)(2,1)}, bf16[2,2,144,512]{3,2,1,0:T(8,128)(2,1)}, bf16[2,2,144,512]{3,2,1,0:T(8,128)(2,1)}) custom-call(s32[2]{0:T(128)} %pad_add_fusion.1.ids, bf16[288,384]{1,0:T(8,128)(2,1)} %convolution_convert_fusion.1.select_ref, bf16[96,2048]{1,0:T(8,128)(2,1)} %copy-done.16, ...), custom_call_target="tpu_custom_call" | custom-call | flops 4831838208 | bytes 16777216 | tf_op jit(solution)/shard_map/pallas_call | solution.py:145
  98.0 1.4 collective-permute-start.13
  100.4 1.4 collective-permute-start.21
  102.7 11.6 %collective-permute-done.13 = bf16[2,288,512]{2,1,0:T(8,128)(2,1)S(1)} collective-permute-done((bf16[2,288,512]{2,1,0:T(8,128)(2,1)S(1)}, bf16[2,288,512]{2,1,0:T(8,128)(2,1)S(1)}, u32[]{:S(2)}, u32[]{:S(2)}) %collective-permute-start.13) | collective-permute-done | bytes 589856 | tf_op jit(solution)/shard_map/ppermute | solution.py:295
  114.5 12.4 %collective-permute-done.11 = bf16[2,288,512]{2,1,0:T(8,128)(2,1)S(1)} collective-permute-done((bf16[2,288,512]{2,1,0:T(8,128)(2,1)S(1)}, bf16[2,288,512]{2,1,0:T(8,128)(2,1)S(1)}, u32[]{:S(2)}, u32[]{:S(2)}) %collective-permute-start.11) | collective-permute-done | bytes 589856 | tf_op jit(solution)/shard_map/ppermute | solution.py:295
  127.3 5.9 %collective-permute-done.21 = bf16[2,144,512]{2,1,0:T(8,128)(2,1)S(1)} collective-permute-done((bf16[2,144,512]{2,1,0:T(8,128)(2,1)S(1)}, bf16[2,144,512]{2,1,0:T(8,128)(2,1)S(1)}, u32[]{:S(2)}, u32[]{:S(2)}) %collective-permute-start.21) | collective-permute-done | bytes 294944 | tf_op jit(solution)/shard_map/ppermute | solution.py:306
  133.7 1.4 collective-permute-start.22
  135.0 4.5 %collective-permute-done.9 = bf16[2,144,512]{2,1,0:T(8,128)(2,1)S(1)} collective-permute-done((bf16[2,144,512]{2,1,0:T(8,128)(2,1)S(1)}, bf16[2,144,512]{2,1,0:T(8,128)(2,1)S(1)}, u32[]{:S(2)}, u32[]{:S(2)}) %collective-permute-start.9) | collective-permute-done | bytes 294944 | tf_op jit(solution)/shard_map/ppermute | solution.py:306
  140.0 1.4 collective-permute-start.14
  142.8 9.4 %collective-permute-done.22.mine = bf16[2,2,144,512]{3,2,1,0:T(8,128)(2,1)S(1)} collective-permute-done((bf16[2,2,144,512]{3,2,1,0:T(8,128)(2,1)S(1)}, bf16[2,2,144,512]{3,2,1,0:T(8,128)(2,1)S(1)}, u32[]{:S(2)}, u32[]{:S(2)}) %collective-permute-start.22) | collective-permute-done | bytes 589856 | tf_op jit(solution)/shard_map/ppermute | solution.py:313
  153.4 10.6 %collective-permute-done.14.mine = bf16[2,2,144,512]{3,2,1,0:T(8,128)(2,1)S(1)} collective-permute-done((bf16[2,2,144,512]{3,2,1,0:T(8,128)(2,1)S(1)}, bf16[2,2,144,512]{3,2,1,0:T(8,128)(2,1)S(1)}, u32[]{:S(2)}, u32[]{:S(2)}) %collective-permute-start.14) | collective-permute-done | bytes 589856 | tf_op jit(solution)/shard_map/ppermute | solution.py:313
  164.9 11.2 %shard_map.78.first = f32[144,2048]{1,0:T(8,128)} custom-call(s32[2]{0:T(128)} %pad_add_fusion.1.ids, bf16[2,2,144,512]{3,2,1,0:T(8,128)(2,1)} %copy-done, bf16[2,2,144,512]{3,2,1,0:T(8,128)(2,1)} %copy-done.12, bf16[2048,4096]{1,0:T(8,128)(2,1)} %gate_ref.11, bf16[2048,4096]{1,0:T(8,128)(2,1)} %up_ref.11), custom_call_target="tpu_custom_call" | custom-call | flops 2415919104 | bytes 16777216 | tf_op jit(solution)/shard_map/pallas_call | solution.py:210
  177.0 11.4 %shard_map.76.first = f32[144,2048]{1,0:T(8,128)} custom-call(s32[2]{0:T(128)} %pad_add_fusion.1.ids, bf16[2,2,144,512]{3,2,1,0:T(8,128)(2,1)} %copy-done.1, bf16[2,2,144,512]{3,2,1,0:T(8,128)(2,1)} %copy-done.14, bf16[2048,4096]{1,0:T(8,128)(2,1)} %gate_ref.11, bf16[2048,4096]{1,0:T(8,128)(2,1)} %up_ref.11), custom_call_target="tpu_custom_call" | custom-call | flops 2415919104 | bytes 16777216 | tf_op jit(solution)/shard_map/pallas_call | solution.py:210
  189.2 11.9 %shard_map.79 = (bf16[48,2048]{1,0:T(8,128)(2,1)}, bf16[48,2048]{1,0:T(8,128)(2,1)}, bf16[48,2048]{1,0:T(8,128)(2,1)}, bf16[48,2048]{1,0:T(8,128)(2,1)}) custom-call(s32[2]{0:T(128)} %pad_add_fusion.1.ids, bf16[2,2,144,512]{3,2,1,0:T(8,128)(2,1)} %copy-done.10, bf16[2,2,144,512]{3,2,1,0:T(8,128)(2,1)} %copy-done.15, bf16[2048,4096]{1,0:T(8,128)(2,1)} %gate_ref.11, ...), custom_call_target="tpu_custom_call" | custom-call | flops 2415919104 | bytes 16777216 | tf_op jit(solution)/shard_map/pallas_call | solution.py:221
  201.2 9.2 %collective-permute-start.27 = (bf16[48,2048]{1,0:T(8,128)(2,1)}, bf16[48,2048]{1,0:T(8,128)(2,1)S(1)}, u32[]{:S(2)}, u32[]{:S(2)}) collective-permute-start(bf16[48,2048]{1,0:T(8,128)(2,1)} %get-tuple-element.38), channel_id=1, source_target_pairs={{0,12},{4,0},{8,4},{12,8},{1,13},{5,1},{9,5},{13,9},{2,14},{6,2},{... | collective-permute-start | bytes 589832 | tf_op jit(solution)/shard_map/ppermute | solution.py:320
  211.8 12.1 %shard_map.77 = (bf16[48,2048]{1,0:T(8,128)(2,1)}, bf16[48,2048]{1,0:T(8,128)(2,1)}, bf16[48,2048]{1,0:T(8,128)(2,1)}, bf16[48,2048]{1,0:T(8,128)(2,1)}) custom-call(s32[2]{0:T(128)} %pad_add_fusion.1.ids, bf16[2,2,144,512]{3,2,1,0:T(8,128)(2,1)} %copy-done.11, bf16[2,2,144,512]{3,2,1,0:T(8,128)(2,1)} %copy-done.13, bf16[2048,4096]{1,0:T(8,128)(2,1)} %gate_ref.11, ...), custom_call_target="tpu_custom_call" | custom-call | flops 2415919104 | bytes 16777216 | tf_op jit(solution)/shard_map/pallas_call | solution.py:221
  223.9 3.2 %collective-permute-start.19 = (bf16[48,2048]{1,0:T(8,128)(2,1)}, bf16[48,2048]{1,0:T(8,128)(2,1)S(1)}, u32[]{:S(2)}, u32[]{:S(2)}) collective-permute-start(bf16[48,2048]{1,0:T(8,128)(2,1)} %get-tuple-element.32), channel_id=1, source_target_pairs={{0,12},{4,0},{8,4},{12,8},{1,13},{5,1},{9,5},{13,9},{2,14},{6,2},{... | collective-permute-start | bytes 589832 | tf_op jit(solution)/shard_map/ppermute | solution.py:320
  228.4 4.4 %collective-permute-done.19 = bf16[48,2048]{1,0:T(8,128)(2,1)S(1)} collective-permute-done((bf16[48,2048]{1,0:T(8,128)(2,1)}, bf16[48,2048]{1,0:T(8,128)(2,1)S(1)}, u32[]{:S(2)}, u32[]{:S(2)}) %collective-permute-start.19) | collective-permute-done | bytes 196640 | tf_op jit(solution)/shard_map/ppermute | solution.py:320
  232.8 12.7 %collective-permute-done.18 = bf16[48,2048]{1,0:T(8,128)(2,1)S(1)} collective-permute-done((bf16[48,2048]{1,0:T(8,128)(2,1)}, bf16[48,2048]{1,0:T(8,128)(2,1)S(1)}, u32[]{:S(2)}, u32[]{:S(2)}) %collective-permute-start.18) | collective-permute-done | bytes 196640 | tf_op jit(solution)/shard_map/ppermute | solution.py:320
  (114 shorter events, 20.5 us)
Async XLA Ops:
  0.0 24.0 %collective-permute-start = (bf16[96,2048]{1,0:T(8,128)(2,1)}, bf16[96,2048]{1,0:T(8,128)(2,1)S(1)}, u32[]{:S(2)}, u32[]{:S(2)}) collective-permute-start(bf16[96,2048]{1,0:T(8,128)(2,1)} %param.7), channel_id=1, source_target_pairs={{0,0},{1,4},{2,8},{3,12},{4,1},{5,5},{6,9},{7,13},{8,2},{9,6},{10,... | collective-permute-start | bytes 1179656 | tf_op jit(solution)/shard_map/ppermute | solution.py:253
  1.6 22.3 %collective-permute-start.1 = (bf16[96,2048]{1,0:T(8,128)(2,1)}, bf16[96,2048]{1,0:T(8,128)(2,1)S(1)}, u32[]{:S(2)}, u32[]{:S(2)}) collective-permute-start(bf16[96,2048]{1,0:T(8,128)(2,1)} %param.7), channel_id=1, source_target_pairs={{0,4},{1,8},{2,12},{3,0},{4,5},{5,9},{6,13},{7,1},{8,6},{9,10},{10... | collective-permute-start | bytes 1179656 | tf_op jit(solution)/shard_map/ppermute | solution.py:253
  5.0 19.0 %collective-permute-start.2 = (bf16[96,2048]{1,0:T(8,128)(2,1)}, bf16[96,2048]{1,0:T(8,128)(2,1)S(1)}, u32[]{:S(2)}, u32[]{:S(2)}) collective-permute-start(bf16[96,2048]{1,0:T(8,128)(2,1)} %param.7), channel_id=1, source_target_pairs={{0,8},{1,12},{2,0},{3,4},{4,9},{5,13},{6,1},{7,5},{8,10},{9,14},{1... | collective-permute-start | bytes 1179656 | tf_op jit(solution)/shard_map/ppermute | solution.py:253
  8.4 22.7 %collective-permute-start.3 = (bf16[96,2048]{1,0:T(8,128)(2,1)}, bf16[96,2048]{1,0:T(8,128)(2,1)S(1)}, u32[]{:S(2)}, u32[]{:S(2)}) collective-permute-start(bf16[96,2048]{1,0:T(8,128)(2,1)} %param.7), channel_id=1, source_target_pairs={{0,12},{1,0},{2,4},{3,8},{4,13},{5,1},{6,5},{7,9},{8,14},{9,2},{10... | collective-permute-start | bytes 1179656 | tf_op jit(solution)/shard_map/ppermute | solution.py:253
  24.0 29.5 %copy-start.2 = (bf16[96,2048]{1,0:T(8,128)(2,1)}, bf16[96,2048]{1,0:T(8,128)(2,1)S(1)}, u32[]{:S(2)}) copy-start(bf16[96,2048]{1,0:T(8,128)(2,1)S(1)} %collective-permute-done.p0) | copy-start | bytes 1179652
  24.0 29.5 %copy-start.3 = (bf16[96,2048]{1,0:T(8,128)(2,1)}, bf16[96,2048]{1,0:T(8,128)(2,1)S(1)}, u32[]{:S(2)}) copy-start(bf16[96,2048]{1,0:T(8,128)(2,1)S(1)} %collective-permute-done.1.p1) | copy-start | bytes 1179652
  24.0 29.5 %copy-start.4 = (bf16[96,2048]{1,0:T(8,128)(2,1)}, bf16[96,2048]{1,0:T(8,128)(2,1)S(1)}, u32[]{:S(2)}) copy-start(bf16[96,2048]{1,0:T(8,128)(2,1)S(1)} %collective-permute-done.2.p2) | copy-start | bytes 1179652
  31.1 48.8 %collective-permute-start.4 = (bf16[96,2048]{1,0:T(8,128)(2,1)}, bf16[96,2048]{1,0:T(8,128)(2,1)S(1)}, u32[]{:S(2)}, u32[]{:S(2)}) collective-permute-start(bf16[96,2048]{1,0:T(8,128)(2,1)} %param.8), channel_id=1, source_target_pairs={{0,0},{1,4},{2,8},{3,12},{4,1},{5,5},{6,9},{7,13},{8,2},{9,6},{10,... | collective-permute-start | bytes 1179656 | tf_op jit(solution)/shard_map/ppermute | solution.py:253
  32.7 47.8 %collective-permute-start.5 = (bf16[96,2048]{1,0:T(8,128)(2,1)}, bf16[96,2048]{1,0:T(8,128)(2,1)S(1)}, u32[]{:S(2)}, u32[]{:S(2)}) collective-permute-start(bf16[96,2048]{1,0:T(8,128)(2,1)} %param.8), channel_id=1, source_target_pairs={{0,4},{1,8},{2,12},{3,0},{4,5},{5,9},{6,13},{7,1},{8,6},{9,10},{10... | collective-permute-start | bytes 1179656 | tf_op jit(solution)/shard_map/ppermute | solution.py:253
  44.2 36.4 %collective-permute-start.6 = (bf16[96,2048]{1,0:T(8,128)(2,1)}, bf16[96,2048]{1,0:T(8,128)(2,1)S(1)}, u32[]{:S(2)}, u32[]{:S(2)}) collective-permute-start(bf16[96,2048]{1,0:T(8,128)(2,1)} %param.8), channel_id=1, source_target_pairs={{0,8},{1,12},{2,0},{3,4},{4,9},{5,13},{6,1},{7,5},{8,10},{9,14},{1... | collective-permute-start | bytes 1179656 | tf_op jit(solution)/shard_map/ppermute | solution.py:253
  53.0 27.6 %collective-permute-start.7 = (bf16[96,2048]{1,0:T(8,128)(2,1)}, bf16[96,2048]{1,0:T(8,128)(2,1)S(1)}, u32[]{:S(2)}, u32[]{:S(2)}) collective-permute-start(bf16[96,2048]{1,0:T(8,128)(2,1)} %param.8), channel_id=1, source_target_pairs={{0,12},{1,0},{2,4},{3,8},{4,13},{5,1},{6,5},{7,9},{8,14},{9,2},{10... | collective-permute-start | bytes 1179656 | tf_op jit(solution)/shard_map/ppermute | solution.py:253
  66.6 31.2 %collective-permute-start.12 = (bf16[2,2,288,512]{3,2,1,0:T(8,128)(2,1)}, bf16[2,2,288,512]{3,2,1,0:T(8,128)(2,1)S(1)}, u32[]{:S(2)}, u32[]{:S(2)}) collective-permute-start(bf16[2,2,288,512]{3,2,1,0:T(8,128)(2,1)} %get-tuple-element.28), channel_id=1, source_target_pairs={{0,1},{1,0},{2,3},{3,2},{4,5},{5,4},{6,7},{7,6},{8,9},{9,8},{10,11... | collective-permute-start | bytes 3538952 | tf_op jit(solution)/shard_map/ppermute | solution.py:293
  79.8 19.6 %collective-permute-start.10 = (bf16[2,2,288,512]{3,2,1,0:T(8,128)(2,1)}, bf16[2,2,288,512]{3,2,1,0:T(8,128)(2,1)S(1)}, u32[]{:S(2)}, u32[]{:S(2)}) collective-permute-start(bf16[2,2,288,512]{3,2,1,0:T(8,128)(2,1)} %get-tuple-element.26), channel_id=1, source_target_pairs={{0,1},{1,0},{2,3},{3,2},{4,5},{5,4},{6,7},{7,6},{8,9},{9,8},{10,11... | collective-permute-start | bytes 3538952 | tf_op jit(solution)/shard_map/ppermute | solution.py:293
  97.1 3.2 %collective-permute-start.20 = (bf16[2,2,144,512]{3,2,1,0:T(8,128)(2,1)}, bf16[2,2,144,512]{3,2,1,0:T(8,128)(2,1)S(1)}, u32[]{:S(2)}, u32[]{:S(2)}) collective-permute-start(bf16[2,2,144,512]{3,2,1,0:T(8,128)(2,1)} %get-tuple-element.34), channel_id=1, source_target_pairs={{0,1},{1,0},{2,3},{3,2},{4,5},{5,4},{6,7},{7,6},{8,9},{9,8},{10,11... | collective-permute-start | bytes 1769480 | tf_op jit(solution)/shard_map/ppermute | solution.py:304
  97.4 4.4 %collective-permute-start.8 = (bf16[2,2,144,512]{3,2,1,0:T(8,128)(2,1)}, bf16[2,2,144,512]{3,2,1,0:T(8,128)(2,1)S(1)}, u32[]{:S(2)}, u32[]{:S(2)}) collective-permute-start(bf16[2,2,144,512]{3,2,1,0:T(8,128)(2,1)} %get-tuple-element.24), channel_id=1, source_target_pairs={{0,1},{1,0},{2,3},{3,2},{4,5},{5,4},{6,7},{7,6},{8,9},{9,8},{10,11... | collective-permute-start | bytes 1769480 | tf_op jit(solution)/shard_map/ppermute | solution.py:304
  98.0 16.2 %collective-permute-start.13 = (bf16[2,288,512]{2,1,0:T(8,128)(2,1)S(1)}, bf16[2,288,512]{2,1,0:T(8,128)(2,1)S(1)}, u32[]{:S(2)}, u32[]{:S(2)}) collective-permute-start(bf16[2,288,512]{2,1,0:T(8,128)(2,1)S(1)} %fusion.1), channel_id=1, source_target_pairs={{0,2},{1,3},{2,0},{3,1},{4,6},{5,7},{6,4},{7,5},{8,10},{9,11},{10,... | collective-permute-start | bytes 1769480 | tf_op jit(solution)/shard_map/ppermute | solution.py:295
  99.5 27.4 %collective-permute-start.11 = (bf16[2,288,512]{2,1,0:T(8,128)(2,1)S(1)}, bf16[2,288,512]{2,1,0:T(8,128)(2,1)S(1)}, u32[]{:S(2)}, u32[]{:S(2)}) collective-permute-start(bf16[2,288,512]{2,1,0:T(8,128)(2,1)S(1)} %fusion), channel_id=1, source_target_pairs={{0,2},{1,3},{2,0},{3,1},{4,6},{5,7},{6,4},{7,5},{8,10},{9,11},{10,... | collective-permute-start | bytes 1769480 | tf_op jit(solution)/shard_map/ppermute | solution.py:295
  100.4 32.8 %collective-permute-start.21 = (bf16[2,144,512]{2,1,0:T(8,128)(2,1)S(1)}, bf16[2,144,512]{2,1,0:T(8,128)(2,1)S(1)}, u32[]{:S(2)}, u32[]{:S(2)}) collective-permute-start(bf16[2,144,512]{2,1,0:T(8,128)(2,1)S(1)} %fusion.14), channel_id=1, source_target_pairs={{0,2},{1,3},{2,0},{3,1},{4,6},{5,7},{6,4},{7,5},{8,10},{9,11},{10,... | collective-permute-start | bytes 884744 | tf_op jit(solution)/shard_map/ppermute | solution.py:306
  101.9 37.7 %collective-permute-start.9 = (bf16[2,144,512]{2,1,0:T(8,128)(2,1)S(1)}, bf16[2,144,512]{2,1,0:T(8,128)(2,1)S(1)}, u32[]{:S(2)}, u32[]{:S(2)}) collective-permute-start(bf16[2,144,512]{2,1,0:T(8,128)(2,1)S(1)} %fusion.13), channel_id=1, source_target_pairs={{0,2},{1,3},{2,0},{3,1},{4,6},{5,7},{6,4},{7,5},{8,10},{9,11},{10,... | collective-permute-start | bytes 884744 | tf_op jit(solution)/shard_map/ppermute | solution.py:306
  133.7 18.5 %collective-permute-start.22 = (bf16[2,2,144,512]{3,2,1,0:T(8,128)(2,1)S(1)}, bf16[2,2,144,512]{3,2,1,0:T(8,128)(2,1)S(1)}, u32[]{:S(2)}, u32[]{:S(2)}) collective-permute-start(bf16[2,2,144,512]{3,2,1,0:T(8,128)(2,1)S(1)} %pad_maximum_fusion.3.mine), channel_id=1, source_target_pairs={{0,2},{1,3},{2,0},{3,1},{4,6},{5,7},{6,4},{7,5},{8,10},{9,11},{10,... | collective-permute-start | bytes 1769480 | tf_op jit(solution)/shard_map/ppermute | solution.py:313
  135.0 29.0 %collective-permute-start.24 = (bf16[2,2,144,512]{3,2,1,0:T(8,128)(2,1)S(1)}, bf16[2,2,144,512]{3,2,1,0:T(8,128)(2,1)S(1)}, u32[]{:S(2)}, u32[]{:S(2)}) collective-permute-start(bf16[2,2,144,512]{3,2,1,0:T(8,128)(2,1)S(1)} %pad_maximum_fusion.3.mine), channel_id=1, source_target_pairs={{0,1},{1,0},{2,3},{3,2},{4,5},{5,4},{6,7},{7,6},{8,9},{9,8},{10,11... | collective-permute-start | bytes 1769480 | tf_op jit(solution)/shard_map/ppermute | solution.py:312
  140.0 36.1 %copy-start.1 = (bf16[2,2,144,512]{3,2,1,0:T(8,128)(2,1)}, bf16[2,2,144,512]{3,2,1,0:T(8,128)(2,1)S(1)}, u32[]{:S(2)}) copy-start(bf16[2,2,144,512]{3,2,1,0:T(8,128)(2,1)S(1)} %pad_maximum_fusion.1.mine) | copy-start | bytes 1769476
  140.0 24.0 %collective-permute-start.14 = (bf16[2,2,144,512]{3,2,1,0:T(8,128)(2,1)S(1)}, bf16[2,2,144,512]{3,2,1,0:T(8,128)(2,1)S(1)}, u32[]{:S(2)}, u32[]{:S(2)}) collective-permute-start(bf16[2,2,144,512]{3,2,1,0:T(8,128)(2,1)S(1)} %pad_maximum_fusion.1.mine), channel_id=1, source_target_pairs={{0,2},{1,3},{2,0},{3,1},{4,6},{5,7},{6,4},{7,5},{8,10},{9,11},{10,... | collective-permute-start | bytes 1769480 | tf_op jit(solution)/shard_map/ppermute | solution.py:313
  142.6 33.5 %collective-permute-start.16 = (bf16[2,2,144,512]{3,2,1,0:T(8,128)(2,1)S(1)}, bf16[2,2,144,512]{3,2,1,0:T(8,128)(2,1)S(1)}, u32[]{:S(2)}, u32[]{:S(2)}) collective-permute-start(bf16[2,2,144,512]{3,2,1,0:T(8,128)(2,1)S(1)} %pad_maximum_fusion.1.mine), channel_id=1, source_target_pairs={{0,1},{1,0},{2,3},{3,2},{4,5},{5,4},{6,7},{7,6},{8,9},{9,8},{10,11... | collective-permute-start | bytes 1769480 | tf_op jit(solution)/shard_map/ppermute | solution.py:312
  152.2 36.2 %collective-permute-start.23 = (bf16[2,2,144,512]{3,2,1,0:T(8,128)(2,1)S(1)}, bf16[2,2,144,512]{3,2,1,0:T(8,128)(2,1)S(1)}, u32[]{:S(2)}, u32[]{:S(2)}) collective-permute-start(bf16[2,2,144,512]{3,2,1,0:T(8,128)(2,1)S(1)} %collective-permute-done.22.mine), channel_id=1, source_target_pairs={{0,1},{1,0},{2,3},{3,2},{4,5},{5,4},{6,7},{7,6},{8,9},{9,8},{10,11... | collective-permute-start | bytes 1769480 | tf_op jit(solution)/shard_map/ppermute | solution.py:314
  164.0 47.0 %collective-permute-start.15 = (bf16[2,2,144,512]{3,2,1,0:T(8,128)(2,1)S(1)}, bf16[2,2,144,512]{3,2,1,0:T(8,128)(2,1)S(1)}, u32[]{:S(2)}, u32[]{:S(2)}) collective-permute-start(bf16[2,2,144,512]{3,2,1,0:T(8,128)(2,1)S(1)} %collective-permute-done.14.mine), channel_id=1, source_target_pairs={{0,1},{1,0},{2,3},{3,2},{4,5},{5,4},{6,7},{7,6},{8,9},{9,8},{10,11... | collective-permute-start | bytes 1769480 | tf_op jit(solution)/shard_map/ppermute | solution.py:314
  201.2 27.1 %collective-permute-start.27 = (bf16[48,2048]{1,0:T(8,128)(2,1)}, bf16[48,2048]{1,0:T(8,128)(2,1)S(1)}, u32[]{:S(2)}, u32[]{:S(2)}) collective-permute-start(bf16[48,2048]{1,0:T(8,128)(2,1)} %get-tuple-element.38), channel_id=1, source_target_pairs={{0,12},{4,0},{8,4},{12,8},{1,13},{5,1},{9,5},{13,9},{2,14},{6,2},{... | collective-permute-start | bytes 589832 | tf_op jit(solution)/shard_map/ppermute | solution.py:320
  210.4 17.9 %collective-permute-start.26 = (bf16[48,2048]{1,0:T(8,128)(2,1)}, bf16[48,2048]{1,0:T(8,128)(2,1)S(1)}, u32[]{:S(2)}, u32[]{:S(2)}) collective-permute-start(bf16[48,2048]{1,0:T(8,128)(2,1)} %get-tuple-element.37), channel_id=1, source_target_pairs={{0,8},{4,12},{8,0},{12,4},{1,9},{5,13},{9,1},{13,5},{2,10},{6,14},... | collective-permute-start | bytes 589832 | tf_op jit(solution)/shard_map/ppermute | solution.py:320
  210.4 17.9 %collective-permute-start.25 = (bf16[48,2048]{1,0:T(8,128)(2,1)}, bf16[48,2048]{1,0:T(8,128)(2,1)S(1)}, u32[]{:S(2)}, u32[]{:S(2)}) collective-permute-start(bf16[48,2048]{1,0:T(8,128)(2,1)} %get-tuple-element.36), channel_id=1, source_target_pairs={{0,4},{4,8},{8,12},{12,0},{1,5},{5,9},{9,13},{13,1},{2,6},{6,10},{... | collective-permute-start | bytes 589832 | tf_op jit(solution)/shard_map/ppermute | solution.py:320
  223.9 8.9 %collective-permute-start.19 = (bf16[48,2048]{1,0:T(8,128)(2,1)}, bf16[48,2048]{1,0:T(8,128)(2,1)S(1)}, u32[]{:S(2)}, u32[]{:S(2)}) collective-permute-start(bf16[48,2048]{1,0:T(8,128)(2,1)} %get-tuple-element.32), channel_id=1, source_target_pairs={{0,12},{4,0},{8,4},{12,8},{1,13},{5,1},{9,5},{13,9},{2,14},{6,2},{... | collective-permute-start | bytes 589832 | tf_op jit(solution)/shard_map/ppermute | solution.py:320
  227.1 18.4 %collective-permute-start.18 = (bf16[48,2048]{1,0:T(8,128)(2,1)}, bf16[48,2048]{1,0:T(8,128)(2,1)S(1)}, u32[]{:S(2)}, u32[]{:S(2)}) collective-permute-start(bf16[48,2048]{1,0:T(8,128)(2,1)} %get-tuple-element.31), channel_id=1, source_target_pairs={{0,8},{4,12},{8,0},{12,4},{1,9},{5,13},{9,1},{13,5},{2,10},{6,14},... | collective-permute-start | bytes 589832 | tf_op jit(solution)/shard_map/ppermute | solution.py:320
  228.3 17.2 %collective-permute-start.17 = (bf16[48,2048]{1,0:T(8,128)(2,1)}, bf16[48,2048]{1,0:T(8,128)(2,1)S(1)}, u32[]{:S(2)}, u32[]{:S(2)}) collective-permute-start(bf16[48,2048]{1,0:T(8,128)(2,1)} %get-tuple-element.30), channel_id=1, source_target_pairs={{0,4},{4,8},{8,12},{12,0},{1,5},{5,9},{9,13},{13,1},{2,6},{6,10},{... | collective-permute-start | bytes 589832 | tf_op jit(solution)/shard_map/ppermute | solution.py:320
  (17 other events, 112.1 us)

commit v2 on v0

v2 whole, which is shorter than its diff:
```python
import functools
import jax
import jax.numpy as jnp
from jax import lax
from jax.experimental import pallas as pl
from jax.experimental.pallas import tpu as pltpu
from jax.sharding import PartitionSpec as P

BF, F32 = jnp.bfloat16, jnp.float32
ROW_CONTRACT = (((1,), (1,)), ((), ()))
VMEM = 56 * 1024 * 1024
GATE_UP_COST, HIDDEN_COST, NEAR_COST, FAR_COST = 40000000, 60000000, 40000000, 40000000


def derive(gate, up, hidden_grad):
    sig = jax.nn.sigmoid(gate)
    d_up = (hidden_grad * gate * sig).astype(BF)
    d_gate = (hidden_grad * up * sig * (1.0 + gate * (1.0 - sig))).astype(BF)
    return (d_gate, d_up)


def general(tokens, grad_out, counts, packing, gate_weight, up_weight, down_weight):
    shard_rows = tokens.shape[0]
    alive_rows = jnp.arange(shard_rows, dtype=jnp.int32) < counts[0]
    masked = jnp.where(alive_rows[:, None], grad_out, jnp.zeros_like(grad_out))
    whole_tokens, whole_cotangent = (
        lax.all_gather(tokens, "tensor", axis=1, tiled=True),
        lax.all_gather(masked, "tensor", axis=1, tiled=True),
    )
    owned_tokens, owned_cotangent = (
        lax.all_to_all(whole_tokens, "seq", split_axis=1, concat_axis=0, tiled=True),
        lax.all_to_all(whole_cotangent, "seq", split_axis=1, concat_axis=0, tiled=True),
    )
    packed_tokens = jnp.take(owned_tokens, packing, axis=0)
    packed_cotangent = jnp.take(owned_cotangent, packing, axis=0)
    gate_part = jnp.dot(packed_tokens, gate_weight, preferred_element_type=F32)
    up_part = jnp.dot(packed_tokens, up_weight, preferred_element_type=F32)
    hidden_part = lax.dot_general(
        packed_cotangent, down_weight, ROW_CONTRACT, preferred_element_type=F32
    )
    gate, up, hidden_grad = (
        lax.psum(gate_part.astype(BF), "seq").astype(F32),
        lax.psum(up_part.astype(BF), "seq").astype(F32),
        lax.psum(hidden_part.astype(BF), "seq").astype(F32),
    )
    d_gate, d_up = derive(gate, up, hidden_grad)
    result = lax.dot_general(d_gate, gate_weight, ROW_CONTRACT, preferred_element_type=F32)
    return lax.psum_scatter(
        (result + lax.dot_general(d_up, up_weight, ROW_CONTRACT, preferred_element_type=F32)).astype(BF),
        "tensor",
        scatter_dimension=0,
        tiled=True,
    )


def region(ref, axis, index, size):
    spot = pl.ds(pl.multiple_of(index * size, size), size)
    return ref.at[spot] if axis == 0 else ref.at[:, spot]


def slot_index(slot, core, x):
    which_core = 1 - core if slot % 2 == 0 else core
    which_x = 1 - x if slot // 2 == 0 else x
    return which_x * 2 + which_core


def start(source, target, sem):
    copy = pltpu.make_async_copy(source, target, sem)
    copy.start()
    return copy


class Stream:
    def __init__(self, copies, ahead):
        self.copies, self.ahead, self.begun = copies, ahead, 0
        self.reach(0)

    def reach(self, index):
        while self.begun < min(index + self.ahead, len(self.copies)):
            for copy in self.copies[self.begun]:
                copy.start()
            self.begun += 1

    def wait(self, index):
        for copy in self.copies[index]:
            copy.wait()
        self.reach(index + 1)


IN_VMEM = pl.BlockSpec(memory_space=pltpu.VMEM)
IN_HBM = pl.BlockSpec(memory_space=pl.ANY)
IN_SMEM = pl.BlockSpec(memory_space=pltpu.SMEM)


def call(kernel, in_specs, out_shape, scratch, cost):
    return pl.pallas_call(
        kernel,
        in_specs=in_specs,
        out_specs=[IN_HBM] * len(out_shape),
        out_shape=[jax.ShapeDtypeStruct(shape, dtype) for shape, dtype in out_shape],
        scratch_shapes=scratch,
        compiler_params=pltpu.CompilerParams(vmem_limit_bytes=VMEM),
        cost_estimate=pl.CostEstimate(flops=0, bytes_accessed=cost, transcendentals=0),
    )


def pick_start(parts, arrived, sems):
    width = parts[0].shape[0]
    return [start(part, arrived.at[pl.ds(k * width, width)], sems.at[k]) for k, part in enumerate(parts)]


def pick_end(moves, select_ref, arrived, rows_v):
    for move in moves:
        move.wait()
    rows_v[...] = jnp.dot(select_ref[...], arrived[...], preferred_element_type=F32).astype(BF)


def gate_up_kernel(ids, select_ref, p0, p1, p2, p3, gate_w, up_w, send_far, keep_far, send_near, keep_near,
                   gate_v, up_v, out_v, rows_v, arrived, sems):
    core, x = ids[0], ids[1]
    block = gate_v.shape[2]
    moves = pick_start((p0, p1, p2, p3), arrived, sems.at[0])
    loads = []
    for slot in range(4):
        index = slot_index(slot, core, x)
        for a, (weight, held) in enumerate(((gate_w, gate_v), (up_w, up_v))):
            loads.append([pltpu.make_async_copy(region(weight, 1, index, block), held.at[slot], sems.at[1 + a, slot])])
    loads = Stream(loads, 3)
    pick_end(moves, select_ref, arrived, rows_v)
    stores = []
    for slot, out in enumerate((send_far, keep_far, send_near, keep_near)):
        for a, held in enumerate((gate_v, up_v)):
            loads.wait(2 * slot + a)
            out_v[slot, a] = jnp.dot(rows_v[...], held[slot], preferred_element_type=F32).astype(BF)
            stores.append(start(out_v.at[slot, a], out.at[a], sems.at[3 + a, slot]))
    for store in stores:
        store.wait()


def gate_up(ids, select, parts, gate_weight, up_weight):
    depth, block = gate_weight.shape[0], gate_weight.shape[1] // 4
    count = select.shape[0]
    return call(
        gate_up_kernel,
        [IN_SMEM, IN_VMEM] + [IN_HBM] * 6,
        [((2, count, block), BF)] * 4,
        [pltpu.VMEM((4, depth, block), BF)] * 2 + [
            pltpu.VMEM((4, 2, count, block), BF),
            pltpu.VMEM((count, depth), BF),
            pltpu.VMEM((select.shape[1], depth), BF),
            pltpu.SemaphoreType.DMA((5, 4)),
        ],
        GATE_UP_COST,
    )(ids, select, *parts, gate_weight, up_weight)


def hidden_kernel(ids, select_ref, p0, p1, p2, p3, down, send_a, send_b, keep_a, keep_b,
                  down_v, out_v, rows_v, arrived, sems):
    core, x = ids[0], ids[1]
    rows, block = send_a.shape[1], send_a.shape[2]
    moves = pick_start((p0, p1, p2, p3), arrived, sems.at[0])
    loads = Stream(
        [[pltpu.make_async_copy(region(down, 0, slot_index(slot, core, x), block), down_v.at[slot], sems.at[1, slot])]
         for slot in range(4)], 3)
    pick_end(moves, select_ref, arrived, rows_v)
    stores = []
    for slot in range(4):
        loads.wait(slot)
        hidden = lax.dot_general(rows_v[...], down_v[slot], ROW_CONTRACT, preferred_element_type=F32)
        out_v[slot] = hidden.astype(BF)
        for m, out in enumerate((send_a, send_b) if slot % 2 == 0 else (keep_a, keep_b)):
            stores.append(start(out_v.at[slot, pl.ds(m * rows, rows)], out.at[slot // 2], sems.at[2 + m, slot]))
    for store in stores:
        store.wait()


def hidden_grads(ids, select, parts, down_weight):
    depth, block = down_weight.shape[1], down_weight.shape[0] // 4
    count = select.shape[0]
    return call(
        hidden_kernel,
        [IN_SMEM, IN_VMEM] + [IN_HBM] * 5,
        [((2, count // 2, block), BF)] * 4,
        [
            pltpu.VMEM((4, block, depth), BF),
            pltpu.VMEM((4, count, block), BF),
            pltpu.VMEM((count, depth), BF),
            pltpu.VMEM((select.shape[1], depth), BF),
            pltpu.SemaphoreType.DMA((4, 4)),
        ],
        HIDDEN_COST,
    )(ids, select, *parts, down_weight)


CHUNKS = 4


def back_begin(core, which_x, pairs, gate_w, up_w, grads_v, weight_v, sems, grad_sems):
    rows, block = pairs[0][0].shape[1], pairs[0][0].shape[2]
    height, width = gate_w.shape[0] // CHUNKS, 2 * block
    moves = []
    for m, pair in enumerate(pairs):
        for source, value in enumerate(pair):
            which_core = core if source == 0 else 1 - core
            spot = pl.ds(pl.multiple_of(which_core * block, block), block)
            for a in range(2):
                moves.append(start(value.at[a], grads_v.at[a, pl.ds(m * rows, rows), spot],
                                   grad_sems.at[m, 2 * source + a]))
    side = pl.ds(pl.multiple_of(which_x * width, width), width)
    loads = []
    for chunk in range(CHUNKS):
        high = pl.ds(chunk * height, height)
        loads.append([
            pltpu.make_async_copy(weight.at[high, side], weight_v.at[a, high], sems.at[chunk, a])
            for a, weight in enumerate((gate_w, up_w))
        ])
    return moves, Stream(loads, 2)


def back_chunk(chunk, grads_v, weight_v, loads):
    height = weight_v.shape[1] // CHUNKS
    spot = pl.ds(chunk * height, height)
    loads.wait(chunk)
    total = lax.dot_general(grads_v[0], weight_v[0, spot], ROW_CONTRACT, preferred_element_type=F32)
    return total + lax.dot_general(grads_v[1], weight_v[1, spot], ROW_CONTRACT, preferred_element_type=F32)


def near_kernel(ids, mine_a, other_a, mine_b, other_b, gate_w, up_w, out_a, out_b,
                grads_v, weight_v, out_v, sems, grad_sems, out_sems):
    moves, loads = back_begin(ids[0], ids[1], ((mine_a, other_a), (mine_b, other_b)), gate_w, up_w,
                              grads_v, weight_v, sems, grad_sems)
    height, rows = gate_w.shape[0] // CHUNKS, out_a.shape[0]
    for move in moves:
        move.wait()
    stores = []
    for chunk in range(CHUNKS):
        spot = pl.ds(chunk * height, height)
        out_v[:, spot] = back_chunk(chunk, grads_v, weight_v, loads)
        for m, out in enumerate((out_a, out_b)):
            stores.append(start(out_v.at[pl.ds(m * rows, rows), spot], out.at[:, spot], out_sems.at[chunk, m]))
    for store in stores:
        store.wait()


def far_kernel(ids, place_ref, mine, other, gate_w, up_w, first, o0, o1, o2, o3,
               grads_v, weight_v, first_v, out_v, sems, grad_sems, out_sems, first_sem):
    moves, loads = back_begin(ids[0], 1 - ids[1], ((mine, other),), gate_w, up_w, grads_v, weight_v, sems, grad_sems)
    moves.append(start(first, first_v, first_sem.at[0]))
    height = gate_w.shape[0] // CHUNKS
    piece = o0.shape[0]
    for move in moves:
        move.wait()
    stores = []
    for chunk in range(CHUNKS):
        spot = pl.ds(chunk * height, height)
        total = first_v[:, spot] + back_chunk(chunk, grads_v, weight_v, loads)
        out_v[:, spot] = jnp.dot(place_ref[...], total.astype(BF), preferred_element_type=F32).astype(BF)
        for k, out in enumerate((o0, o1, o2, o3)):
            part = out_v.at[pl.ds(k * piece, piece), spot]
            stores.append(start(part, out.at[:, spot], out_sems.at[chunk, k]))
    for store in stores:
        store.wait()


def near(ids, mine, other, gate_weight, up_weight):
    sets, rows, block, depth = len(mine), mine[0].shape[1], mine[0].shape[2], gate_weight.shape[0]
    count = sets * rows
    return call(
        near_kernel,
        [IN_SMEM] + [IN_HBM] * 6,
        [((rows, depth), F32)] * 2,
        [
            pltpu.VMEM((2, count, 2 * block), BF),
            pltpu.VMEM((2, depth, 2 * block), BF),
            pltpu.VMEM((count, depth), F32),
            pltpu.SemaphoreType.DMA((CHUNKS, 2)),
            pltpu.SemaphoreType.DMA((sets, 4)),
            pltpu.SemaphoreType.DMA((CHUNKS, sets)),
        ],
        NEAR_COST,
    )(ids, mine[0], other[0], mine[1], other[1], gate_weight, up_weight)


def far(ids, place, mine, other, gate_weight, up_weight, first):
    rows, block, depth = mine.shape[1], mine.shape[2], gate_weight.shape[0]
    count = place.shape[0]
    return call(
        far_kernel,
        [IN_SMEM, IN_VMEM] + [IN_HBM] * 5,
        [((count // 4, depth), BF)] * 4,
        [
            pltpu.VMEM((2, rows, 2 * block), BF),
            pltpu.VMEM((2, depth, 2 * block), BF),
            pltpu.VMEM((rows, depth), F32),
            pltpu.VMEM((count, depth), BF),
            pltpu.SemaphoreType.DMA((CHUNKS, 2)),
            pltpu.SemaphoreType.DMA((1, 4)),
            pltpu.SemaphoreType.DMA((CHUNKS, 4)),
            pltpu.SemaphoreType.DMA((1,)),
        ],
        FAR_COST,
    )(ids, place, mine, other, gate_weight, up_weight, first)


def after(value, *others):
    return lax.optimization_barrier((value,) + others)[0]


def tuned(n, tokens, grad_out, counts, packing, gate_weight, up_weight, down_weight):
    shard_rows, depth = tokens.shape
    rows = packing.shape[0]
    live_rows = rows * 3 // 4
    sets = 2
    set_rows, piece = live_rows // sets, shard_rows // sets
    t, s = lax.axis_index("tensor"), lax.axis_index("seq")
    core, x = s % 2, s // 2
    ids = jnp.stack([core, x]).astype(jnp.int32)
    sibling = [(i, i ^ 1) for i in range(n)]
    across = [(i, i ^ 2) for i in range(n)]

    def spread(value, k):
        pairs = [(a * n + b, ((b + k) % n) * n + a) for a in range(n) for b in range(n)]
        return lax.ppermute(value, ("tensor", "seq"), pairs)

    token_parts = [spread(tokens, k) for k in range(n)]
    held = after(grad_out, *token_parts)
    grad_parts = [spread(held, k) for k in range(n)]

    all_counts = lax.all_gather(counts, "seq", tiled=True)
    home, place_in = packing // shard_rows, packing % shard_rows
    bound = jnp.sum(jnp.where(home[:, None] == jnp.arange(n)[None, :], all_counts[None, :], 0), axis=1)
    alive = place_in < bound
    order = jnp.arange(rows, dtype=jnp.int32)
    rank = jnp.sum(jnp.where(order[None, :] < order[:, None], alive[None, :].astype(jnp.int32), 0), axis=1)
    index = jnp.where(alive, (rank % sets) * set_rows + rank // sets, -1)
    slot = jnp.arange(rows, dtype=jnp.int32)
    arriving = ((t - slot // shard_rows) % n) * shard_rows + slot % shard_rows
    to_row = (index[None, :] == jnp.arange(live_rows, dtype=jnp.int32)[:, None]).astype(BF)
    from_slot = (packing[:, None] == arriving[None, :]).astype(BF)
    select = jnp.dot(to_row, from_slot, preferred_element_type=F32).astype(BF)
    before = jnp.sum(
        jnp.where(order[None, :] < (jnp.arange(n) * shard_rows)[:, None], alive[None, :].astype(jnp.int32), 0), axis=1
    )
    begin = jnp.stack([(before + sets - 1 - m) // sets for m in range(sets)])
    target = (t + jnp.arange(n)) % n
    target_begin = jnp.sum(
        jnp.where(target[None, :, None] == jnp.arange(n)[None, None, :], begin[:, None, :], 0), axis=2
    )
    place = (
        target_begin[:, :, None, None] + jnp.arange(piece)[None, None, :, None]
        == jnp.arange(set_rows)[None, None, None, :]
    ).astype(BF)
    own = (order // shard_rows == t)
    mine_rank = jnp.sum(jnp.where((order[None, :] == t * shard_rows + jnp.arange(shard_rows)[:, None]),
                                  jnp.where(alive, rank, -1)[None, :], 0), axis=1)
    spot = jnp.where(mine_rank >= 0, (mine_rank % sets) * piece + mine_rank // sets
                     - jnp.where(mine_rank % sets == 0, target_begin[0, 0], target_begin[1, 0]), -1)
    final = (spot[:, None] == jnp.arange(sets * piece)[None, :]).astype(BF)

    def project(ids, select, gate_weight, up_weight, *token_parts):
        send_far, keep_far, send_near, keep_near = gate_up(ids, select, token_parts, gate_weight, up_weight)
        got_far = lax.ppermute(send_far, "seq", sibling)
        return (keep_far.astype(F32) + got_far.astype(F32)).astype(BF), send_near, keep_near

    def absent(ids, select, *rest):
        nothing = jnp.zeros((2, live_rows, gate_weight.shape[1] // 4), BF)
        return nothing, nothing, nothing

    pair_far, send_near, keep_near = lax.cond(
        packing[0] >= 0, project, absent, ids, select, gate_weight, up_weight, *token_parts
    )

    across_near = lax.ppermute(pair_far, "seq", across)

    outs = hidden_grads(ids, after(select, pair_far), grad_parts, down_weight)
    got_near = lax.ppermute(after(send_near, outs[0]), "seq", sibling)
    gate_near = keep_near.astype(F32) + got_near.astype(F32) + across_near.astype(F32)
    ds, ds_core = [], []
    for m in range(sets):
        send, keep = outs[m], outs[sets + m]
        got = lax.ppermute(send, "seq", sibling)
        pair_far = (keep[0].astype(F32) + got[0].astype(F32)).astype(BF)
        hid = keep[1].astype(F32) + got[1].astype(F32) + lax.ppermute(pair_far, "seq", across).astype(F32)
        part = slice(m * set_rows, (m + 1) * set_rows)
        ds.append(jnp.stack(derive(gate_near[0, part], gate_near[1, part], hid)))
        ds_core.append(lax.ppermute(ds[m], "seq", sibling))
    ds_far = [lax.ppermute(d, "seq", across) for d in ds]
    firsts = near(ids, ds, ds_core, gate_weight, up_weight)
    pieces = []
    for m in range(sets):
        d_both = lax.ppermute(after(ds_far[m], firsts[0]), "seq", sibling)
        parts = far(ids, place[m].reshape(n * piece, set_rows), ds_far[m], d_both, gate_weight, up_weight, firsts[m])
        total = parts[0].astype(F32)
        for k in range(1, n):
            shift = [(i, (i + k) % n) for i in range(n)]
            total += lax.ppermute(parts[k], "tensor", shift).astype(F32)
        pieces.append(total.astype(BF))
    return jnp.dot(final, jnp.concatenate(pieces), preferred_element_type=F32).astype(BF)


def solution(mesh):
    placed = (
        P(("group", "seq"), "tensor"),
        P(("group", "seq"), "tensor"),
        P(("group", "seq")),
        P("group"),
        P("seq", "tensor"),
        P("seq", "tensor"),
        P("tensor", "seq"),
    )
    if mesh.shape["tensor"] == 4 and mesh.shape["seq"] == 4:
        body = functools.partial(tuned, 4)
    else:
        body = general
    return jax.shard_map(
        body, mesh=mesh, in_specs=placed, out_specs=P(("group", "tensor"), "seq"), check_vma=False
    )
```

time: 395 us -> 203 us (0.51)
  waiting for transfers between devices: 292 us -> 58.5 us
  matrix products: 67.9 us -> 2.17 us
  Pallas kernels: 0 us -> 62.6 us
  starting transfers between devices: 7.43 us -> 51.5 us
  between operations: 13.8 us -> 1.61 us
  other arithmetic: 1.86 us -> 10.8 us
  blocking collectives: 0 us -> 5.96 us
  local copies, waits for them, and re-layouts: 11.8 us -> 7.71 us
    psum x1 -> x0, waiting for transfers between devices: 168 us -> none  [shards(): lax.psum(gate_part.astype(jnp.bfloat16), 'seq').astype(jnp.float32)]
    all_gather x2 -> x0, waiting for transfers between devices: 70.2 us -> none  [the longest x1 38.9 us: shards(): lax.all_gather(tokens, 'tensor', axis=1, tiled=True)]
    dot_general x5 -> x2, matrix products: 67.9 us -> 2.17 us  [the longest x1 1.11 us: tuned(): select = jnp.dot(to_row, from_slot, preferred_element_type=F32).astype(BF)]
    pallas_call x0 -> x5, Pallas kernels: none -> 62.6 us  [the longest x2 25.7 us: far(): call(far_kernel, [IN_SMEM, IN_VMEM] + [IN_HBM] * 5, [((count // 4, depth)...]
    ppermute x0 -> x27, waiting for transfers between devices: none -> 58.5 us  [the longest x6 12.9 us: tuned(): total += lax.ppermute(parts[k], 'tensor', shift).astype(F32)]
    ppermute x0 -> x27, starting transfers between devices: none -> 51.5 us  [the longest x8 33.4 us: spread(): return lax.ppermute(value, ('tensor', 'seq'), pairs)]
    reduce_scatter x1 -> x0, waiting for transfers between devices: 35.6 us -> none  [shards(): lax.psum_scatter((result + lax.dot_general(d_up, up_weight, contract, pre...]
    all_to_all x2 -> x0, waiting for transfers between devices: 16.8 us -> none  [the longest x1 16.8 us: shards(): lax.all_to_all(whole_cotangent, 'seq', split_axis=1, concat_axis=0, tiled...]
  transfers between devices with their start and end apart: 6 -> 27, of which waited for: 5 -> 12; matrix products, arithmetic and copies ran while one was open for 3% -> 7% of each run, Pallas kernels for 0% -> 31%
where the time goes in v2:
time: 203 us; the launch traced here: 201 us
  Pallas kernels  62.6 us (31%)
  waiting for transfers between devices  58.5 us (29%)
  starting transfers between devices  51.5 us (25%)
  other arithmetic  10.8 us (5%)
  local copies, waits for them, and re-layouts  7.71 us (4%)
  blocking collectives  5.96 us (3%)
  matrix products  2.17 us (1%)
    ppermute x8, starting transfers between devices, spread(): return lax.ppermute(value, ('tensor', 'seq'), pairs)  33.4 us
    pallas_call x2, Pallas kernels, far(): call(far_kernel, [IN_SMEM, IN_VMEM] + [IN_HBM] * 5, [((count // 4, depth)...  25.7 us
    pallas_call x1, Pallas kernels, gate_up(): call(gate_up_kernel, [IN_SMEM, IN_VMEM] + [IN_HBM] * 6, [((2, count, bloc...  15.9 us
    ppermute x6, waiting for transfers between devices, tuned(): total += lax.ppermute(parts[k], 'tensor', shift).astype(F32)  12.9 us
    ppermute x2, waiting for transfers between devices, tuned(): ds_far = [lax.ppermute(d, 'seq', across) for d in ds]  12 us
    ppermute x2, waiting for transfers between devices, tuned(): lax.ppermute(pair_far, 'seq', across).astype(F32)  11.4 us
    pallas_call x1, Pallas kernels, near(): call(near_kernel, [IN_SMEM] + [IN_HBM] * 6, [((rows, depth), F32)] * 2, [...  10.7 us
    pallas_call x1, Pallas kernels, hidden_grads(): call(hidden_kernel, [IN_SMEM, IN_VMEM] + [IN_HBM] * 5, [((2, count // 2,...  10.3 us
  transfers between devices with their start and end apart: 27, of which 12 were waited for; matrix products, arithmetic and copies ran while one was open for 7% of the time, Pallas kernels for 31%

profile of v2, /device:TPU:0, one launch (start us, length us, event | category | flops | bytes accessed | tf_op | source)
XLA Modules:
  0.0 201.1 jit_solution(1960359678467399337)
XLA Ops:
  0.0 1.6 collective-permute-start.1
  1.6 3.4 %collective-permute-start.2 = (bf16[96,2048]{1,0:T(8,128)(2,1)}, bf16[96,2048]{1,0:T(8,128)(2,1)S(1)}, u32[]{:S(2)}, u32[]{:S(2)}) collective-permute-start(bf16[96,2048]{1,0:T(8,128)(2,1)} %param.9), channel_id=1, source_target_pairs={{0,4},{1,8},{2,12},{3,0},{4,5},{5,9},{6,13},{7,1},{8,6},{9,10},{10... | collective-permute-start | bytes 1179656 | tf_op jit(solution)/shard_map/ppermute | solution.py:323
  5.0 3.4 %collective-permute-start.3 = (bf16[96,2048]{1,0:T(8,128)(2,1)}, bf16[96,2048]{1,0:T(8,128)(2,1)S(1)}, u32[]{:S(2)}, u32[]{:S(2)}) collective-permute-start(bf16[96,2048]{1,0:T(8,128)(2,1)} %param.9), channel_id=1, source_target_pairs={{0,8},{1,12},{2,0},{3,4},{4,9},{5,13},{6,1},{7,5},{8,10},{9,14},{1... | collective-permute-start | bytes 1179656 | tf_op jit(solution)/shard_map/ppermute | solution.py:323
  11.0 2.6 %collective-permute-start.4 = (bf16[96,2048]{1,0:T(8,128)(2,1)}, bf16[96,2048]{1,0:T(8,128)(2,1)S(1)}, u32[]{:S(2)}, u32[]{:S(2)}) collective-permute-start(bf16[96,2048]{1,0:T(8,128)(2,1)} %param.9), channel_id=1, source_target_pairs={{0,12},{1,0},{2,4},{3,8},{4,13},{5,1},{6,5},{7,9},{8,14},{9,2},{10... | collective-permute-start | bytes 1179656 | tf_op jit(solution)/shard_map/ppermute | solution.py:323
  13.7 6.0 %all-reduce = s32[4]{0:T(128)S(1)} all-reduce(s32[4]{0:T(128)S(1)} %dynamic-update-slice), channel_id=1, replica_groups=mesh['group'=2,'tensor'=4,'seq'=4] {'seq'}, use_global_device_ids=true, to_apply=%add | all-reduce | flops 4 | bytes 32
  21.3 1.9 collective-permute-done.3
  23.2 7.8 %collective-permute-done.4 = bf16[96,2048]{1,0:T(8,128)(2,1)S(1)} collective-permute-done((bf16[96,2048]{1,0:T(8,128)(2,1)}, bf16[96,2048]{1,0:T(8,128)(2,1)S(1)}, u32[]{:S(2)}, u32[]{:S(2)}) %collective-permute-start.4) | collective-permute-done | bytes 393248 | tf_op jit(solution)/shard_map/ppermute | solution.py:323
  31.1 4.5 %collective-permute-start.5 = (bf16[96,2048]{1,0:T(8,128)(2,1)}, bf16[96,2048]{1,0:T(8,128)(2,1)}, u32[]{:S(2)}, u32[]{:S(2)}) collective-permute-start(bf16[96,2048]{1,0:T(8,128)(2,1)} %param.10), channel_id=1, source_target_pairs={{0,0},{1,4},{2,8},{3,12},{4,1},{5,5},{6,9},{7,13},{8,2},{9,6},{10,... | collective-permute-start | bytes 1179656 | tf_op jit(solution)/shard_map/ppermute | solution.py:323
  35.5 8.6 %collective-permute-start.6 = (bf16[96,2048]{1,0:T(8,128)(2,1)}, bf16[96,2048]{1,0:T(8,128)(2,1)}, u32[]{:S(2)}, u32[]{:S(2)}) collective-permute-start(bf16[96,2048]{1,0:T(8,128)(2,1)} %param.10), channel_id=1, source_target_pairs={{0,4},{1,8},{2,12},{3,0},{4,5},{5,9},{6,13},{7,1},{8,6},{9,10},{10... | collective-permute-start | bytes 1179656 | tf_op jit(solution)/shard_map/ppermute | solution.py:323
  44.2 8.8 %collective-permute-start.7 = (bf16[96,2048]{1,0:T(8,128)(2,1)}, bf16[96,2048]{1,0:T(8,128)(2,1)}, u32[]{:S(2)}, u32[]{:S(2)}) collective-permute-start(bf16[96,2048]{1,0:T(8,128)(2,1)} %param.10), channel_id=1, source_target_pairs={{0,8},{1,12},{2,0},{3,4},{4,9},{5,13},{6,1},{7,5},{8,10},{9,14},{1... | collective-permute-start | bytes 1179656 | tf_op jit(solution)/shard_map/ppermute | solution.py:323
  57.2 19.7 %conditional.1 = (bf16[2,288,1024]{2,1,0:T(8,128)(2,1)S(1)}, bf16[2,288,1024]{2,1,0:T(8,128)(2,1)}, f32[2,288,1024]{2,1,0:T(8,128)S(1)}) conditional(s32[]{:T(128)} %bitcast.7, () %tuple.20, (s32[2]{0:T(128)S(1)}, bf16[288,384]{1,0:T(8,128)(2,1)S(1)}, bf16[96,2048]{1,0:T(8,128)(2,1)S(1)}, bf16[96,2048]{1,0:T(8,128)(2,1)S(1)}, ...), branch_computations={%region_5.6_spmd, %region_6.7_spmd} | conditional | flops 2949120 | bytes 56515164 | solution.py:369
  57.2 15.9 %branch_1_fun.1 = (bf16[2,288,1024]{2,1,0:T(8,128)(2,1)}, bf16[2,288,1024]{2,1,0:T(8,128)(2,1)}, bf16[2,288,1024]{2,1,0:T(8,128)(2,1)}, bf16[2,288,1024]{2,1,0:T(8,128)(2,1)}) custom-call(s32[2]{0:T(128)S(1)} %get-tuple-element.22.ids, bf16[288,384]{1,0:T(8,128)(2,1)S(1)} %get-tuple-element.23.select_ref, bf16[96,2048]{1,0:T(8,128)(2,1)S(1)} %get-tuple-element.24.p0, ...), custom_call_target="tpu_custom_call" | custom-call | bytes 40000000 | tf_op jit(solution)/shard_map/cond/branch_1_fun/pallas_call | solution.py:143
  73.3 1.7 convert_element_type.99
  74.9 1.3 collective-permute-done
  76.9 2.0 collective-permute-start.12
  78.9 10.3 %shard_map.73 = (bf16[2,144,1024]{2,1,0:T(8,128)(2,1)}, bf16[2,144,1024]{2,1,0:T(8,128)(2,1)}, bf16[2,144,1024]{2,1,0:T(8,128)(2,1)}, bf16[2,144,1024]{2,1,0:T(8,128)(2,1)}) custom-call(s32[2]{0:T(128)S(1)} %pad_add_fusion.1.ids, bf16[288,384]{1,0:T(8,128)(2,1)} %copy-done.4, bf16[96,2048]{1,0:T(8,128)(2,1)} %collective-permute-done.5.p0, ...), custom_call_target="tpu_custom_call" | custom-call | bytes 60000000 | tf_op jit(solution)/shard_map/pallas_call | solution.py:180
  90.1 3.0 %collective-permute-done.15 = bf16[2,144,1024]{2,1,0:T(8,128)(2,1)S(1)} collective-permute-done((bf16[2,144,1024]{2,1,0:T(8,128)(2,1)}, bf16[2,144,1024]{2,1,0:T(8,128)(2,1)S(1)}, u32[]{:S(2)}, u32[]{:S(2)}) %collective-permute-start.15) | collective-permute-done | bytes 589856 | tf_op jit(solution)/shard_map/ppermute | solution.py:381
  94.2 3.5 %collective-permute-start.16 = (bf16[144,1024]{1,0:T(8,128)(2,1)S(1)}, bf16[144,1024]{1,0:T(8,128)(2,1)S(1)}, u32[]{:S(2)}, u32[]{:S(2)}) collective-permute-start(bf16[144,1024]{1,0:T(8,128)(2,1)S(1)} %fusion.14), channel_id=1, source_target_pairs={{0,2},{1,3},{2,0},{3,1},{4,6},{5,7},{6,4},{7,5},{8,10},{9,11},{10,... | collective-permute-start | bytes 884744 | tf_op jit(solution)/shard_map/ppermute | solution.py:383
  98.9 6.9 %collective-permute-done.12 = bf16[2,288,1024]{2,1,0:T(8,128)(2,1)S(1)} collective-permute-done((bf16[2,288,1024]{2,1,0:T(8,128)(2,1)S(1)}, bf16[2,288,1024]{2,1,0:T(8,128)(2,1)S(1)}, u32[]{:S(2)}, u32[]{:S(2)}) %collective-permute-start.12) | collective-permute-done | bytes 1179680 | tf_op jit(solution)/shard_map/ppermute | solution.py:373
  106.4 5.7 %collective-permute-done.16 = bf16[144,1024]{1,0:T(8,128)(2,1)S(1)} collective-permute-done((bf16[144,1024]{1,0:T(8,128)(2,1)S(1)}, bf16[144,1024]{1,0:T(8,128)(2,1)S(1)}, u32[]{:S(2)}, u32[]{:S(2)}) %collective-permute-start.16) | collective-permute-done | bytes 294944 | tf_op jit(solution)/shard_map/ppermute | solution.py:383
  112.1 5.7 %collective-permute-done.10 = bf16[144,1024]{1,0:T(8,128)(2,1)S(1)} collective-permute-done((bf16[144,1024]{1,0:T(8,128)(2,1)S(1)}, bf16[144,1024]{1,0:T(8,128)(2,1)S(1)}, u32[]{:S(2)}, u32[]{:S(2)}) %collective-permute-start.10) | collective-permute-done | bytes 294944 | tf_op jit(solution)/shard_map/ppermute | solution.py:383
  118.7 2.1 %collective-permute-start.13 = (bf16[2,144,1024]{2,1,0:T(8,128)(2,1)S(1)}, bf16[2,144,1024]{2,1,0:T(8,128)(2,1)S(1)}, u32[]{:S(2)}, u32[]{:S(2)}) collective-permute-start(bf16[2,144,1024]{2,1,0:T(8,128)(2,1)S(1)} %pad_maximum_fusion.mine_a), channel_id=1, source_target_pairs={{0,2},{1,3},{2,0},{3,1},{4,6},{5,7},{6,4},{7,5},{8,10},{9,11},{10,... | collective-permute-start | bytes 1769480 | tf_op jit(solution)/shard_map/ppermute | solution.py:387
  123.8 10.7 %shard_map.74 = (f32[144,2048]{1,0:T(8,128)}, f32[144,2048]{1,0:T(8,128)}) custom-call(s32[2]{0:T(128)S(1)} %pad_add_fusion.1.ids, bf16[2,144,1024]{2,1,0:T(8,128)(2,1)} %copy-done.1, bf16[2,144,1024]{2,1,0:T(8,128)(2,1)} %copy-done.11, bf16[2,144,1024]{2,1,0:T(8,128)(2,1)} %copy-done, bf16[2,144,1024]{2,1,0:T(8,128)(2,1)} %copy-done.12, ...), custom_call_target="tpu_custom_call" | custom-call | bytes 40000000 | tf_op jit(solution)/shard_map/pallas_call | solution.py:268
  136.0 11.5 %collective-permute-done.22.mine = bf16[2,144,1024]{2,1,0:T(8,128)(2,1)S(1)} collective-permute-done((bf16[2,144,1024]{2,1,0:T(8,128)(2,1)S(1)}, bf16[2,144,1024]{2,1,0:T(8,128)(2,1)S(1)}, u32[]{:S(2)}, u32[]{:S(2)}) %collective-permute-start.22) | collective-permute-done | bytes 589856 | tf_op jit(solution)/shard_map/ppermute | solution.py:387
  149.2 12.8 %shard_map.75 = (bf16[48,2048]{1,0:T(8,128)(2,1)}, bf16[48,2048]{1,0:T(8,128)(2,1)}, bf16[48,2048]{1,0:T(8,128)(2,1)}, bf16[48,2048]{1,0:T(8,128)(2,1)}) custom-call(s32[2]{0:T(128)S(1)} %pad_add_fusion.1.ids, bf16[192,144]{1,0:T(8,128)(2,1)} %bitcast.96, bf16[2,144,1024]{2,1,0:T(8,128)(2,1)} %copy-done.8, bf16[2,144,1024]{2,1,0:T(8,128)(2,1)} %copy-done.10, ...), custom_call_target="tpu_custom_call" | custom-call | bytes 40000000 | tf_op jit(solution)/shard_map/pallas_call | solution.py:287
  163.3 2.2 %collective-permute-start.20 = (bf16[48,2048]{1,0:T(8,128)(2,1)}, bf16[48,2048]{1,0:T(8,128)(2,1)S(1)}, u32[]{:S(2)}, u32[]{:S(2)}) collective-permute-start(bf16[48,2048]{1,0:T(8,128)(2,1)} %get-tuple-element.70), channel_id=1, source_target_pairs={{0,8},{4,12},{8,0},{12,4},{1,9},{5,13},{9,1},{13,5},{2,10},{6,14},... | collective-permute-start | bytes 589832 | tf_op jit(solution)/shard_map/ppermute | solution.py:396
  165.5 1.3 collective-permute-start.21
  166.8 1.3 compare_select_fusion.3
  168.9 12.9 %shard_map.76 = (bf16[48,2048]{1,0:T(8,128)(2,1)}, bf16[48,2048]{1,0:T(8,128)(2,1)}, bf16[48,2048]{1,0:T(8,128)(2,1)}, bf16[48,2048]{1,0:T(8,128)(2,1)}) custom-call(s32[2]{0:T(128)S(1)} %pad_add_fusion.1.ids, bf16[192,144]{1,0:T(8,128)(2,1)} %bitcast.95, bf16[2,144,1024]{2,1,0:T(8,128)(2,1)} %copy-done.7, bf16[2,144,1024]{2,1,0:T(8,128)(2,1)} %copy-done.9, ...), custom_call_target="tpu_custom_call" | custom-call | bytes 40000000 | tf_op jit(solution)/shard_map/pallas_call | solution.py:287
  183.3 2.6 %collective-permute-start.26 = (bf16[48,2048]{1,0:T(8,128)(2,1)}, bf16[48,2048]{1,0:T(8,128)(2,1)S(1)}, u32[]{:S(2)}, u32[]{:S(2)}) collective-permute-start(bf16[48,2048]{1,0:T(8,128)(2,1)} %get-tuple-element.77), channel_id=1, source_target_pairs={{0,12},{4,0},{8,4},{12,8},{1,13},{5,1},{9,5},{13,9},{2,14},{6,2},{... | collective-permute-start | bytes 589832 | tf_op jit(solution)/shard_map/ppermute | solution.py:396
  186.1 5.7 %collective-permute-done.24 = bf16[48,2048]{1,0:T(8,128)(2,1)S(1)} collective-permute-done((bf16[48,2048]{1,0:T(8,128)(2,1)}, bf16[48,2048]{1,0:T(8,128)(2,1)S(1)}, u32[]{:S(2)}, u32[]{:S(2)}) %collective-permute-start.24) | collective-permute-done | bytes 196640 | tf_op jit(solution)/shard_map/ppermute | solution.py:396
  191.8 7.2 %collective-permute-done.25 = bf16[48,2048]{1,0:T(8,128)(2,1)S(1)} collective-permute-done((bf16[48,2048]{1,0:T(8,128)(2,1)}, bf16[48,2048]{1,0:T(8,128)(2,1)S(1)}, u32[]{:S(2)}, u32[]{:S(2)}) %collective-permute-start.25) | collective-permute-done | bytes 196640 | tf_op jit(solution)/shard_map/ppermute | solution.py:396
  (94 shorter events, 24.3 us)
Async XLA Ops:
  0.0 21.3 %collective-permute-start.1 = (bf16[96,2048]{1,0:T(8,128)(2,1)}, bf16[96,2048]{1,0:T(8,128)(2,1)S(1)}, u32[]{:S(2)}, u32[]{:S(2)}) collective-permute-start(bf16[96,2048]{1,0:T(8,128)(2,1)} %param.9), channel_id=1, source_target_pairs={{0,0},{1,4},{2,8},{3,12},{4,1},{5,5},{6,9},{7,13},{8,2},{9,6},{10,... | collective-permute-start | bytes 1179656 | tf_op jit(solution)/shard_map/ppermute | solution.py:323
  1.6 19.7 %collective-permute-start.2 = (bf16[96,2048]{1,0:T(8,128)(2,1)}, bf16[96,2048]{1,0:T(8,128)(2,1)S(1)}, u32[]{:S(2)}, u32[]{:S(2)}) collective-permute-start(bf16[96,2048]{1,0:T(8,128)(2,1)} %param.9), channel_id=1, source_target_pairs={{0,4},{1,8},{2,12},{3,0},{4,5},{5,9},{6,13},{7,1},{8,6},{9,10},{10... | collective-permute-start | bytes 1179656 | tf_op jit(solution)/shard_map/ppermute | solution.py:323
  5.0 18.2 %collective-permute-start.3 = (bf16[96,2048]{1,0:T(8,128)(2,1)}, bf16[96,2048]{1,0:T(8,128)(2,1)S(1)}, u32[]{:S(2)}, u32[]{:S(2)}) collective-permute-start(bf16[96,2048]{1,0:T(8,128)(2,1)} %param.9), channel_id=1, source_target_pairs={{0,8},{1,12},{2,0},{3,4},{4,9},{5,13},{6,1},{7,5},{8,10},{9,14},{1... | collective-permute-start | bytes 1179656 | tf_op jit(solution)/shard_map/ppermute | solution.py:323
  11.0 20.0 %collective-permute-start.4 = (bf16[96,2048]{1,0:T(8,128)(2,1)}, bf16[96,2048]{1,0:T(8,128)(2,1)S(1)}, u32[]{:S(2)}, u32[]{:S(2)}) collective-permute-start(bf16[96,2048]{1,0:T(8,128)(2,1)} %param.9), channel_id=1, source_target_pairs={{0,12},{1,0},{2,4},{3,8},{4,13},{5,1},{6,5},{7,9},{8,14},{9,2},{10... | collective-permute-start | bytes 1179656 | tf_op jit(solution)/shard_map/ppermute | solution.py:323
  31.1 47.9 %collective-permute-start.5 = (bf16[96,2048]{1,0:T(8,128)(2,1)}, bf16[96,2048]{1,0:T(8,128)(2,1)}, u32[]{:S(2)}, u32[]{:S(2)}) collective-permute-start(bf16[96,2048]{1,0:T(8,128)(2,1)} %param.10), channel_id=1, source_target_pairs={{0,0},{1,4},{2,8},{3,12},{4,1},{5,5},{6,9},{7,13},{8,2},{9,6},{10,... | collective-permute-start | bytes 1179656 | tf_op jit(solution)/shard_map/ppermute | solution.py:323
  35.5 43.4 %collective-permute-start.6 = (bf16[96,2048]{1,0:T(8,128)(2,1)}, bf16[96,2048]{1,0:T(8,128)(2,1)}, u32[]{:S(2)}, u32[]{:S(2)}) collective-permute-start(bf16[96,2048]{1,0:T(8,128)(2,1)} %param.10), channel_id=1, source_target_pairs={{0,4},{1,8},{2,12},{3,0},{4,5},{5,9},{6,13},{7,1},{8,6},{9,10},{10... | collective-permute-start | bytes 1179656 | tf_op jit(solution)/shard_map/ppermute | solution.py:323
  44.2 34.8 %collective-permute-start.7 = (bf16[96,2048]{1,0:T(8,128)(2,1)}, bf16[96,2048]{1,0:T(8,128)(2,1)}, u32[]{:S(2)}, u32[]{:S(2)}) collective-permute-start(bf16[96,2048]{1,0:T(8,128)(2,1)} %param.10), channel_id=1, source_target_pairs={{0,8},{1,12},{2,0},{3,4},{4,9},{5,13},{6,1},{7,5},{8,10},{9,14},{1... | collective-permute-start | bytes 1179656 | tf_op jit(solution)/shard_map/ppermute | solution.py:323
  53.0 26.0 %collective-permute-start.8 = (bf16[96,2048]{1,0:T(8,128)(2,1)}, bf16[96,2048]{1,0:T(8,128)(2,1)}, u32[]{:S(2)}, u32[]{:S(2)}) collective-permute-start(bf16[96,2048]{1,0:T(8,128)(2,1)} %param.10), channel_id=1, source_target_pairs={{0,12},{1,0},{2,4},{3,8},{4,13},{5,1},{6,5},{7,9},{8,14},{9,2},{10... | collective-permute-start | bytes 1179656 | tf_op jit(solution)/shard_map/ppermute | solution.py:323
  73.1 3.1 %collective-permute-start = (bf16[2,288,1024]{2,1,0:T(8,128)(2,1)}, bf16[2,288,1024]{2,1,0:T(8,128)(2,1)S(1)}, u32[]{:S(2)}, u32[]{:S(2)}) collective-permute-start(bf16[2,288,1024]{2,1,0:T(8,128)(2,1)} %get-tuple-element.31), channel_id=1, source_target_pairs={{0,1},{1,0},{2,3},{3,2},{4,5},{5,4},{6,7},{7,6},{8,9},{9,8},{10,11... | collective-permute-start | bytes 3538952 | tf_op jit(solution)/shard_map/cond/branch_1_fun/ppermute | solution.py:362
  76.9 12.3 %copy-start.3 = (bf16[2,288,1024]{2,1,0:T(8,128)(2,1)S(1)}, bf16[2,288,1024]{2,1,0:T(8,128)(2,1)}, u32[]{:S(2)}) copy-start(bf16[2,288,1024]{2,1,0:T(8,128)(2,1)} %get-tuple-element.63) | copy-start | bytes 3538948
  76.9 28.9 %collective-permute-start.12 = (bf16[2,288,1024]{2,1,0:T(8,128)(2,1)S(1)}, bf16[2,288,1024]{2,1,0:T(8,128)(2,1)S(1)}, u32[]{:S(2)}, u32[]{:S(2)}) collective-permute-start(bf16[2,288,1024]{2,1,0:T(8,128)(2,1)S(1)} %get-tuple-element.56), channel_id=1, source_target_pairs={{0,2},{1,3},{2,0},{3,1},{4,6},{5,7},{6,4},{7,5},{8,10},{9,11},{10,... | collective-permute-start | bytes 3538952 | tf_op jit(solution)/shard_map/ppermute | solution.py:373
  89.3 16.5 %collective-permute-start.11 = (bf16[2,288,1024]{2,1,0:T(8,128)(2,1)S(1)}, bf16[2,288,1024]{2,1,0:T(8,128)(2,1)S(1)}, u32[]{:S(2)}, u32[]{:S(2)}) collective-permute-start(bf16[2,288,1024]{2,1,0:T(8,128)(2,1)S(1)} %copy-done.3), channel_id=1, source_target_pairs={{0,1},{1,0},{2,3},{3,2},{4,5},{5,4},{6,7},{7,6},{8,9},{9,8},{10,11... | collective-permute-start | bytes 3538952 | tf_op jit(solution)/shard_map/ppermute | solution.py:376
  89.3 3.8 %collective-permute-start.15 = (bf16[2,144,1024]{2,1,0:T(8,128)(2,1)}, bf16[2,144,1024]{2,1,0:T(8,128)(2,1)S(1)}, u32[]{:S(2)}, u32[]{:S(2)}) collective-permute-start(bf16[2,144,1024]{2,1,0:T(8,128)(2,1)} %get-tuple-element.65), channel_id=1, source_target_pairs={{0,1},{1,0},{2,3},{3,2},{4,5},{5,4},{6,7},{7,6},{8,9},{9,8},{10,11... | collective-permute-start | bytes 1769480 | tf_op jit(solution)/shard_map/ppermute | solution.py:381
  89.8 7.9 %collective-permute-start.9 = (bf16[2,144,1024]{2,1,0:T(8,128)(2,1)}, bf16[2,144,1024]{2,1,0:T(8,128)(2,1)S(1)}, u32[]{:S(2)}, u32[]{:S(2)}) collective-permute-start(bf16[2,144,1024]{2,1,0:T(8,128)(2,1)} %get-tuple-element.60), channel_id=1, source_target_pairs={{0,1},{1,0},{2,3},{3,2},{4,5},{5,4},{6,7},{7,6},{8,9},{9,8},{10,11... | collective-permute-start | bytes 1769480 | tf_op jit(solution)/shard_map/ppermute | solution.py:381
  94.2 17.9 %collective-permute-start.16 = (bf16[144,1024]{1,0:T(8,128)(2,1)S(1)}, bf16[144,1024]{1,0:T(8,128)(2,1)S(1)}, u32[]{:S(2)}, u32[]{:S(2)}) collective-permute-start(bf16[144,1024]{1,0:T(8,128)(2,1)S(1)} %fusion.14), channel_id=1, source_target_pairs={{0,2},{1,3},{2,0},{3,1},{4,6},{5,7},{6,4},{7,5},{8,10},{9,11},{10,... | collective-permute-start | bytes 884744 | tf_op jit(solution)/shard_map/ppermute | solution.py:383
  98.8 19.0 %collective-permute-start.10 = (bf16[144,1024]{1,0:T(8,128)(2,1)S(1)}, bf16[144,1024]{1,0:T(8,128)(2,1)S(1)}, u32[]{:S(2)}, u32[]{:S(2)}) collective-permute-start(bf16[144,1024]{1,0:T(8,128)(2,1)S(1)} %fusion.13), channel_id=1, source_target_pairs={{0,2},{1,3},{2,0},{3,1},{4,6},{5,7},{6,4},{7,5},{8,10},{9,11},{10,... | collective-permute-start | bytes 884744 | tf_op jit(solution)/shard_map/ppermute | solution.py:383
  105.8 12.1 %copy-start.6 = (bf16[2,144,1024]{2,1,0:T(8,128)(2,1)S(1)}, bf16[2,144,1024]{2,1,0:T(8,128)(2,1)}, u32[]{:S(2)}) copy-start(bf16[2,144,1024]{2,1,0:T(8,128)(2,1)} %get-tuple-element.64) | copy-start | bytes 1769476
  118.7 3.1 %collective-permute-start.14 = (bf16[2,144,1024]{2,1,0:T(8,128)(2,1)S(1)}, bf16[2,144,1024]{2,1,0:T(8,128)(2,1)S(1)}, u32[]{:S(2)}, u32[]{:S(2)}) collective-permute-start(bf16[2,144,1024]{2,1,0:T(8,128)(2,1)S(1)} %pad_maximum_fusion.mine_a), channel_id=1, source_target_pairs={{0,1},{1,0},{2,3},{3,2},{4,5},{5,4},{6,7},{7,6},{8,9},{9,8},{10,11... | collective-permute-start | bytes 1769480 | tf_op jit(solution)/shard_map/ppermute | solution.py:386
  118.7 16.3 %collective-permute-start.13 = (bf16[2,144,1024]{2,1,0:T(8,128)(2,1)S(1)}, bf16[2,144,1024]{2,1,0:T(8,128)(2,1)S(1)}, u32[]{:S(2)}, u32[]{:S(2)}) collective-permute-start(bf16[2,144,1024]{2,1,0:T(8,128)(2,1)S(1)} %pad_maximum_fusion.mine_a), channel_id=1, source_target_pairs={{0,2},{1,3},{2,0},{3,1},{4,6},{5,7},{6,4},{7,5},{8,10},{9,11},{10,... | collective-permute-start | bytes 1769480 | tf_op jit(solution)/shard_map/ppermute | solution.py:387
  120.9 2.1 %collective-permute-start.17 = (bf16[2,144,1024]{2,1,0:T(8,128)(2,1)S(1)}, bf16[2,144,1024]{2,1,0:T(8,128)(2,1)S(1)}, u32[]{:S(2)}, u32[]{:S(2)}) collective-permute-start(bf16[2,144,1024]{2,1,0:T(8,128)(2,1)S(1)} %pad_maximum_fusion.1.mine_b), channel_id=1, source_target_pairs={{0,1},{1,0},{2,3},{3,2},{4,5},{5,4},{6,7},{7,6},{8,9},{9,8},{10,11... | collective-permute-start | bytes 1769480 | tf_op jit(solution)/shard_map/ppermute | solution.py:386
  121.3 26.2 %collective-permute-start.22 = (bf16[2,144,1024]{2,1,0:T(8,128)(2,1)S(1)}, bf16[2,144,1024]{2,1,0:T(8,128)(2,1)S(1)}, u32[]{:S(2)}, u32[]{:S(2)}) collective-permute-start(bf16[2,144,1024]{2,1,0:T(8,128)(2,1)S(1)} %pad_maximum_fusion.1.mine_b), channel_id=1, source_target_pairs={{0,2},{1,3},{2,0},{3,1},{4,6},{5,7},{6,4},{7,5},{8,10},{9,11},{10,... | collective-permute-start | bytes 1769480 | tf_op jit(solution)/shard_map/ppermute | solution.py:387
  135.0 13.3 %copy-start.8 = (bf16[2,144,1024]{2,1,0:T(8,128)(2,1)}, bf16[2,144,1024]{2,1,0:T(8,128)(2,1)S(1)}, u32[]{:S(2)}) copy-start(bf16[2,144,1024]{2,1,0:T(8,128)(2,1)S(1)} %collective-permute-done.13.mine) | copy-start | bytes 1769476
  135.0 13.3 %collective-permute-start.18 = (bf16[2,144,1024]{2,1,0:T(8,128)(2,1)S(1)}, bf16[2,144,1024]{2,1,0:T(8,128)(2,1)S(1)}, u32[]{:S(2)}, u32[]{:S(2)}) collective-permute-start(bf16[2,144,1024]{2,1,0:T(8,128)(2,1)S(1)} %collective-permute-done.13.mine), channel_id=1, source_target_pairs={{0,1},{1,0},{2,3},{3,2},{4,5},{5,4},{6,7},{7,6},{8,9},{9,8},{10,11... | collective-permute-start | bytes 1769480 | tf_op jit(solution)/shard_map/ppermute | solution.py:391
  147.4 14.6 %copy-start.7 = (bf16[2,144,1024]{2,1,0:T(8,128)(2,1)}, bf16[2,144,1024]{2,1,0:T(8,128)(2,1)S(1)}, u32[]{:S(2)}) copy-start(bf16[2,144,1024]{2,1,0:T(8,128)(2,1)S(1)} %collective-permute-done.22.mine) | copy-start | bytes 1769476
  147.4 20.6 %collective-permute-start.23 = (bf16[2,144,1024]{2,1,0:T(8,128)(2,1)S(1)}, bf16[2,144,1024]{2,1,0:T(8,128)(2,1)S(1)}, u32[]{:S(2)}, u32[]{:S(2)}) collective-permute-start(bf16[2,144,1024]{2,1,0:T(8,128)(2,1)S(1)} %collective-permute-done.22.mine), channel_id=1, source_target_pairs={{0,1},{1,0},{2,3},{3,2},{4,5},{5,4},{6,7},{7,6},{8,9},{9,8},{10,11... | collective-permute-start | bytes 1769480 | tf_op jit(solution)/shard_map/ppermute | solution.py:391
  162.0 21.3 %collective-permute-start.19 = (bf16[48,2048]{1,0:T(8,128)(2,1)}, bf16[48,2048]{1,0:T(8,128)(2,1)S(1)}, u32[]{:S(2)}, u32[]{:S(2)}) collective-permute-start(bf16[48,2048]{1,0:T(8,128)(2,1)} %get-tuple-element.69), channel_id=1, source_target_pairs={{0,4},{4,8},{8,12},{12,0},{1,5},{5,9},{9,13},{13,1},{2,6},{6,10},{... | collective-permute-start | bytes 589832 | tf_op jit(solution)/shard_map/ppermute | solution.py:396
  163.3 22.7 %collective-permute-start.20 = (bf16[48,2048]{1,0:T(8,128)(2,1)}, bf16[48,2048]{1,0:T(8,128)(2,1)S(1)}, u32[]{:S(2)}, u32[]{:S(2)}) collective-permute-start(bf16[48,2048]{1,0:T(8,128)(2,1)} %get-tuple-element.70), channel_id=1, source_target_pairs={{0,8},{4,12},{8,0},{12,4},{1,9},{5,13},{9,1},{13,5},{2,10},{6,14},... | collective-permute-start | bytes 589832 | tf_op jit(solution)/shard_map/ppermute | solution.py:396
  165.5 20.5 %collective-permute-start.21 = (bf16[48,2048]{1,0:T(8,128)(2,1)}, bf16[48,2048]{1,0:T(8,128)(2,1)S(1)}, u32[]{:S(2)}, u32[]{:S(2)}) collective-permute-start(bf16[48,2048]{1,0:T(8,128)(2,1)} %get-tuple-element.71), channel_id=1, source_target_pairs={{0,12},{4,0},{8,4},{12,8},{1,13},{5,1},{9,5},{13,9},{2,14},{6,2},{... | collective-permute-start | bytes 589832 | tf_op jit(solution)/shard_map/ppermute | solution.py:396
  168.9 17.1 %copy-start.13 = (bf16[48,2048]{1,0:T(8,128)(2,1)S(1)}, bf16[48,2048]{1,0:T(8,128)(2,1)}, u32[]{:S(2)}) copy-start(bf16[48,2048]{1,0:T(8,128)(2,1)} %get-tuple-element.68) | copy-start | bytes 589828
  181.8 10.0 %collective-permute-start.24 = (bf16[48,2048]{1,0:T(8,128)(2,1)}, bf16[48,2048]{1,0:T(8,128)(2,1)S(1)}, u32[]{:S(2)}, u32[]{:S(2)}) collective-permute-start(bf16[48,2048]{1,0:T(8,128)(2,1)} %get-tuple-element.75), channel_id=1, source_target_pairs={{0,4},{4,8},{8,12},{12,0},{1,5},{5,9},{9,13},{13,1},{2,6},{6,10},{... | collective-permute-start | bytes 589832 | tf_op jit(solution)/shard_map/ppermute | solution.py:396
  182.6 16.3 %collective-permute-start.25 = (bf16[48,2048]{1,0:T(8,128)(2,1)}, bf16[48,2048]{1,0:T(8,128)(2,1)S(1)}, u32[]{:S(2)}, u32[]{:S(2)}) collective-permute-start(bf16[48,2048]{1,0:T(8,128)(2,1)} %get-tuple-element.76), channel_id=1, source_target_pairs={{0,8},{4,12},{8,0},{12,4},{1,9},{5,13},{9,1},{13,5},{2,10},{6,14},... | collective-permute-start | bytes 589832 | tf_op jit(solution)/shard_map/ppermute | solution.py:396
  183.3 15.6 %collective-permute-start.26 = (bf16[48,2048]{1,0:T(8,128)(2,1)}, bf16[48,2048]{1,0:T(8,128)(2,1)S(1)}, u32[]{:S(2)}, u32[]{:S(2)}) collective-permute-start(bf16[48,2048]{1,0:T(8,128)(2,1)} %get-tuple-element.77), channel_id=1, source_target_pairs={{0,12},{4,0},{8,4},{12,8},{1,13},{5,1},{9,5},{13,9},{2,14},{6,2},{... | collective-permute-start | bytes 589832 | tf_op jit(solution)/shard_map/ppermute | solution.py:396
  (9 other events, 25.9 us)

commit v3 on v2

--- a/solution.py
+++ b/solution.py
@@ -8,7 +8,7 @@
 
 BF, F32 = jnp.bfloat16, jnp.float32
 ROW_CONTRACT = (((1,), (1,)), ((), ()))
-VMEM = 56 * 1024 * 1024
+VMEM = 49 * 1024 * 1024
 GATE_UP_COST, HIDDEN_COST, NEAR_COST, FAR_COST = 40000000, 60000000, 40000000, 40000000
 
 
@@ -244,11 +244,11 @@
 
 def far_kernel(ids, place_ref, mine, other, gate_w, up_w, first, o0, o1, o2, o3,
                grads_v, weight_v, first_v, out_v, sems, grad_sems, out_sems, first_sem):
+    begun = start(first, first_v, first_sem.at[0])
     moves, loads = back_begin(ids[0], 1 - ids[1], ((mine, other),), gate_w, up_w, grads_v, weight_v, sems, grad_sems)
-    moves.append(start(first, first_v, first_sem.at[0]))
     height = gate_w.shape[0] // CHUNKS
     piece = o0.shape[0]
-    for move in moves:
+    for move in [begun] + moves:
         move.wait()
     stores = []
     for chunk in range(CHUNKS):
@@ -323,8 +323,6 @@
         return lax.ppermute(value, ("tensor", "seq"), pairs)
 
     token_parts = [spread(tokens, k) for k in range(n)]
-    held = after(grad_out, *token_parts)
-    grad_parts = [spread(held, k) for k in range(n)]
 
     all_counts = lax.all_gather(counts, "seq", tiled=True)
     home, place_in = packing // shard_rows, packing % shard_rows
@@ -357,38 +355,44 @@
                      - jnp.where(mine_rank % sets == 0, target_begin[0, 0], target_begin[1, 0]), -1)
     final = (spot[:, None] == jnp.arange(sets * piece)[None, :]).astype(BF)
 
+    present = all_counts[0] >= 0
+    held = after(grad_out, select, present, *token_parts)
+    grad_parts = [spread(held, k) for k in range(n)]
+
     def project(ids, select, gate_weight, up_weight, *token_parts):
         send_far, keep_far, send_near, keep_near = gate_up(ids, select, token_parts, gate_weight, up_weight)
         got_far = lax.ppermute(send_far, "seq", sibling)
         return (keep_far.astype(F32) + got_far.astype(F32)).astype(BF), send_near, keep_near
 
-    def absent(ids, select, *rest):
+    def absent(*_):
         nothing = jnp.zeros((2, live_rows, gate_weight.shape[1] // 4), BF)
         return nothing, nothing, nothing
 
-    pair_far, send_near, keep_near = lax.cond(
-        packing[0] >= 0, project, absent, ids, select, gate_weight, up_weight, *token_parts
-    )
-
+    pair_far, send_near, keep_near = lax.cond(present, project, absent, ids, select, gate_weight, up_weight, *token_parts)
     across_near = lax.ppermute(pair_far, "seq", across)
 
     outs = hidden_grads(ids, after(select, pair_far), grad_parts, down_weight)
+    pairs = []
+    for m in range(sets):
+        got = lax.ppermute(outs[m], "seq", sibling)
+        keep = outs[sets + m]
+        pairs.append(((keep[0].astype(F32) + got[0].astype(F32)).astype(BF), keep[1].astype(F32) + got[1].astype(F32)))
     got_near = lax.ppermute(after(send_near, outs[0]), "seq", sibling)
     gate_near = keep_near.astype(F32) + got_near.astype(F32) + across_near.astype(F32)
-    ds, ds_core = [], []
+    ds, ds_core, ds_far = [], [], []
     for m in range(sets):
-        send, keep = outs[m], outs[sets + m]
-        got = lax.ppermute(send, "seq", sibling)
-        pair_far = (keep[0].astype(F32) + got[0].astype(F32)).astype(BF)
-        hid = keep[1].astype(F32) + got[1].astype(F32) + lax.ppermute(pair_far, "seq", across).astype(F32)
+        pair_far, pair_near = pairs[m]
+        got = lax.ppermute(pair_far, "seq", across)
+        if m > 0:
+            got = after(got, ds[m - 1])
         part = slice(m * set_rows, (m + 1) * set_rows)
-        ds.append(jnp.stack(derive(gate_near[0, part], gate_near[1, part], hid)))
+        ds.append(jnp.stack(derive(gate_near[0, part], gate_near[1, part], pair_near + got.astype(F32))))
         ds_core.append(lax.ppermute(ds[m], "seq", sibling))
-    ds_far = [lax.ppermute(d, "seq", across) for d in ds]
+        ds_far.append(lax.ppermute(ds[m], "seq", across))
     firsts = near(ids, ds, ds_core, gate_weight, up_weight)
-    pieces = []
+    pieces, parts = [], firsts
     for m in range(sets):
-        d_both = lax.ppermute(after(ds_far[m], firsts[0]), "seq", sibling)
+        d_both = lax.ppermute(after(ds_far[m], parts[0]), "seq", sibling)
         parts = far(ids, place[m].reshape(n * piece, set_rows), ds_far[m], d_both, gate_weight, up_weight, firsts[m])
         total = parts[0].astype(F32)
         for k in range(1, n):

time: 203 us -> 181 us (0.89)
  waiting for transfers between devices: 58.5 us -> 46.5 us
  Pallas kernels: 62.6 us -> 55.3 us
  starting transfers between devices: 51.5 us -> 57.8 us
  other arithmetic: 10.8 us -> 6.33 us
  local copies, waits for them, and re-layouts: 7.71 us -> 3.29 us
    ppermute x8, waiting for transfers between devices: 26.5 us -> 13.6 us  [the longest x2 9 us: tuned(): got = lax.ppermute(pair_far, 'seq', across)]
    ppermute x8, starting transfers between devices: 6.61 us -> 13.3 us  [the longest x2 7.17 us: tuned(): got = lax.ppermute(pair_far, 'seq', across)]
    pallas_call x2, Pallas kernels: 25.7 us -> 20.8 us  [far(): call(far_kernel, [IN_SMEM, IN_VMEM] + [IN_HBM] * 5, [((count // 4, depth)...]
    unnamed x29 -> x5, local copies, waits for them, and re-layouts: 5.18 us -> 2.74 us
  transfers between devices with their start and end apart: 27 -> 27, of which waited for: 12 -> 11; matrix products, arithmetic and copies ran while one was open for 7% -> 6% of each run, Pallas kernels for 31% -> 31%
where the time goes in v3:
time: 181 us; the launch traced here: 179 us
  starting transfers between devices  57.8 us (32%)
  Pallas kernels  55.3 us (31%)
  waiting for transfers between devices  46.5 us (26%)
  other arithmetic  6.33 us (3%)
  blocking collectives  6.02 us (3%)
  local copies, waits for them, and re-layouts  3.29 us (2%)
  matrix products  2.17 us (1%)
    ppermute x8, starting transfers between devices, spread(): return lax.ppermute(value, ('tensor', 'seq'), pairs)  33.5 us
    pallas_call x2, Pallas kernels, far(): call(far_kernel, [IN_SMEM, IN_VMEM] + [IN_HBM] * 5, [((count // 4, depth)...  20.8 us
    pallas_call x1, Pallas kernels, gate_up(): call(gate_up_kernel, [IN_SMEM, IN_VMEM] + [IN_HBM] * 6, [((2, count, bloc...  15.5 us
    ppermute x6, waiting for transfers between devices, tuned(): total += lax.ppermute(parts[k], 'tensor', shift).astype(F32)  13.9 us
    pallas_call x1, Pallas kernels, hidden_grads(): call(hidden_kernel, [IN_SMEM, IN_VMEM] + [IN_HBM] * 5, [((2, count // 2,...  9.78 us
    ppermute x6, starting transfers between devices, tuned(): total += lax.ppermute(parts[k], 'tensor', shift).astype(F32)  9.42 us
    pallas_call x1, Pallas kernels, near(): call(near_kernel, [IN_SMEM] + [IN_HBM] * 6, [((rows, depth), F32)] * 2, [...  9.21 us
    ppermute x2, waiting for transfers between devices, tuned(): got = lax.ppermute(pair_far, 'seq', across)  9 us
  transfers between devices with their start and end apart: 27, of which 11 were waited for; matrix products, arithmetic and copies ran while one was open for 6% of the time, Pallas kernels for 31%

profile of v3, /device:TPU:0, one launch (start us, length us, event | category | flops | bytes accessed | tf_op | source)
XLA Modules:
  0.0 178.5 jit_solution(8965402775225312871)
XLA Ops:
  0.0 1.6 collective-permute-start.1
  1.6 3.4 %collective-permute-start.2 = (bf16[96,2048]{1,0:T(8,128)(2,1)}, bf16[96,2048]{1,0:T(8,128)(2,1)}, u32[]{:S(2)}, u32[]{:S(2)}) collective-permute-start(bf16[96,2048]{1,0:T(8,128)(2,1)} %param.9), channel_id=1, source_target_pairs={{0,4},{1,8},{2,12},{3,0},{4,5},{5,9},{6,13},{7,1},{8,6},{9,10},{10... | collective-permute-start | bytes 1179656 | tf_op jit(solution)/shard_map/ppermute | solution.py:323
  5.0 3.4 %collective-permute-start.3 = (bf16[96,2048]{1,0:T(8,128)(2,1)}, bf16[96,2048]{1,0:T(8,128)(2,1)}, u32[]{:S(2)}, u32[]{:S(2)}) collective-permute-start(bf16[96,2048]{1,0:T(8,128)(2,1)} %param.9), channel_id=1, source_target_pairs={{0,8},{1,12},{2,0},{3,4},{4,9},{5,13},{6,1},{7,5},{8,10},{9,14},{1... | collective-permute-start | bytes 1179656 | tf_op jit(solution)/shard_map/ppermute | solution.py:323
  9.0 1.2 dynamic-slice
  11.0 2.6 %collective-permute-start.4 = (bf16[96,2048]{1,0:T(8,128)(2,1)}, bf16[96,2048]{1,0:T(8,128)(2,1)S(1)}, u32[]{:S(2)}, u32[]{:S(2)}) collective-permute-start(bf16[96,2048]{1,0:T(8,128)(2,1)} %param.9), channel_id=1, source_target_pairs={{0,12},{1,0},{2,4},{3,8},{4,13},{5,1},{6,5},{7,9},{8,14},{9,2},{10... | collective-permute-start | bytes 1179656 | tf_op jit(solution)/shard_map/ppermute | solution.py:323
  13.7 6.0 %all-reduce = s32[4]{0:T(128)S(1)} all-reduce(s32[4]{0:T(128)S(1)} %dynamic-update-slice), channel_id=1, replica_groups=mesh['group'=2,'tensor'=4,'seq'=4] {'seq'}, use_global_device_ids=true, to_apply=%add | all-reduce | flops 4 | bytes 32
  23.2 7.8 %collective-permute-done.4 = bf16[96,2048]{1,0:T(8,128)(2,1)S(1)} collective-permute-done((bf16[96,2048]{1,0:T(8,128)(2,1)}, bf16[96,2048]{1,0:T(8,128)(2,1)S(1)}, u32[]{:S(2)}, u32[]{:S(2)}) %collective-permute-start.4) | collective-permute-done | bytes 393248 | tf_op jit(solution)/shard_map/ppermute | solution.py:323
  31.8 1.6 collective-permute-start.5
  33.4 11.5 %collective-permute-start.6 = (bf16[96,2048]{1,0:T(8,128)(2,1)}, bf16[96,2048]{1,0:T(8,128)(2,1)S(1)}, u32[]{:S(2)}, u32[]{:S(2)}) collective-permute-start(bf16[96,2048]{1,0:T(8,128)(2,1)} %param.10), channel_id=1, source_target_pairs={{0,4},{1,8},{2,12},{3,0},{4,5},{5,9},{6,13},{7,1},{8,6},{9,10},{10... | collective-permute-start | bytes 1179656 | tf_op jit(solution)/shard_map/ppermute | solution.py:323
  44.9 8.8 %collective-permute-start.7 = (bf16[96,2048]{1,0:T(8,128)(2,1)}, bf16[96,2048]{1,0:T(8,128)(2,1)S(1)}, u32[]{:S(2)}, u32[]{:S(2)}) collective-permute-start(bf16[96,2048]{1,0:T(8,128)(2,1)} %param.10), channel_id=1, source_target_pairs={{0,8},{1,12},{2,0},{3,4},{4,9},{5,13},{6,1},{7,5},{8,10},{9,14},{1... | collective-permute-start | bytes 1179656 | tf_op jit(solution)/shard_map/ppermute | solution.py:323
  54.4 19.1 %conditional.1 = (bf16[2,288,1024]{2,1,0:T(8,128)(2,1)S(1)}, bf16[2,288,1024]{2,1,0:T(8,128)(2,1)S(1)}, f32[2,288,1024]{2,1,0:T(8,128)S(1)}) conditional(s32[]{:T(128)} %convert_element_type.136, () %tuple.21, (s32[2]{0:T(128)S(1)}, bf16[288,384]{1,0:T(8,128)(2,1)S(1)}, bf16[96,2048]{1,0:T(8,128)(2,1)S(1)}, bf16[96,2048]{1,0:T(8,128)(2,1)}, ...), branch_computations={%region_5.6_spmd, %region_6.7_spmd} | conditional | flops 2949120 | bytes 51796544 | solution.py:371
  54.4 15.5 %branch_1_fun.1 = (bf16[2,288,1024]{2,1,0:T(8,128)(2,1)S(1)}, bf16[2,288,1024]{2,1,0:T(8,128)(2,1)S(1)}, bf16[2,288,1024]{2,1,0:T(8,128)(2,1)S(1)}, bf16[2,288,1024]{2,1,0:T(8,128)(2,1)S(1)}) custom-call(s32[2]{0:T(128)S(1)} %get-tuple-element.22.ids, bf16[288,384]{1,0:T(8,128)(2,1)S(1)} %get-tuple-element.23.select_ref, ...), custom_call_target="tpu_custom_call" | custom-call | bytes 40000000 | tf_op jit(solution)/shard_map/cond/branch_1_fun/pallas_call | solution.py:143
  70.4 2.5 %collective-permute-done = bf16[2,288,1024]{2,1,0:T(8,128)(2,1)S(1)} collective-permute-done((bf16[2,288,1024]{2,1,0:T(8,128)(2,1)S(1)}, bf16[2,288,1024]{2,1,0:T(8,128)(2,1)S(1)}, u32[]{:S(2)}, u32[]{:S(2)}) %collective-permute-start) | collective-permute-done | bytes 1179680 | tf_op jit(solution)/shard_map/cond/branch_1_fun/ppermute | solution.py:364
  74.8 9.8 %shard_map.73 = (bf16[2,144,1024]{2,1,0:T(8,128)(2,1)S(1)}, bf16[2,144,1024]{2,1,0:T(8,128)(2,1)S(1)}, bf16[2,144,1024]{2,1,0:T(8,128)(2,1)S(1)}, bf16[2,144,1024]{2,1,0:T(8,128)(2,1)S(1)}) custom-call(s32[2]{0:T(128)S(1)} %pad_add_fusion.1.ids, bf16[288,384]{1,0:T(8,128)(2,1)S(1)} %convolution_convert_fusion.1.select_ref, ...), custom_call_target="tpu_custom_call" | custom-call | bytes 60000000 | tf_op jit(solution)/shard_map/pallas_call | solution.py:180
  85.4 2.9 %collective-permute-done.9 = bf16[2,144,1024]{2,1,0:T(8,128)(2,1)S(1)} collective-permute-done((bf16[2,144,1024]{2,1,0:T(8,128)(2,1)S(1)}, bf16[2,144,1024]{2,1,0:T(8,128)(2,1)S(1)}, u32[]{:S(2)}, u32[]{:S(2)}) %collective-permute-start.9) | collective-permute-done | bytes 589856 | tf_op jit(solution)/shard_map/ppermute | solution.py:377
  88.4 6.4 %collective-permute-start.10 = (bf16[144,1024]{1,0:T(8,128)(2,1)S(1)}, bf16[144,1024]{1,0:T(8,128)(2,1)S(1)}, u32[]{:S(2)}, u32[]{:S(2)}) collective-permute-start(bf16[144,1024]{1,0:T(8,128)(2,1)S(1)} %fusion.13), channel_id=1, source_target_pairs={{0,2},{1,3},{2,0},{3,1},{4,6},{5,7},{6,4},{7,5},{8,10},{9,11},{10,... | collective-permute-start | bytes 884744 | tf_op jit(solution)/shard_map/ppermute | solution.py:385
  95.7 7.9 %collective-permute-done.12 = bf16[2,288,1024]{2,1,0:T(8,128)(2,1)S(1)} collective-permute-done((bf16[2,288,1024]{2,1,0:T(8,128)(2,1)S(1)}, bf16[2,288,1024]{2,1,0:T(8,128)(2,1)S(1)}, u32[]{:S(2)}, u32[]{:S(2)}) %collective-permute-start.12) | collective-permute-done | bytes 1179680 | tf_op jit(solution)/shard_map/ppermute | solution.py:372
  104.1 5.8 %collective-permute-done.10 = bf16[144,1024]{1,0:T(8,128)(2,1)S(1)} collective-permute-done((bf16[144,1024]{1,0:T(8,128)(2,1)S(1)}, bf16[144,1024]{1,0:T(8,128)(2,1)S(1)}, u32[]{:S(2)}, u32[]{:S(2)}) %collective-permute-start.10) | collective-permute-done | bytes 294944 | tf_op jit(solution)/shard_map/ppermute | solution.py:385
  110.4 2.5 %collective-permute-start.13 = (bf16[2,144,1024]{2,1,0:T(8,128)(2,1)S(1)}, bf16[2,144,1024]{2,1,0:T(8,128)(2,1)S(1)}, u32[]{:S(2)}, u32[]{:S(2)}) collective-permute-start(bf16[2,144,1024]{2,1,0:T(8,128)(2,1)S(1)} %pad_maximum_fusion.mine_a), channel_id=1, source_target_pairs={{0,2},{1,3},{2,0},{3,1},{4,6},{5,7},{6,4},{7,5},{8,10},{9,11},{10,... | collective-permute-start | bytes 1769480 | tf_op jit(solution)/shard_map/ppermute | solution.py:391
  112.9 3.2 %collective-permute-done.16 = bf16[144,1024]{1,0:T(8,128)(2,1)S(1)} collective-permute-done((bf16[144,1024]{1,0:T(8,128)(2,1)S(1)}, bf16[144,1024]{1,0:T(8,128)(2,1)S(1)}, u32[]{:S(2)}, u32[]{:S(2)}) %collective-permute-start.16) | collective-permute-done | bytes 294944 | tf_op jit(solution)/shard_map/ppermute | solution.py:385
  117.0 2.5 %collective-permute-start.22 = (bf16[2,144,1024]{2,1,0:T(8,128)(2,1)S(1)}, bf16[2,144,1024]{2,1,0:T(8,128)(2,1)S(1)}, u32[]{:S(2)}, u32[]{:S(2)}) collective-permute-start(bf16[2,144,1024]{2,1,0:T(8,128)(2,1)S(1)} %pad_maximum_fusion.1.mine_b), channel_id=1, source_target_pairs={{0,2},{1,3},{2,0},{3,1},{4,6},{5,7},{6,4},{7,5},{8,10},{9,11},{10,... | collective-permute-start | bytes 1769480 | tf_op jit(solution)/shard_map/ppermute | solution.py:391
  119.5 9.2 %shard_map.74 = (f32[144,2048]{1,0:T(8,128)S(1)}, f32[144,2048]{1,0:T(8,128)S(1)}) custom-call(s32[2]{0:T(128)S(1)} %pad_add_fusion.1.ids, bf16[2,144,1024]{2,1,0:T(8,128)(2,1)S(1)} %pad_maximum_fusion.mine_a, bf16[2,144,1024]{2,1,0:T(8,128)(2,1)S(1)} %collective-permute-done.14.other_a, bf16[2,144,1024]{2,1,0:T(8,128)(2,1)S(1)} %pad_maximum_fusion.1.mine_b, ...), custom_call_target="tpu_custom_call" | custom-call | bytes 40000000 | tf_op jit(solution)/shard_map/pallas_call | solution.py:268
  129.3 1.6 collective-permute-done.18.other
  130.8 10.4 %shard_map.75 = (bf16[48,2048]{1,0:T(8,128)(2,1)S(1)}, bf16[48,2048]{1,0:T(8,128)(2,1)S(1)}, bf16[48,2048]{1,0:T(8,128)(2,1)S(1)}, bf16[48,2048]{1,0:T(8,128)(2,1)S(1)}) custom-call(s32[2]{0:T(128)S(1)} %pad_add_fusion.1.ids, bf16[192,144]{1,0:T(8,128)(2,1)S(1)} %bitcast.97, bf16[2,144,1024]{2,1,0:T(8,128)(2,1)S(1)} %collective-permute-done.13.mine, ...), custom_call_target="tpu_custom_call" | custom-call | bytes 40000000 | tf_op jit(solution)/shard_map/pallas_call | solution.py:287
  142.2 2.2 %collective-permute-start.19 = (bf16[48,2048]{1,0:T(8,128)(2,1)S(1)}, bf16[48,2048]{1,0:T(8,128)(2,1)S(1)}, u32[]{:S(2)}, u32[]{:S(2)}) collective-permute-start(bf16[48,2048]{1,0:T(8,128)(2,1)S(1)} %get-tuple-element.71), channel_id=1, source_target_pairs={{0,4},{4,8},{8,12},{12,0},{1,5},{5,9},{9,13},{13,1},{2,6},{6,10},{... | collective-permute-start | bytes 589832 | tf_op jit(solution)/shard_map/ppermute | solution.py:400
  144.4 2.7 %collective-permute-start.20 = (bf16[48,2048]{1,0:T(8,128)(2,1)S(1)}, bf16[48,2048]{1,0:T(8,128)(2,1)S(1)}, u32[]{:S(2)}, u32[]{:S(2)}) collective-permute-start(bf16[48,2048]{1,0:T(8,128)(2,1)S(1)} %get-tuple-element.72), channel_id=1, source_target_pairs={{0,8},{4,12},{8,0},{12,4},{1,9},{5,13},{9,1},{13,5},{2,10},{6,14},... | collective-permute-start | bytes 589832 | tf_op jit(solution)/shard_map/ppermute | solution.py:400
  147.1 1.3 compare_select_fusion.3
  148.4 10.4 %shard_map.76 = (bf16[48,2048]{1,0:T(8,128)(2,1)S(1)}, bf16[48,2048]{1,0:T(8,128)(2,1)S(1)}, bf16[48,2048]{1,0:T(8,128)(2,1)S(1)}, bf16[48,2048]{1,0:T(8,128)(2,1)S(1)}) custom-call(s32[2]{0:T(128)S(1)} %pad_add_fusion.1.ids, bf16[192,144]{1,0:T(8,128)(2,1)S(1)} %bitcast.96, bf16[2,144,1024]{2,1,0:T(8,128)(2,1)S(1)} %collective-permute-done.22.mine, ...), custom_call_target="tpu_custom_call" | custom-call | bytes 40000000 | tf_op jit(solution)/shard_map/pallas_call | solution.py:287
  158.8 2.1 %collective-permute-start.24 = (bf16[48,2048]{1,0:T(8,128)(2,1)S(1)}, bf16[48,2048]{1,0:T(8,128)(2,1)S(1)}, u32[]{:S(2)}, u32[]{:S(2)}) collective-permute-start(bf16[48,2048]{1,0:T(8,128)(2,1)S(1)} %get-tuple-element.77), channel_id=1, source_target_pairs={{0,4},{4,8},{8,12},{12,0},{1,5},{5,9},{9,13},{13,1},{2,6},{6,10},{... | collective-permute-start | bytes 589832 | tf_op jit(solution)/shard_map/ppermute | solution.py:400
  161.1 2.2 %collective-permute-start.26 = (bf16[48,2048]{1,0:T(8,128)(2,1)S(1)}, bf16[48,2048]{1,0:T(8,128)(2,1)S(1)}, u32[]{:S(2)}, u32[]{:S(2)}) collective-permute-start(bf16[48,2048]{1,0:T(8,128)(2,1)S(1)} %get-tuple-element.79), channel_id=1, source_target_pairs={{0,12},{4,0},{8,4},{12,8},{1,13},{5,1},{9,5},{13,9},{2,14},{6,2},{... | collective-permute-start | bytes 589832 | tf_op jit(solution)/shard_map/ppermute | solution.py:400
  163.4 5.1 %collective-permute-done.24 = bf16[48,2048]{1,0:T(8,128)(2,1)S(1)} collective-permute-done((bf16[48,2048]{1,0:T(8,128)(2,1)S(1)}, bf16[48,2048]{1,0:T(8,128)(2,1)S(1)}, u32[]{:S(2)}, u32[]{:S(2)}) %collective-permute-start.24) | collective-permute-done | bytes 196640 | tf_op jit(solution)/shard_map/ppermute | solution.py:400
  168.5 8.8 %collective-permute-done.25 = bf16[48,2048]{1,0:T(8,128)(2,1)S(1)} collective-permute-done((bf16[48,2048]{1,0:T(8,128)(2,1)S(1)}, bf16[48,2048]{1,0:T(8,128)(2,1)S(1)}, u32[]{:S(2)}, u32[]{:S(2)}) %collective-permute-start.25) | collective-permute-done | bytes 196640 | tf_op jit(solution)/shard_map/ppermute | solution.py:400
  (68 shorter events, 14.3 us)
Async XLA Ops:
  0.0 22.5 %collective-permute-start.1 = (bf16[96,2048]{1,0:T(8,128)(2,1)}, bf16[96,2048]{1,0:T(8,128)(2,1)S(1)}, u32[]{:S(2)}, u32[]{:S(2)}) collective-permute-start(bf16[96,2048]{1,0:T(8,128)(2,1)} %param.9), channel_id=1, source_target_pairs={{0,0},{1,4},{2,8},{3,12},{4,1},{5,5},{6,9},{7,13},{8,2},{9,6},{10,... | collective-permute-start | bytes 1179656 | tf_op jit(solution)/shard_map/ppermute | solution.py:323
  1.6 20.9 %collective-permute-start.2 = (bf16[96,2048]{1,0:T(8,128)(2,1)}, bf16[96,2048]{1,0:T(8,128)(2,1)}, u32[]{:S(2)}, u32[]{:S(2)}) collective-permute-start(bf16[96,2048]{1,0:T(8,128)(2,1)} %param.9), channel_id=1, source_target_pairs={{0,4},{1,8},{2,12},{3,0},{4,5},{5,9},{6,13},{7,1},{8,6},{9,10},{10... | collective-permute-start | bytes 1179656 | tf_op jit(solution)/shard_map/ppermute | solution.py:323
  5.0 18.2 %collective-permute-start.3 = (bf16[96,2048]{1,0:T(8,128)(2,1)}, bf16[96,2048]{1,0:T(8,128)(2,1)}, u32[]{:S(2)}, u32[]{:S(2)}) collective-permute-start(bf16[96,2048]{1,0:T(8,128)(2,1)} %param.9), channel_id=1, source_target_pairs={{0,8},{1,12},{2,0},{3,4},{4,9},{5,13},{6,1},{7,5},{8,10},{9,14},{1... | collective-permute-start | bytes 1179656 | tf_op jit(solution)/shard_map/ppermute | solution.py:323
  11.0 20.0 %collective-permute-start.4 = (bf16[96,2048]{1,0:T(8,128)(2,1)}, bf16[96,2048]{1,0:T(8,128)(2,1)S(1)}, u32[]{:S(2)}, u32[]{:S(2)}) collective-permute-start(bf16[96,2048]{1,0:T(8,128)(2,1)} %param.9), channel_id=1, source_target_pairs={{0,12},{1,0},{2,4},{3,8},{4,13},{5,1},{6,5},{7,9},{8,14},{9,2},{10... | collective-permute-start | bytes 1179656 | tf_op jit(solution)/shard_map/ppermute | solution.py:323
  31.1 0.7 copy-start
  31.8 43.0 %collective-permute-start.5 = (bf16[96,2048]{1,0:T(8,128)(2,1)}, bf16[96,2048]{1,0:T(8,128)(2,1)S(1)}, u32[]{:S(2)}, u32[]{:S(2)}) collective-permute-start(bf16[96,2048]{1,0:T(8,128)(2,1)} %param.10), channel_id=1, source_target_pairs={{0,0},{1,4},{2,8},{3,12},{4,1},{5,5},{6,9},{7,13},{8,2},{9,6},{10,... | collective-permute-start | bytes 1179656 | tf_op jit(solution)/shard_map/ppermute | solution.py:323
  33.4 41.3 %collective-permute-start.6 = (bf16[96,2048]{1,0:T(8,128)(2,1)}, bf16[96,2048]{1,0:T(8,128)(2,1)S(1)}, u32[]{:S(2)}, u32[]{:S(2)}) collective-permute-start(bf16[96,2048]{1,0:T(8,128)(2,1)} %param.10), channel_id=1, source_target_pairs={{0,4},{1,8},{2,12},{3,0},{4,5},{5,9},{6,13},{7,1},{8,6},{9,10},{10... | collective-permute-start | bytes 1179656 | tf_op jit(solution)/shard_map/ppermute | solution.py:323
  44.9 29.8 %collective-permute-start.7 = (bf16[96,2048]{1,0:T(8,128)(2,1)}, bf16[96,2048]{1,0:T(8,128)(2,1)S(1)}, u32[]{:S(2)}, u32[]{:S(2)}) collective-permute-start(bf16[96,2048]{1,0:T(8,128)(2,1)} %param.10), channel_id=1, source_target_pairs={{0,8},{1,12},{2,0},{3,4},{4,9},{5,13},{6,1},{7,5},{8,10},{9,14},{1... | collective-permute-start | bytes 1179656 | tf_op jit(solution)/shard_map/ppermute | solution.py:323
  53.7 21.0 %collective-permute-start.8 = (bf16[96,2048]{1,0:T(8,128)(2,1)}, bf16[96,2048]{1,0:T(8,128)(2,1)S(1)}, u32[]{:S(2)}, u32[]{:S(2)}) collective-permute-start(bf16[96,2048]{1,0:T(8,128)(2,1)} %param.10), channel_id=1, source_target_pairs={{0,12},{1,0},{2,4},{3,8},{4,13},{5,1},{6,5},{7,9},{8,14},{9,2},{10... | collective-permute-start | bytes 1179656 | tf_op jit(solution)/shard_map/ppermute | solution.py:323
  70.0 2.9 %collective-permute-start = (bf16[2,288,1024]{2,1,0:T(8,128)(2,1)S(1)}, bf16[2,288,1024]{2,1,0:T(8,128)(2,1)S(1)}, u32[]{:S(2)}, u32[]{:S(2)}) collective-permute-start(bf16[2,288,1024]{2,1,0:T(8,128)(2,1)S(1)} %get-tuple-element.31), channel_id=1, source_target_pairs={{0,1},{1,0},{2,3},{3,2},{4,5},{5,4},{6,7},{7,6},{8,9},{9,8},{10,11... | collective-permute-start | bytes 3538952 | tf_op jit(solution)/shard_map/cond/branch_1_fun/ppermute | solution.py:364
  73.5 30.0 %collective-permute-start.12 = (bf16[2,288,1024]{2,1,0:T(8,128)(2,1)S(1)}, bf16[2,288,1024]{2,1,0:T(8,128)(2,1)S(1)}, u32[]{:S(2)}, u32[]{:S(2)}) collective-permute-start(bf16[2,288,1024]{2,1,0:T(8,128)(2,1)S(1)} %get-tuple-element.57), channel_id=1, source_target_pairs={{0,2},{1,3},{2,0},{3,1},{4,6},{5,7},{6,4},{7,5},{8,10},{9,11},{10,... | collective-permute-start | bytes 3538952 | tf_op jit(solution)/shard_map/ppermute | solution.py:372
  84.6 19.0 %collective-permute-start.11 = (bf16[2,288,1024]{2,1,0:T(8,128)(2,1)S(1)}, bf16[2,288,1024]{2,1,0:T(8,128)(2,1)S(1)}, u32[]{:S(2)}, u32[]{:S(2)}) collective-permute-start(bf16[2,288,1024]{2,1,0:T(8,128)(2,1)S(1)} %get-tuple-element.64), channel_id=1, source_target_pairs={{0,1},{1,0},{2,3},{3,2},{4,5},{5,4},{6,7},{7,6},{8,9},{9,8},{10,11... | collective-permute-start | bytes 3538952 | tf_op jit(solution)/shard_map/ppermute | solution.py:380
  84.6 3.7 %collective-permute-start.9 = (bf16[2,144,1024]{2,1,0:T(8,128)(2,1)S(1)}, bf16[2,144,1024]{2,1,0:T(8,128)(2,1)S(1)}, u32[]{:S(2)}, u32[]{:S(2)}) collective-permute-start(bf16[2,144,1024]{2,1,0:T(8,128)(2,1)S(1)} %get-tuple-element.61), channel_id=1, source_target_pairs={{0,1},{1,0},{2,3},{3,2},{4,5},{5,4},{6,7},{7,6},{8,9},{9,8},{10,11... | collective-permute-start | bytes 1769480 | tf_op jit(solution)/shard_map/ppermute | solution.py:377
  85.1 9.7 %collective-permute-start.15 = (bf16[2,144,1024]{2,1,0:T(8,128)(2,1)S(1)}, bf16[2,144,1024]{2,1,0:T(8,128)(2,1)S(1)}, u32[]{:S(2)}, u32[]{:S(2)}) collective-permute-start(bf16[2,144,1024]{2,1,0:T(8,128)(2,1)S(1)} %get-tuple-element.66), channel_id=1, source_target_pairs={{0,1},{1,0},{2,3},{3,2},{4,5},{5,4},{6,7},{7,6},{8,9},{9,8},{10,11... | collective-permute-start | bytes 1769480 | tf_op jit(solution)/shard_map/ppermute | solution.py:377
  88.4 21.5 %collective-permute-start.10 = (bf16[144,1024]{1,0:T(8,128)(2,1)S(1)}, bf16[144,1024]{1,0:T(8,128)(2,1)S(1)}, u32[]{:S(2)}, u32[]{:S(2)}) collective-permute-start(bf16[144,1024]{1,0:T(8,128)(2,1)S(1)} %fusion.13), channel_id=1, source_target_pairs={{0,2},{1,3},{2,0},{3,1},{4,6},{5,7},{6,4},{7,5},{8,10},{9,11},{10,... | collective-permute-start | bytes 884744 | tf_op jit(solution)/shard_map/ppermute | solution.py:385
  94.9 21.3 %collective-permute-start.16 = (bf16[144,1024]{1,0:T(8,128)(2,1)S(1)}, bf16[144,1024]{1,0:T(8,128)(2,1)S(1)}, u32[]{:S(2)}, u32[]{:S(2)}) collective-permute-start(bf16[144,1024]{1,0:T(8,128)(2,1)S(1)} %fusion.14), channel_id=1, source_target_pairs={{0,2},{1,3},{2,0},{3,1},{4,6},{5,7},{6,4},{7,5},{8,10},{9,11},{10,... | collective-permute-start | bytes 884744 | tf_op jit(solution)/shard_map/ppermute | solution.py:385
  110.3 9.2 %collective-permute-start.14 = (bf16[2,144,1024]{2,1,0:T(8,128)(2,1)S(1)}, bf16[2,144,1024]{2,1,0:T(8,128)(2,1)S(1)}, u32[]{:S(2)}, u32[]{:S(2)}) collective-permute-start(bf16[2,144,1024]{2,1,0:T(8,128)(2,1)S(1)} %pad_maximum_fusion.mine_a), channel_id=1, source_target_pairs={{0,1},{1,0},{2,3},{3,2},{4,5},{5,4},{6,7},{7,6},{8,9},{9,8},{10,11... | collective-permute-start | bytes 1769480 | tf_op jit(solution)/shard_map/ppermute | solution.py:390
  110.4 18.4 %collective-permute-start.13 = (bf16[2,144,1024]{2,1,0:T(8,128)(2,1)S(1)}, bf16[2,144,1024]{2,1,0:T(8,128)(2,1)S(1)}, u32[]{:S(2)}, u32[]{:S(2)}) collective-permute-start(bf16[2,144,1024]{2,1,0:T(8,128)(2,1)S(1)} %pad_maximum_fusion.mine_a), channel_id=1, source_target_pairs={{0,2},{1,3},{2,0},{3,1},{4,6},{5,7},{6,4},{7,5},{8,10},{9,11},{10,... | collective-permute-start | bytes 1769480 | tf_op jit(solution)/shard_map/ppermute | solution.py:391
  116.6 2.9 %collective-permute-start.17 = (bf16[2,144,1024]{2,1,0:T(8,128)(2,1)S(1)}, bf16[2,144,1024]{2,1,0:T(8,128)(2,1)S(1)}, u32[]{:S(2)}, u32[]{:S(2)}) collective-permute-start(bf16[2,144,1024]{2,1,0:T(8,128)(2,1)S(1)} %pad_maximum_fusion.1.mine_b), channel_id=1, source_target_pairs={{0,1},{1,0},{2,3},{3,2},{4,5},{5,4},{6,7},{7,6},{8,9},{9,8},{10,11... | collective-permute-start | bytes 1769480 | tf_op jit(solution)/shard_map/ppermute | solution.py:390
  117.0 24.2 %collective-permute-start.22 = (bf16[2,144,1024]{2,1,0:T(8,128)(2,1)S(1)}, bf16[2,144,1024]{2,1,0:T(8,128)(2,1)S(1)}, u32[]{:S(2)}, u32[]{:S(2)}) collective-permute-start(bf16[2,144,1024]{2,1,0:T(8,128)(2,1)S(1)} %pad_maximum_fusion.1.mine_b), channel_id=1, source_target_pairs={{0,2},{1,3},{2,0},{3,1},{4,6},{5,7},{6,4},{7,5},{8,10},{9,11},{10,... | collective-permute-start | bytes 1769480 | tf_op jit(solution)/shard_map/ppermute | solution.py:391
  128.8 2.0 %collective-permute-start.18 = (bf16[2,144,1024]{2,1,0:T(8,128)(2,1)S(1)}, bf16[2,144,1024]{2,1,0:T(8,128)(2,1)S(1)}, u32[]{:S(2)}, u32[]{:S(2)}) collective-permute-start(bf16[2,144,1024]{2,1,0:T(8,128)(2,1)S(1)} %collective-permute-done.13.mine), channel_id=1, source_target_pairs={{0,1},{1,0},{2,3},{3,2},{4,5},{5,4},{6,7},{7,6},{8,9},{9,8},{10,11... | collective-permute-start | bytes 1769480 | tf_op jit(solution)/shard_map/ppermute | solution.py:395
  141.2 7.2 %collective-permute-start.23 = (bf16[2,144,1024]{2,1,0:T(8,128)(2,1)S(1)}, bf16[2,144,1024]{2,1,0:T(8,128)(2,1)S(1)}, u32[]{:S(2)}, u32[]{:S(2)}) collective-permute-start(bf16[2,144,1024]{2,1,0:T(8,128)(2,1)S(1)} %collective-permute-done.22.mine), channel_id=1, source_target_pairs={{0,1},{1,0},{2,3},{3,2},{4,5},{5,4},{6,7},{7,6},{8,9},{9,8},{10,11... | collective-permute-start | bytes 1769480 | tf_op jit(solution)/shard_map/ppermute | solution.py:395
  142.2 18.9 %collective-permute-start.19 = (bf16[48,2048]{1,0:T(8,128)(2,1)S(1)}, bf16[48,2048]{1,0:T(8,128)(2,1)S(1)}, u32[]{:S(2)}, u32[]{:S(2)}) collective-permute-start(bf16[48,2048]{1,0:T(8,128)(2,1)S(1)} %get-tuple-element.71), channel_id=1, source_target_pairs={{0,4},{4,8},{8,12},{12,0},{1,5},{5,9},{9,13},{13,1},{2,6},{6,10},{... | collective-permute-start | bytes 589832 | tf_op jit(solution)/shard_map/ppermute | solution.py:400
  144.4 18.9 %collective-permute-start.20 = (bf16[48,2048]{1,0:T(8,128)(2,1)S(1)}, bf16[48,2048]{1,0:T(8,128)(2,1)S(1)}, u32[]{:S(2)}, u32[]{:S(2)}) collective-permute-start(bf16[48,2048]{1,0:T(8,128)(2,1)S(1)} %get-tuple-element.72), channel_id=1, source_target_pairs={{0,8},{4,12},{8,0},{12,4},{1,9},{5,13},{9,1},{13,5},{2,10},{6,14},... | collective-permute-start | bytes 589832 | tf_op jit(solution)/shard_map/ppermute | solution.py:400
  147.1 16.2 %collective-permute-start.21 = (bf16[48,2048]{1,0:T(8,128)(2,1)S(1)}, bf16[48,2048]{1,0:T(8,128)(2,1)S(1)}, u32[]{:S(2)}, u32[]{:S(2)}) collective-permute-start(bf16[48,2048]{1,0:T(8,128)(2,1)S(1)} %get-tuple-element.73), channel_id=1, source_target_pairs={{0,12},{4,0},{8,4},{12,8},{1,13},{5,1},{9,5},{13,9},{2,14},{6,2},{... | collective-permute-start | bytes 589832 | tf_op jit(solution)/shard_map/ppermute | solution.py:400
  158.8 9.7 %collective-permute-start.24 = (bf16[48,2048]{1,0:T(8,128)(2,1)S(1)}, bf16[48,2048]{1,0:T(8,128)(2,1)S(1)}, u32[]{:S(2)}, u32[]{:S(2)}) collective-permute-start(bf16[48,2048]{1,0:T(8,128)(2,1)S(1)} %get-tuple-element.77), channel_id=1, source_target_pairs={{0,4},{4,8},{8,12},{12,0},{1,5},{5,9},{9,13},{13,1},{2,6},{6,10},{... | collective-permute-start | bytes 589832 | tf_op jit(solution)/shard_map/ppermute | solution.py:400
  160.9 16.5 %collective-permute-start.25 = (bf16[48,2048]{1,0:T(8,128)(2,1)S(1)}, bf16[48,2048]{1,0:T(8,128)(2,1)S(1)}, u32[]{:S(2)}, u32[]{:S(2)}) collective-permute-start(bf16[48,2048]{1,0:T(8,128)(2,1)S(1)} %get-tuple-element.78), channel_id=1, source_target_pairs={{0,8},{4,12},{8,0},{12,4},{1,9},{5,13},{9,1},{13,5},{2,10},{6,14},... | collective-permute-start | bytes 589832 | tf_op jit(solution)/shard_map/ppermute | solution.py:400
  161.1 16.3 %collective-permute-start.26 = (bf16[48,2048]{1,0:T(8,128)(2,1)S(1)}, bf16[48,2048]{1,0:T(8,128)(2,1)S(1)}, u32[]{:S(2)}, u32[]{:S(2)}) collective-permute-start(bf16[48,2048]{1,0:T(8,128)(2,1)S(1)} %get-tuple-element.79), channel_id=1, source_target_pairs={{0,12},{4,0},{8,4},{12,8},{1,13},{5,1},{9,5},{13,9},{2,14},{6,2},{... | collective-permute-start | bytes 589832 | tf_op jit(solution)/shard_map/ppermute | solution.py:400

commit v4 on v3

--- a/solution.py
+++ b/solution.py
@@ -9,7 +9,7 @@
 BF, F32 = jnp.bfloat16, jnp.float32
 ROW_CONTRACT = (((1,), (1,)), ((), ()))
 VMEM = 49 * 1024 * 1024
-GATE_UP_COST, HIDDEN_COST, NEAR_COST, FAR_COST = 40000000, 60000000, 40000000, 40000000
+PROJECT_COST, HIDDEN_COST, NEAR_COST, FAR_COST = 20000000, 60000000, 40000000, 40000000
 
 
 def derive(gate, up, hidden_grad):
@@ -115,81 +115,102 @@
     rows_v[...] = jnp.dot(select_ref[...], arrived[...], preferred_element_type=F32).astype(BF)
 
 
-def gate_up_kernel(ids, select_ref, p0, p1, p2, p3, gate_w, up_w, send_far, keep_far, send_near, keep_near,
-                   gate_v, up_v, out_v, rows_v, arrived, sems):
+def project_kernel(near, ids, *refs):
+    if near:
+        rows_in, gate_w, up_w, send, keep, gate_v, up_v, out_v, rows_v, sems = refs
+        moves = [start(rows_in, rows_v, sems.at[0, 0])]
+    else:
+        select_ref, p0, p1, p2, p3, gate_w, up_w, send, keep, rows_out, gate_v, up_v, out_v, rows_v, arrived, sems = refs
+        moves = pick_start((p0, p1, p2, p3), arrived, sems.at[0])
     core, x = ids[0], ids[1]
     block = gate_v.shape[2]
-    moves = pick_start((p0, p1, p2, p3), arrived, sems.at[0])
     loads = []
-    for slot in range(4):
-        index = slot_index(slot, core, x)
+    for i in range(2):
+        index = slot_index(2 * near + i, core, x)
         for a, (weight, held) in enumerate(((gate_w, gate_v), (up_w, up_v))):
-            loads.append([pltpu.make_async_copy(region(weight, 1, index, block), held.at[slot], sems.at[1 + a, slot])])
-    loads = Stream(loads, 3)
-    pick_end(moves, select_ref, arrived, rows_v)
+            loads.append([pltpu.make_async_copy(region(weight, 1, index, block), held.at[i], sems.at[1 + a, i])])
+    loads = Stream(loads, 2)
     stores = []
-    for slot, out in enumerate((send_far, keep_far, send_near, keep_near)):
+    if near:
+        moves[0].wait()
+    else:
+        pick_end(moves, select_ref, arrived, rows_v)
+        stores.append(start(rows_v, rows_out, sems.at[0, 0]))
+    for i, out in enumerate((send, keep)):
         for a, held in enumerate((gate_v, up_v)):
-            loads.wait(2 * slot + a)
-            out_v[slot, a] = jnp.dot(rows_v[...], held[slot], preferred_element_type=F32).astype(BF)
-            stores.append(start(out_v.at[slot, a], out.at[a], sems.at[3 + a, slot]))
+            loads.wait(2 * i + a)
+            out_v[i, a] = jnp.dot(rows_v[...], held[i], preferred_element_type=F32).astype(BF)
+            stores.append(start(out_v.at[i, a], out.at[a], sems.at[3 + a, i]))
     for store in stores:
         store.wait()
 
 
-def gate_up(ids, select, parts, gate_weight, up_weight):
+def project(near, ids, rows, gate_weight, up_weight):
     depth, block = gate_weight.shape[0], gate_weight.shape[1] // 4
-    count = select.shape[0]
+    count = rows.shape[0] if near else rows[0].shape[0]
+    args = (rows,) if near else rows
+    picked = [] if near else [((count, depth), BF)]
+    arrived = [] if near else [pltpu.VMEM((rows[0].shape[1], depth), BF)]
     return call(
-        gate_up_kernel,
-        [IN_SMEM, IN_VMEM] + [IN_HBM] * 6,
-        [((2, count, block), BF)] * 4,
-        [pltpu.VMEM((4, depth, block), BF)] * 2 + [
-            pltpu.VMEM((4, 2, count, block), BF),
+        functools.partial(project_kernel, near),
+        [IN_SMEM] + [IN_HBM if near else IN_VMEM] + [IN_HBM] * (len(args) + 1),
+        [((2, count, block), BF)] * 2 + picked,
+        [pltpu.VMEM((2, depth, block), BF)] * 2 + [
+            pltpu.VMEM((2, 2, count, block), BF),
             pltpu.VMEM((count, depth), BF),
-            pltpu.VMEM((select.shape[1], depth), BF),
-            pltpu.SemaphoreType.DMA((5, 4)),
-        ],
-        GATE_UP_COST,
-    )(ids, select, *parts, gate_weight, up_weight)
-
-
-def hidden_kernel(ids, select_ref, p0, p1, p2, p3, down, send_a, send_b, keep_a, keep_b,
-                  down_v, out_v, rows_v, arrived, sems):
+        ] + arrived + [pltpu.SemaphoreType.DMA((5, 4))],
+        PROJECT_COST,
+    )(ids, *args, gate_weight, up_weight)
+
+
+def hidden_kernel(near, ids, *refs):
+    if near:
+        rows_in, down, send, keep, down_v, out_v, rows_v, sems = refs
+        moves = [start(rows_in, rows_v, sems.at[0, 0])]
+        outs = ((send,), (keep,))
+    else:
+        select_ref, p0, p1, p2, p3, down, *sides, rows_out, down_v, out_v, rows_v, arrived, sems = refs
+        moves = pick_start((p0, p1, p2, p3), arrived, sems.at[0])
+        outs = (sides[:2], sides[2:])
     core, x = ids[0], ids[1]
-    rows, block = send_a.shape[1], send_a.shape[2]
-    moves = pick_start((p0, p1, p2, p3), arrived, sems.at[0])
+    block = down_v.shape[1]
     loads = Stream(
-        [[pltpu.make_async_copy(region(down, 0, slot_index(slot, core, x), block), down_v.at[slot], sems.at[1, slot])]
-         for slot in range(4)], 3)
-    pick_end(moves, select_ref, arrived, rows_v)
+        [[pltpu.make_async_copy(region(down, 0, slot_index(2 * near + i, core, x), block), down_v.at[i], sems.at[1, i])]
+         for i in range(2)], 2)
     stores = []
-    for slot in range(4):
-        loads.wait(slot)
-        hidden = lax.dot_general(rows_v[...], down_v[slot], ROW_CONTRACT, preferred_element_type=F32)
-        out_v[slot] = hidden.astype(BF)
-        for m, out in enumerate((send_a, send_b) if slot % 2 == 0 else (keep_a, keep_b)):
-            stores.append(start(out_v.at[slot, pl.ds(m * rows, rows)], out.at[slot // 2], sems.at[2 + m, slot]))
+    if near:
+        moves[0].wait()
+    else:
+        pick_end(moves, select_ref, arrived, rows_v)
+        stores.append(start(rows_v, rows_out, sems.at[0, 0]))
+    for i in range(2):
+        loads.wait(i)
+        hidden = lax.dot_general(rows_v[...], down_v[i], ROW_CONTRACT, preferred_element_type=F32)
+        out_v[i] = hidden.astype(BF)
+        for m, out in enumerate(outs[i]):
+            rows = out.shape[0]
+            stores.append(start(out_v.at[i, pl.ds(m * rows, rows)], out, sems.at[2 + m, i]))
     for store in stores:
         store.wait()
 
 
-def hidden_grads(ids, select, parts, down_weight):
+def hidden_grads(near, ids, rows, down_weight):
     depth, block = down_weight.shape[1], down_weight.shape[0] // 4
-    count = select.shape[0]
+    count = rows.shape[0] if near else rows[0].shape[0]
+    args = (rows,) if near else rows
+    outs = [((count, block), BF)] * 2 if near else [((count // 2, block), BF)] * 4 + [((count, depth), BF)]
+    arrived = [] if near else [pltpu.VMEM((rows[0].shape[1], depth), BF)]
     return call(
-        hidden_kernel,
-        [IN_SMEM, IN_VMEM] + [IN_HBM] * 5,
-        [((2, count // 2, block), BF)] * 4,
+        functools.partial(hidden_kernel, near),
+        [IN_SMEM] + [IN_HBM if near else IN_VMEM] + [IN_HBM] * len(args),
+        outs,
         [
-            pltpu.VMEM((4, block, depth), BF),
-            pltpu.VMEM((4, count, block), BF),
+            pltpu.VMEM((2, block, depth), BF),
+            pltpu.VMEM((2, count, block), BF),
             pltpu.VMEM((count, depth), BF),
-            pltpu.VMEM((select.shape[1], depth), BF),
-            pltpu.SemaphoreType.DMA((4, 4)),
-        ],
+        ] + arrived + [pltpu.SemaphoreType.DMA((4, 4))],
         HIDDEN_COST,
-    )(ids, select, *parts, down_weight)
+    )(ids, *args, down_weight)
 
 
 CHUNKS = 4
@@ -262,7 +283,7 @@
         store.wait()
 
 
-def near(ids, mine, other, gate_weight, up_weight):
+def near_back(ids, mine, other, gate_weight, up_weight):
     sets, rows, block, depth = len(mine), mine[0].shape[1], mine[0].shape[2], gate_weight.shape[0]
     count = sets * rows
     return call(
@@ -281,7 +302,7 @@
     )(ids, mine[0], other[0], mine[1], other[1], gate_weight, up_weight)
 
 
-def far(ids, place, mine, other, gate_weight, up_weight, first):
+def far_back(ids, place, mine, other, gate_weight, up_weight, first):
     rows, block, depth = mine.shape[1], mine.shape[2], gate_weight.shape[0]
     count = place.shape[0]
     return call(
@@ -310,7 +331,7 @@
     shard_rows, depth = tokens.shape
     rows = packing.shape[0]
     live_rows = rows * 3 // 4
-    sets = 2
+    sets, block = 2, gate_weight.shape[1] // 4
     set_rows, piece = live_rows // sets, shard_rows // sets
     t, s = lax.axis_index("tensor"), lax.axis_index("seq")
     core, x = s % 2, s // 2
@@ -359,41 +380,48 @@
     held = after(grad_out, select, present, *token_parts)
     grad_parts = [spread(held, k) for k in range(n)]
 
-    def project(ids, select, gate_weight, up_weight, *token_parts):
-        send_far, keep_far, send_near, keep_near = gate_up(ids, select, token_parts, gate_weight, up_weight)
-        got_far = lax.ppermute(send_far, "seq", sibling)
-        return (keep_far.astype(F32) + got_far.astype(F32)).astype(BF), send_near, keep_near
+    def far_side(ids, select, gate_weight, up_weight, *token_parts):
+        send, keep, picked = project(False, ids, (select, *token_parts), gate_weight, up_weight)
+        got = lax.ppermute(send, "seq", sibling)
+        return (keep.astype(F32) + got.astype(F32)).astype(BF), picked
 
     def absent(*_):
-        nothing = jnp.zeros((2, live_rows, gate_weight.shape[1] // 4), BF)
-        return nothing, nothing, nothing
-
-    pair_far, send_near, keep_near = lax.cond(present, project, absent, ids, select, gate_weight, up_weight, *token_parts)
+        return jnp.zeros((2, live_rows, block), BF), jnp.zeros((live_rows, depth), BF)
+
+    pair_far, picked = lax.cond(present, far_side, absent, ids, select, gate_weight, up_weight, *token_parts)
     across_near = lax.ppermute(pair_far, "seq", across)
 
-    outs = hidden_grads(ids, after(select, pair_far), grad_parts, down_weight)
+    send, keep = project(True, ids, picked, gate_weight, up_weight)
+    *outs, picked = hidden_grads(False, ids, (after(select, send), *grad_parts), down_weight)
+    near = keep.astype(F32) + lax.ppermute(after(send, outs[0]), "seq", sibling).astype(F32) + across_near.astype(F32)
     pairs = []
     for m in range(sets):
         got = lax.ppermute(outs[m], "seq", sibling)
-        keep = outs[sets + m]
-        pairs.append(((keep[0].astype(F32) + got[0].astype(F32)).astype(BF), keep[1].astype(F32) + got[1].astype(F32)))
-    got_near = lax.ppermute(after(send_near, outs[0]), "seq", sibling)
-    gate_near = keep_near.astype(F32) + got_near.astype(F32) + across_near.astype(F32)
+        keep = after(outs[sets + m], pairs[0]) if m else outs[sets]
+        pairs.append((keep.astype(F32) + got.astype(F32)).astype(BF))
+    def near_side(ids, picked, down_weight):
+        send, keep = hidden_grads(True, ids, picked, down_weight)
+        return keep, lax.ppermute(send, "seq", sibling)
+
+    def no_near(*_):
+        return (jnp.zeros((live_rows, block), BF),) * 2
+
+    keep, got = lax.cond(present, near_side, no_near, after(ids, pairs[-1]), picked, down_weight)
+    hidden = keep.astype(F32) + got.astype(F32)
     ds, ds_core, ds_far = [], [], []
     for m in range(sets):
-        pair_far, pair_near = pairs[m]
-        got = lax.ppermute(pair_far, "seq", across)
+        got = lax.ppermute(pairs[m], "seq", across)
         if m > 0:
             got = after(got, ds[m - 1])
         part = slice(m * set_rows, (m + 1) * set_rows)
-        ds.append(jnp.stack(derive(gate_near[0, part], gate_near[1, part], pair_near + got.astype(F32))))
+        ds.append(jnp.stack(derive(near[0, part], near[1, part], hidden[part] + got.astype(F32))))
         ds_core.append(lax.ppermute(ds[m], "seq", sibling))
         ds_far.append(lax.ppermute(ds[m], "seq", across))
-    firsts = near(ids, ds, ds_core, gate_weight, up_weight)
+    firsts = near_back(ids, ds, ds_core, gate_weight, up_weight)
     pieces, parts = [], firsts
     for m in range(sets):
         d_both = lax.ppermute(after(ds_far[m], parts[0]), "seq", sibling)
-        parts = far(ids, place[m].reshape(n * piece, set_rows), ds_far[m], d_both, gate_weight, up_weight, firsts[m])
+        parts = far_back(ids, place[m].reshape(n * piece, set_rows), ds_far[m], d_both, gate_weight, up_weight, firsts[m])
         total = parts[0].astype(F32)
         for k in range(1, n):
             shift = [(i, (i + k) % n) for i in range(n)]

time: 181 us -> 180 us (level)
  waiting for transfers between devices: 46.5 us -> 39.7 us
  Pallas kernels: 55.3 us -> 61.4 us
  other arithmetic: 6.33 us -> 10.1 us
    ppermute x1, waiting for transfers between devices: 7.89 us -> 0.01 us  [tuned(): across_near = lax.ppermute(pair_far, 'seq', across)]
    pallas_call x5 -> x7, Pallas kernels: 55.3 us -> 61.4 us  [the longest x2 20.8 us: far_back(): call(far_kernel, [IN_SMEM, IN_VMEM] + [IN_HBM] * 5, [((count // 4, depth)...]
    ppermute x6, waiting for transfers between devices: 13.9 us -> 16.8 us  [tuned(): total += lax.ppermute(parts[k], 'tensor', shift).astype(F32)]
    ppermute x4 -> x5, starting transfers between devices: 7.35 us -> 5.16 us  [the longest x2 4.86 us: tuned(): got = lax.ppermute(pairs[m], 'seq', across)]
    add x1 -> x2, other arithmetic: 0.55 us -> 2.48 us  [the longest x1 2.31 us: tuned(): keep.astype(F32)]
    ppermute x4 -> x5, waiting for transfers between devices: 11.5 us -> 9.93 us  [the longest x2 5.31 us: tuned(): got = lax.ppermute(pairs[m], 'seq', across)]
  transfers between devices with their start and end apart: 27 -> 28, of which waited for: 11 -> 12; matrix products, arithmetic and copies ran while one was open for 6% -> 8% of each run, Pallas kernels for 31% -> 34%
where the time goes in v4:
time: 180 us; the launch traced here: 179 us
  Pallas kernels  61.4 us (34%)
  starting transfers between devices  56 us (31%)
  waiting for transfers between devices  39.7 us (22%)
  other arithmetic  10.1 us (6%)
  blocking collectives  5.96 us (3%)
  local copies, waits for them, and re-layouts  2.61 us (1%)
  matrix products  2.17 us (1%)
    ppermute x8, starting transfers between devices, spread(): return lax.ppermute(value, ('tensor', 'seq'), pairs)  33.4 us
    pallas_call x2, Pallas kernels, far_back(): call(far_kernel, [IN_SMEM, IN_VMEM] + [IN_HBM] * 5, [((count // 4, depth)...  20.8 us
    pallas_call x2, Pallas kernels, project(): call(functools.partial(project_kernel, near), [IN_SMEM] + [IN_HBM if near...  18.8 us
    ppermute x6, waiting for transfers between devices, tuned(): total += lax.ppermute(parts[k], 'tensor', shift).astype(F32)  16.8 us
    pallas_call x2, Pallas kernels, hidden_grads(): call(functools.partial(hidden_kernel, near), [IN_SMEM] + [IN_HBM if near...  12.9 us
    ppermute x6, starting transfers between devices, tuned(): total += lax.ppermute(parts[k], 'tensor', shift).astype(F32)  10.1 us
    pallas_call x1, Pallas kernels, near_back(): call(near_kernel, [IN_SMEM] + [IN_HBM] * 6, [((rows, depth), F32)] * 2, [...  8.99 us
    ppermute x8, waiting for transfers between devices, spread(): return lax.ppermute(value, ('tensor', 'seq'), pairs)  8.6 us
  transfers between devices with their start and end apart: 28, of which 12 were waited for; matrix products, arithmetic and copies ran while one was open for 8% of the time, Pallas kernels for 34%

profile of v4, /device:TPU:0, one launch (start us, length us, event | category | flops | bytes accessed | tf_op | source)
XLA Modules:
  0.0 179.2 jit_solution(5973376528513680185)
XLA Ops:
  0.0 1.6 collective-permute-start.2
  1.6 3.4 %collective-permute-start.3 = (bf16[96,2048]{1,0:T(8,128)(2,1)}, bf16[96,2048]{1,0:T(8,128)(2,1)S(1)}, u32[]{:S(2)}, u32[]{:S(2)}) collective-permute-start(bf16[96,2048]{1,0:T(8,128)(2,1)} %param.11), channel_id=1, source_target_pairs={{0,4},{1,8},{2,12},{3,0},{4,5},{5,9},{6,13},{7,1},{8,6},{9,10},{10... | collective-permute-start | bytes 1179656 | tf_op jit(solution)/shard_map/ppermute | solution.py:344
  5.0 3.4 %collective-permute-start.4 = (bf16[96,2048]{1,0:T(8,128)(2,1)}, bf16[96,2048]{1,0:T(8,128)(2,1)S(1)}, u32[]{:S(2)}, u32[]{:S(2)}) collective-permute-start(bf16[96,2048]{1,0:T(8,128)(2,1)} %param.11), channel_id=1, source_target_pairs={{0,8},{1,12},{2,0},{3,4},{4,9},{5,13},{6,1},{7,5},{8,10},{9,14},{1... | collective-permute-start | bytes 1179656 | tf_op jit(solution)/shard_map/ppermute | solution.py:344
  11.0 2.6 %collective-permute-start.5 = (bf16[96,2048]{1,0:T(8,128)(2,1)}, bf16[96,2048]{1,0:T(8,128)(2,1)S(1)}, u32[]{:S(2)}, u32[]{:S(2)}) collective-permute-start(bf16[96,2048]{1,0:T(8,128)(2,1)} %param.11), channel_id=1, source_target_pairs={{0,12},{1,0},{2,4},{3,8},{4,13},{5,1},{6,5},{7,9},{8,14},{9,2},{10... | collective-permute-start | bytes 1179656 | tf_op jit(solution)/shard_map/ppermute | solution.py:344
  13.7 6.0 %all-reduce = s32[4]{0:T(128)S(1)} all-reduce(s32[4]{0:T(128)S(1)} %dynamic-update-slice), channel_id=1, replica_groups=mesh['group'=2,'tensor'=4,'seq'=4] {'seq'}, use_global_device_ids=true, to_apply=%add | all-reduce | flops 4 | bytes 32
  23.2 7.8 %collective-permute-done.5 = bf16[96,2048]{1,0:T(8,128)(2,1)S(1)} collective-permute-done((bf16[96,2048]{1,0:T(8,128)(2,1)}, bf16[96,2048]{1,0:T(8,128)(2,1)S(1)}, u32[]{:S(2)}, u32[]{:S(2)}) %collective-permute-start.5) | collective-permute-done | bytes 393248 | tf_op jit(solution)/shard_map/ppermute | solution.py:344
  31.1 1.6 collective-permute-start.6
  32.7 11.5 %collective-permute-start.7 = (bf16[96,2048]{1,0:T(8,128)(2,1)}, bf16[96,2048]{1,0:T(8,128)(2,1)S(1)}, u32[]{:S(2)}, u32[]{:S(2)}) collective-permute-start(bf16[96,2048]{1,0:T(8,128)(2,1)} %param.12), channel_id=1, source_target_pairs={{0,4},{1,8},{2,12},{3,0},{4,5},{5,9},{6,13},{7,1},{8,6},{9,10},{10... | collective-permute-start | bytes 1179656 | tf_op jit(solution)/shard_map/ppermute | solution.py:344
  44.2 8.8 %collective-permute-start.8 = (bf16[96,2048]{1,0:T(8,128)(2,1)}, bf16[96,2048]{1,0:T(8,128)(2,1)S(1)}, u32[]{:S(2)}, u32[]{:S(2)}) collective-permute-start(bf16[96,2048]{1,0:T(8,128)(2,1)} %param.12), channel_id=1, source_target_pairs={{0,8},{1,12},{2,0},{3,4},{4,9},{5,13},{6,1},{7,5},{8,10},{9,14},{1... | collective-permute-start | bytes 1179656 | tf_op jit(solution)/shard_map/ppermute | solution.py:344
  53.6 14.1 %conditional.2 = (bf16[2,288,1024]{2,1,0:T(8,128)(2,1)}, bf16[288,2048]{1,0:T(8,128)(2,1)S(1)}) conditional(s32[]{:T(128)} %convert_element_type.119, () %tuple.34, (s32[2]{0:T(128)S(1)}, bf16[288,384]{1,0:T(8,128)(2,1)S(1)}, bf16[96,2048]{1,0:T(8,128)(2,1)S(1)}, bf16[96,2048]{1,0:T(8,128)(2,1)S(1)}, bf16[96,2048]{1,0:T(8,128)(2,1)S(1)}, ...), branch_computations={%region_5.6_spmd, %region_6.7_spmd} | conditional | flops 2359296 | bytes 28257592 | solution.py:391
  53.6 9.7 %branch_1_fun.2 = (bf16[2,288,1024]{2,1,0:T(8,128)(2,1)S(1)}, bf16[2,288,1024]{2,1,0:T(8,128)(2,1)S(1)}, bf16[288,2048]{1,0:T(8,128)(2,1)S(1)}) custom-call(s32[2]{0:T(128)S(1)} %get-tuple-element.29.ids, bf16[288,384]{1,0:T(8,128)(2,1)S(1)} %get-tuple-element.30.refs_0_, bf16[96,2048]{1,0:T(8,128)(2,1)S(1)} %get-tuple-element.31.refs_1_, ...), custom_call_target="tpu_custom_call" | custom-call | bytes 20000000 | tf_op jit(solution)/shard_map/cond/branch_1_fun/pallas_call | solution.py:154
  63.4 2.8 %collective-permute-done.1 = bf16[2,288,1024]{2,1,0:T(8,128)(2,1)S(1)} collective-permute-done((bf16[2,288,1024]{2,1,0:T(8,128)(2,1)S(1)}, bf16[2,288,1024]{2,1,0:T(8,128)(2,1)S(1)}, u32[]{:S(2)}, u32[]{:S(2)}) %collective-permute-start.1) | collective-permute-done | bytes 1179680 | tf_op jit(solution)/shard_map/cond/branch_1_fun/ppermute | solution.py:385
  69.0 9.1 %shard_map.73 = (bf16[2,288,1024]{2,1,0:T(8,128)(2,1)}, bf16[2,288,1024]{2,1,0:T(8,128)(2,1)S(1)}) custom-call(s32[2]{0:T(128)S(1)} %pad_add_fusion.1.ids, bf16[288,2048]{1,0:T(8,128)(2,1)S(1)} %get-tuple-element.74.refs_0_, bf16[2048,4096]{1,0:T(8,128)(2,1)} %gate_w.5, bf16[2048,4096]{1,0:T(8,128)(2,1)} %up_w.5), custom_call_target="tpu_custom_call" | custom-call | bytes 20000000 | tf_op jit(solution)/shard_map/pallas_call | solution.py:154
  78.1 6.7 %shard_map.74 = (bf16[144,1024]{1,0:T(8,128)(2,1)S(1)}, bf16[144,1024]{1,0:T(8,128)(2,1)S(1)}, bf16[144,1024]{1,0:T(8,128)(2,1)S(1)}, bf16[144,1024]{1,0:T(8,128)(2,1)S(1)}, bf16[288,2048]{1,0:T(8,128)(2,1)S(1)}) custom-call(s32[2]{0:T(128)S(1)} %pad_add_fusion.1.ids, bf16[288,384]{1,0:T(8,128)(2,1)S(1)} %convolution_convert_fusion.1.refs_0_, ...), custom_call_target="tpu_custom_call" | custom-call | bytes 60000000 | tf_op jit(solution)/shard_map/pallas_call | solution.py:203
  85.7 2.1 %collective-permute-done.10 = bf16[144,1024]{1,0:T(8,128)(2,1)S(1)} collective-permute-done((bf16[144,1024]{1,0:T(8,128)(2,1)S(1)}, bf16[144,1024]{1,0:T(8,128)(2,1)S(1)}, u32[]{:S(2)}, u32[]{:S(2)}) %collective-permute-start.10) | collective-permute-done | bytes 294944 | tf_op jit(solution)/shard_map/ppermute | solution.py:399
  87.9 4.2 %collective-permute-start.12 = (bf16[144,1024]{1,0:T(8,128)(2,1)S(1)}, bf16[144,1024]{1,0:T(8,128)(2,1)}, u32[]{:S(2)}, u32[]{:S(2)}) collective-permute-start(bf16[144,1024]{1,0:T(8,128)(2,1)S(1)} %add_convert_fusion.2), channel_id=1, source_target_pairs={{0,2},{1,3},{2,0},{3,1},{4,6},{5,7},{6,4},{7,5},{8,10},{9,11},{10,... | collective-permute-start | bytes 884744 | tf_op jit(solution)/shard_map/ppermute | solution.py:413
  92.8 8.6 %conditional.3 = (f32[288,1024]{1,0:T(8,128)S(1)}, f32[288,1024]{1,0:T(8,128)S(1)}) conditional(s32[]{:T(128)} %convert_element_type.119, () %tuple.33, (s32[2]{0:T(128)S(1)}, bf16[288,2048]{1,0:T(8,128)(2,1)S(1)}, bf16[4096,2048]{1,0:T(8,128)(2,1)}) %tuple.40), branch_computations={%region_7.8_spmd, %region_8.9_spmd} | conditional | flops 589824 | bytes 65898296 | solution.py:409
  92.8 6.2 %branch_1_fun.3 = (bf16[288,1024]{1,0:T(8,128)(2,1)S(1)}, bf16[288,1024]{1,0:T(8,128)(2,1)S(1)}) custom-call(s32[2]{0:T(128)S(1)} %get-tuple-element.40.ids, bf16[288,2048]{1,0:T(8,128)(2,1)S(1)} %get-tuple-element.41.refs_0_, bf16[4096,2048]{1,0:T(8,128)(2,1)} %get-tuple-element.42.refs_1_), custom_call_target="tpu_custom_call" | custom-call | bytes 60000000 | tf_op jit(solution)/shard_map/cond/branch_1_fun/pallas_call | solution.py:203
  99.2 1.9 %collective-permute-done = bf16[288,1024]{1,0:T(8,128)(2,1)S(1)} collective-permute-done((bf16[288,1024]{1,0:T(8,128)(2,1)S(1)}, bf16[288,1024]{1,0:T(8,128)(2,1)S(1)}, u32[]{:S(2)}, u32[]{:S(2)}) %collective-permute-start) | collective-permute-done | bytes 589856 | tf_op jit(solution)/shard_map/cond/branch_1_fun/ppermute | solution.py:404
  101.6 2.3 %convert_add_fusion = f32[2,288,1024]{2,1,0:T(8,128)S(1)} fusion(bf16[2,288,1024]{2,1,0:T(8,128)(2,1)} %collective-permute-done.14, bf16[2,288,1024]{2,1,0:T(8,128)(2,1)} %collective-permute-done.13, bf16[2,288,1024]{2,1,0:T(8,128)(2,1)S(1)} %get-tuple-element.87), kind=kLoop, calls=%fused_computation.1 | loop fusion | flops 2949120 | bytes 5898240 | tf_op jit(solution)/shard_map/add | solution.py:396
  103.9 3.0 %collective-permute-done.12 = bf16[144,1024]{1,0:T(8,128)(2,1)} collective-permute-done((bf16[144,1024]{1,0:T(8,128)(2,1)S(1)}, bf16[144,1024]{1,0:T(8,128)(2,1)}, u32[]{:S(2)}, u32[]{:S(2)}) %collective-permute-start.12) | collective-permute-done | bytes 294944 | tf_op jit(solution)/shard_map/ppermute | solution.py:413
  108.3 2.7 %collective-permute-start.15 = (bf16[2,144,1024]{2,1,0:T(8,128)(2,1)S(1)}, bf16[2,144,1024]{2,1,0:T(8,128)(2,1)S(1)}, u32[]{:S(2)}, u32[]{:S(2)}) collective-permute-start(bf16[2,144,1024]{2,1,0:T(8,128)(2,1)S(1)} %pad_maximum_fusion.mine_a), channel_id=1, source_target_pairs={{0,2},{1,3},{2,0},{3,1},{4,6},{5,7},{6,4},{7,5},{8,10},{9,11},{10,... | collective-permute-start | bytes 1769480 | tf_op jit(solution)/shard_map/ppermute | solution.py:419
  110.9 2.3 %collective-permute-done.17 = bf16[144,1024]{1,0:T(8,128)(2,1)S(1)} collective-permute-done((bf16[144,1024]{1,0:T(8,128)(2,1)S(1)}, bf16[144,1024]{1,0:T(8,128)(2,1)S(1)}, u32[]{:S(2)}, u32[]{:S(2)}) %collective-permute-start.17) | collective-permute-done | bytes 294944 | tf_op jit(solution)/shard_map/ppermute | solution.py:413
  114.0 2.5 %collective-permute-start.23 = (bf16[2,144,1024]{2,1,0:T(8,128)(2,1)S(1)}, bf16[2,144,1024]{2,1,0:T(8,128)(2,1)S(1)}, u32[]{:S(2)}, u32[]{:S(2)}) collective-permute-start(bf16[2,144,1024]{2,1,0:T(8,128)(2,1)S(1)} %pad_maximum_fusion.1.mine_b), channel_id=1, source_target_pairs={{0,2},{1,3},{2,0},{3,1},{4,6},{5,7},{6,4},{7,5},{8,10},{9,11},{10,... | collective-permute-start | bytes 1769480 | tf_op jit(solution)/shard_map/ppermute | solution.py:419
  116.5 9.0 %shard_map.75 = (f32[144,2048]{1,0:T(8,128)S(1)}, f32[144,2048]{1,0:T(8,128)S(1)}) custom-call(s32[2]{0:T(128)S(1)} %pad_add_fusion.1.ids, bf16[2,144,1024]{2,1,0:T(8,128)(2,1)S(1)} %pad_maximum_fusion.mine_a, bf16[2,144,1024]{2,1,0:T(8,128)(2,1)S(1)} %collective-permute-done.16.other_a, bf16[2,144,1024]{2,1,0:T(8,128)(2,1)S(1)} %pad_maximum_fusion.1.mine_b, ...), custom_call_target="tpu_custom_call" | custom-call | bytes 40000000 | tf_op jit(solution)/shard_map/pallas_call | solution.py:289
  126.1 1.8 collective-permute-done.19.other
  127.9 10.4 %shard_map.76 = (bf16[48,2048]{1,0:T(8,128)(2,1)S(1)}, bf16[48,2048]{1,0:T(8,128)(2,1)S(1)}, bf16[48,2048]{1,0:T(8,128)(2,1)S(1)}, bf16[48,2048]{1,0:T(8,128)(2,1)S(1)}) custom-call(s32[2]{0:T(128)S(1)} %pad_add_fusion.1.ids, bf16[192,144]{1,0:T(8,128)(2,1)S(1)} %bitcast.73, bf16[2,144,1024]{2,1,0:T(8,128)(2,1)S(1)} %collective-permute-done.15.mine, ...), custom_call_target="tpu_custom_call" | custom-call | bytes 40000000 | tf_op jit(solution)/shard_map/pallas_call | solution.py:308
  139.3 5.1 %collective-permute-start.22 = (bf16[48,2048]{1,0:T(8,128)(2,1)S(1)}, bf16[48,2048]{1,0:T(8,128)(2,1)S(1)}, u32[]{:S(2)}, u32[]{:S(2)}) collective-permute-start(bf16[48,2048]{1,0:T(8,128)(2,1)S(1)} %get-tuple-element.96), channel_id=1, source_target_pairs={{0,12},{4,0},{8,4},{12,8},{1,13},{5,1},{9,5},{13,9},{2,14},{6,2},{... | collective-permute-start | bytes 589832 | tf_op jit(solution)/shard_map/ppermute | solution.py:428
  146.3 10.4 %shard_map.77 = (bf16[48,2048]{1,0:T(8,128)(2,1)S(1)}, bf16[48,2048]{1,0:T(8,128)(2,1)S(1)}, bf16[48,2048]{1,0:T(8,128)(2,1)S(1)}, bf16[48,2048]{1,0:T(8,128)(2,1)S(1)}) custom-call(s32[2]{0:T(128)S(1)} %pad_add_fusion.1.ids, bf16[192,144]{1,0:T(8,128)(2,1)S(1)} %bitcast.72, bf16[2,144,1024]{2,1,0:T(8,128)(2,1)S(1)} %collective-permute-done.23.mine, ...), custom_call_target="tpu_custom_call" | custom-call | bytes 40000000 | tf_op jit(solution)/shard_map/pallas_call | solution.py:308
  156.7 3.2 %collective-permute-start.27 = (bf16[48,2048]{1,0:T(8,128)(2,1)S(1)}, bf16[48,2048]{1,0:T(8,128)(2,1)S(1)}, u32[]{:S(2)}, u32[]{:S(2)}) collective-permute-start(bf16[48,2048]{1,0:T(8,128)(2,1)S(1)} %get-tuple-element.102), channel_id=1, source_target_pairs={{0,12},{4,0},{8,4},{12,8},{1,13},{5,1},{9,5},{13,9},{2,14},{6,2},{... | collective-permute-start | bytes 589832 | tf_op jit(solution)/shard_map/ppermute | solution.py:428
  161.4 4.5 %collective-permute-done.27 = bf16[48,2048]{1,0:T(8,128)(2,1)S(1)} collective-permute-done((bf16[48,2048]{1,0:T(8,128)(2,1)S(1)}, bf16[48,2048]{1,0:T(8,128)(2,1)S(1)}, u32[]{:S(2)}, u32[]{:S(2)}) %collective-permute-start.27) | collective-permute-done | bytes 196640 | tf_op jit(solution)/shard_map/ppermute | solution.py:428
  165.9 12.1 %collective-permute-done.26 = bf16[48,2048]{1,0:T(8,128)(2,1)S(1)} collective-permute-done((bf16[48,2048]{1,0:T(8,128)(2,1)S(1)}, bf16[48,2048]{1,0:T(8,128)(2,1)S(1)}, u32[]{:S(2)}, u32[]{:S(2)}) %collective-permute-start.26) | collective-permute-done | bytes 196640 | tf_op jit(solution)/shard_map/ppermute | solution.py:428
  (73 shorter events, 19.4 us)
Async XLA Ops:
  0.0 22.4 %collective-permute-start.2 = (bf16[96,2048]{1,0:T(8,128)(2,1)}, bf16[96,2048]{1,0:T(8,128)(2,1)S(1)}, u32[]{:S(2)}, u32[]{:S(2)}) collective-permute-start(bf16[96,2048]{1,0:T(8,128)(2,1)} %param.11), channel_id=1, source_target_pairs={{0,0},{1,4},{2,8},{3,12},{4,1},{5,5},{6,9},{7,13},{8,2},{9,6},{10,... | collective-permute-start | bytes 1179656 | tf_op jit(solution)/shard_map/ppermute | solution.py:344
  1.6 20.8 %collective-permute-start.3 = (bf16[96,2048]{1,0:T(8,128)(2,1)}, bf16[96,2048]{1,0:T(8,128)(2,1)S(1)}, u32[]{:S(2)}, u32[]{:S(2)}) collective-permute-start(bf16[96,2048]{1,0:T(8,128)(2,1)} %param.11), channel_id=1, source_target_pairs={{0,4},{1,8},{2,12},{3,0},{4,5},{5,9},{6,13},{7,1},{8,6},{9,10},{10... | collective-permute-start | bytes 1179656 | tf_op jit(solution)/shard_map/ppermute | solution.py:344
  5.0 18.2 %collective-permute-start.4 = (bf16[96,2048]{1,0:T(8,128)(2,1)}, bf16[96,2048]{1,0:T(8,128)(2,1)S(1)}, u32[]{:S(2)}, u32[]{:S(2)}) collective-permute-start(bf16[96,2048]{1,0:T(8,128)(2,1)} %param.11), channel_id=1, source_target_pairs={{0,8},{1,12},{2,0},{3,4},{4,9},{5,13},{6,1},{7,5},{8,10},{9,14},{1... | collective-permute-start | bytes 1179656 | tf_op jit(solution)/shard_map/ppermute | solution.py:344
  11.0 20.0 %collective-permute-start.5 = (bf16[96,2048]{1,0:T(8,128)(2,1)}, bf16[96,2048]{1,0:T(8,128)(2,1)S(1)}, u32[]{:S(2)}, u32[]{:S(2)}) collective-permute-start(bf16[96,2048]{1,0:T(8,128)(2,1)} %param.11), channel_id=1, source_target_pairs={{0,12},{1,0},{2,4},{3,8},{4,13},{5,1},{6,5},{7,9},{8,14},{9,2},{10... | collective-permute-start | bytes 1179656 | tf_op jit(solution)/shard_map/ppermute | solution.py:344
  31.1 47.0 %collective-permute-start.6 = (bf16[96,2048]{1,0:T(8,128)(2,1)}, bf16[96,2048]{1,0:T(8,128)(2,1)S(1)}, u32[]{:S(2)}, u32[]{:S(2)}) collective-permute-start(bf16[96,2048]{1,0:T(8,128)(2,1)} %param.12), channel_id=1, source_target_pairs={{0,0},{1,4},{2,8},{3,12},{4,1},{5,5},{6,9},{7,13},{8,2},{9,6},{10,... | collective-permute-start | bytes 1179656 | tf_op jit(solution)/shard_map/ppermute | solution.py:344
  32.7 45.4 %collective-permute-start.7 = (bf16[96,2048]{1,0:T(8,128)(2,1)}, bf16[96,2048]{1,0:T(8,128)(2,1)S(1)}, u32[]{:S(2)}, u32[]{:S(2)}) collective-permute-start(bf16[96,2048]{1,0:T(8,128)(2,1)} %param.12), channel_id=1, source_target_pairs={{0,4},{1,8},{2,12},{3,0},{4,5},{5,9},{6,13},{7,1},{8,6},{9,10},{10... | collective-permute-start | bytes 1179656 | tf_op jit(solution)/shard_map/ppermute | solution.py:344
  44.2 33.9 %collective-permute-start.8 = (bf16[96,2048]{1,0:T(8,128)(2,1)}, bf16[96,2048]{1,0:T(8,128)(2,1)S(1)}, u32[]{:S(2)}, u32[]{:S(2)}) collective-permute-start(bf16[96,2048]{1,0:T(8,128)(2,1)} %param.12), channel_id=1, source_target_pairs={{0,8},{1,12},{2,0},{3,4},{4,9},{5,13},{6,1},{7,5},{8,10},{9,14},{1... | collective-permute-start | bytes 1179656 | tf_op jit(solution)/shard_map/ppermute | solution.py:344
  53.0 25.1 %collective-permute-start.9 = (bf16[96,2048]{1,0:T(8,128)(2,1)}, bf16[96,2048]{1,0:T(8,128)(2,1)S(1)}, u32[]{:S(2)}, u32[]{:S(2)}) collective-permute-start(bf16[96,2048]{1,0:T(8,128)(2,1)} %param.12), channel_id=1, source_target_pairs={{0,12},{1,0},{2,4},{3,8},{4,13},{5,1},{6,5},{7,9},{8,14},{9,2},{10... | collective-permute-start | bytes 1179656 | tf_op jit(solution)/shard_map/ppermute | solution.py:344
  63.2 2.9 %collective-permute-start.1 = (bf16[2,288,1024]{2,1,0:T(8,128)(2,1)S(1)}, bf16[2,288,1024]{2,1,0:T(8,128)(2,1)S(1)}, u32[]{:S(2)}, u32[]{:S(2)}) collective-permute-start(bf16[2,288,1024]{2,1,0:T(8,128)(2,1)S(1)} %get-tuple-element.38), channel_id=1, source_target_pairs={{0,1},{1,0},{2,3},{3,2},{4,5},{5,4},{6,7},{7,6},{8,9},{9,8},{10,11... | collective-permute-start | bytes 3538952 | tf_op jit(solution)/shard_map/cond/branch_1_fun/ppermute | solution.py:385
  67.7 33.9 %collective-permute-start.14 = (bf16[2,288,1024]{2,1,0:T(8,128)(2,1)}, bf16[2,288,1024]{2,1,0:T(8,128)(2,1)}, u32[]{:S(2)}, u32[]{:S(2)}) collective-permute-start(bf16[2,288,1024]{2,1,0:T(8,128)(2,1)} %get-tuple-element.89), channel_id=1, source_target_pairs={{0,2},{1,3},{2,0},{3,1},{4,6},{5,7},{6,4},{7,5},{8,10},{9,11},{10,... | collective-permute-start | bytes 3538952 | tf_op jit(solution)/shard_map/ppermute | solution.py:392
  84.8 16.8 %collective-permute-start.13 = (bf16[2,288,1024]{2,1,0:T(8,128)(2,1)}, bf16[2,288,1024]{2,1,0:T(8,128)(2,1)}, u32[]{:S(2)}, u32[]{:S(2)}) collective-permute-start(bf16[2,288,1024]{2,1,0:T(8,128)(2,1)} %get-tuple-element.88), channel_id=1, source_target_pairs={{0,1},{1,0},{2,3},{3,2},{4,5},{5,4},{6,7},{7,6},{8,9},{9,8},{10,11... | collective-permute-start | bytes 3538952 | tf_op jit(solution)/shard_map/ppermute | solution.py:396
  84.9 2.9 %collective-permute-start.10 = (bf16[144,1024]{1,0:T(8,128)(2,1)S(1)}, bf16[144,1024]{1,0:T(8,128)(2,1)S(1)}, u32[]{:S(2)}, u32[]{:S(2)}) collective-permute-start(bf16[144,1024]{1,0:T(8,128)(2,1)S(1)} %get-tuple-element.80), channel_id=1, source_target_pairs={{0,1},{1,0},{2,3},{3,2},{4,5},{5,4},{6,7},{7,6},{8,9},{9,8},{10,11... | collective-permute-start | bytes 884744 | tf_op jit(solution)/shard_map/ppermute | solution.py:399
  85.4 6.7 %collective-permute-start.11 = (bf16[144,1024]{1,0:T(8,128)(2,1)S(1)}, bf16[144,1024]{1,0:T(8,128)(2,1)S(1)}, u32[]{:S(2)}, u32[]{:S(2)}) collective-permute-start(bf16[144,1024]{1,0:T(8,128)(2,1)S(1)} %get-tuple-element.82), channel_id=1, source_target_pairs={{0,1},{1,0},{2,3},{3,2},{4,5},{5,4},{6,7},{7,6},{8,9},{9,8},{10,11... | collective-permute-start | bytes 884744 | tf_op jit(solution)/shard_map/ppermute | solution.py:399
  87.9 19.1 %collective-permute-start.12 = (bf16[144,1024]{1,0:T(8,128)(2,1)S(1)}, bf16[144,1024]{1,0:T(8,128)(2,1)}, u32[]{:S(2)}, u32[]{:S(2)}) collective-permute-start(bf16[144,1024]{1,0:T(8,128)(2,1)S(1)} %add_convert_fusion.2), channel_id=1, source_target_pairs={{0,2},{1,3},{2,0},{3,1},{4,6},{5,7},{6,4},{7,5},{8,10},{9,11},{10,... | collective-permute-start | bytes 884744 | tf_op jit(solution)/shard_map/ppermute | solution.py:413
  92.2 21.1 %collective-permute-start.17 = (bf16[144,1024]{1,0:T(8,128)(2,1)S(1)}, bf16[144,1024]{1,0:T(8,128)(2,1)S(1)}, u32[]{:S(2)}, u32[]{:S(2)}) collective-permute-start(bf16[144,1024]{1,0:T(8,128)(2,1)S(1)} %add_convert_fusion.1), channel_id=1, source_target_pairs={{0,2},{1,3},{2,0},{3,1},{4,6},{5,7},{6,4},{7,5},{8,10},{9,11},{10,... | collective-permute-start | bytes 884744 | tf_op jit(solution)/shard_map/ppermute | solution.py:413
  99.0 2.1 %collective-permute-start = (bf16[288,1024]{1,0:T(8,128)(2,1)S(1)}, bf16[288,1024]{1,0:T(8,128)(2,1)S(1)}, u32[]{:S(2)}, u32[]{:S(2)}) collective-permute-start(bf16[288,1024]{1,0:T(8,128)(2,1)S(1)} %get-tuple-element.44), channel_id=1, source_target_pairs={{0,1},{1,0},{2,3},{3,2},{4,5},{5,4},{6,7},{7,6},{8,9},{9,8},{10,11... | collective-permute-start | bytes 1769480 | tf_op jit(solution)/shard_map/cond/branch_1_fun/ppermute | solution.py:404
  108.3 17.6 %collective-permute-start.15 = (bf16[2,144,1024]{2,1,0:T(8,128)(2,1)S(1)}, bf16[2,144,1024]{2,1,0:T(8,128)(2,1)S(1)}, u32[]{:S(2)}, u32[]{:S(2)}) collective-permute-start(bf16[2,144,1024]{2,1,0:T(8,128)(2,1)S(1)} %pad_maximum_fusion.mine_a), channel_id=1, source_target_pairs={{0,2},{1,3},{2,0},{3,1},{4,6},{5,7},{6,4},{7,5},{8,10},{9,11},{10,... | collective-permute-start | bytes 1769480 | tf_op jit(solution)/shard_map/ppermute | solution.py:419
  110.9 5.6 %collective-permute-start.16 = (bf16[2,144,1024]{2,1,0:T(8,128)(2,1)S(1)}, bf16[2,144,1024]{2,1,0:T(8,128)(2,1)S(1)}, u32[]{:S(2)}, u32[]{:S(2)}) collective-permute-start(bf16[2,144,1024]{2,1,0:T(8,128)(2,1)S(1)} %pad_maximum_fusion.mine_a), channel_id=1, source_target_pairs={{0,1},{1,0},{2,3},{3,2},{4,5},{5,4},{6,7},{7,6},{8,9},{9,8},{10,11... | collective-permute-start | bytes 1769480 | tf_op jit(solution)/shard_map/ppermute | solution.py:418
  113.6 2.9 %collective-permute-start.18 = (bf16[2,144,1024]{2,1,0:T(8,128)(2,1)S(1)}, bf16[2,144,1024]{2,1,0:T(8,128)(2,1)S(1)}, u32[]{:S(2)}, u32[]{:S(2)}) collective-permute-start(bf16[2,144,1024]{2,1,0:T(8,128)(2,1)S(1)} %pad_maximum_fusion.1.mine_b), channel_id=1, source_target_pairs={{0,1},{1,0},{2,3},{3,2},{4,5},{5,4},{6,7},{7,6},{8,9},{9,8},{10,11... | collective-permute-start | bytes 1769480 | tf_op jit(solution)/shard_map/ppermute | solution.py:418
  114.0 24.3 %collective-permute-start.23 = (bf16[2,144,1024]{2,1,0:T(8,128)(2,1)S(1)}, bf16[2,144,1024]{2,1,0:T(8,128)(2,1)S(1)}, u32[]{:S(2)}, u32[]{:S(2)}) collective-permute-start(bf16[2,144,1024]{2,1,0:T(8,128)(2,1)S(1)} %pad_maximum_fusion.1.mine_b), channel_id=1, source_target_pairs={{0,2},{1,3},{2,0},{3,1},{4,6},{5,7},{6,4},{7,5},{8,10},{9,11},{10,... | collective-permute-start | bytes 1769480 | tf_op jit(solution)/shard_map/ppermute | solution.py:419
  125.9 2.0 %collective-permute-start.19 = (bf16[2,144,1024]{2,1,0:T(8,128)(2,1)S(1)}, bf16[2,144,1024]{2,1,0:T(8,128)(2,1)S(1)}, u32[]{:S(2)}, u32[]{:S(2)}) collective-permute-start(bf16[2,144,1024]{2,1,0:T(8,128)(2,1)S(1)} %collective-permute-done.15.mine), channel_id=1, source_target_pairs={{0,1},{1,0},{2,3},{3,2},{4,5},{5,4},{6,7},{7,6},{8,9},{9,8},{10,11... | collective-permute-start | bytes 1769480 | tf_op jit(solution)/shard_map/ppermute | solution.py:423
  138.3 8.0 %collective-permute-start.24 = (bf16[2,144,1024]{2,1,0:T(8,128)(2,1)S(1)}, bf16[2,144,1024]{2,1,0:T(8,128)(2,1)S(1)}, u32[]{:S(2)}, u32[]{:S(2)}) collective-permute-start(bf16[2,144,1024]{2,1,0:T(8,128)(2,1)S(1)} %collective-permute-done.23.mine), channel_id=1, source_target_pairs={{0,1},{1,0},{2,3},{3,2},{4,5},{5,4},{6,7},{7,6},{8,9},{9,8},{10,11... | collective-permute-start | bytes 1769480 | tf_op jit(solution)/shard_map/ppermute | solution.py:423
  139.3 21.8 %collective-permute-start.22 = (bf16[48,2048]{1,0:T(8,128)(2,1)S(1)}, bf16[48,2048]{1,0:T(8,128)(2,1)S(1)}, u32[]{:S(2)}, u32[]{:S(2)}) collective-permute-start(bf16[48,2048]{1,0:T(8,128)(2,1)S(1)} %get-tuple-element.96), channel_id=1, source_target_pairs={{0,12},{4,0},{8,4},{12,8},{1,13},{5,1},{9,5},{13,9},{2,14},{6,2},{... | collective-permute-start | bytes 589832 | tf_op jit(solution)/shard_map/ppermute | solution.py:428
  144.3 17.0 %collective-permute-start.21 = (bf16[48,2048]{1,0:T(8,128)(2,1)S(1)}, bf16[48,2048]{1,0:T(8,128)(2,1)S(1)}, u32[]{:S(2)}, u32[]{:S(2)}) collective-permute-start(bf16[48,2048]{1,0:T(8,128)(2,1)S(1)} %get-tuple-element.95), channel_id=1, source_target_pairs={{0,8},{4,12},{8,0},{12,4},{1,9},{5,13},{9,1},{13,5},{2,10},{6,14},... | collective-permute-start | bytes 589832 | tf_op jit(solution)/shard_map/ppermute | solution.py:428
  144.3 17.0 %collective-permute-start.20 = (bf16[48,2048]{1,0:T(8,128)(2,1)S(1)}, bf16[48,2048]{1,0:T(8,128)(2,1)S(1)}, u32[]{:S(2)}, u32[]{:S(2)}) collective-permute-start(bf16[48,2048]{1,0:T(8,128)(2,1)S(1)} %get-tuple-element.94), channel_id=1, source_target_pairs={{0,4},{4,8},{8,12},{12,0},{1,5},{5,9},{9,13},{13,1},{2,6},{6,10},{... | collective-permute-start | bytes 589832 | tf_op jit(solution)/shard_map/ppermute | solution.py:428
  156.7 9.2 %collective-permute-start.27 = (bf16[48,2048]{1,0:T(8,128)(2,1)S(1)}, bf16[48,2048]{1,0:T(8,128)(2,1)S(1)}, u32[]{:S(2)}, u32[]{:S(2)}) collective-permute-start(bf16[48,2048]{1,0:T(8,128)(2,1)S(1)} %get-tuple-element.102), channel_id=1, source_target_pairs={{0,12},{4,0},{8,4},{12,8},{1,13},{5,1},{9,5},{13,9},{2,14},{6,2},{... | collective-permute-start | bytes 589832 | tf_op jit(solution)/shard_map/ppermute | solution.py:428
  160.0 18.1 %collective-permute-start.26 = (bf16[48,2048]{1,0:T(8,128)(2,1)S(1)}, bf16[48,2048]{1,0:T(8,128)(2,1)S(1)}, u32[]{:S(2)}, u32[]{:S(2)}) collective-permute-start(bf16[48,2048]{1,0:T(8,128)(2,1)S(1)} %get-tuple-element.101), channel_id=1, source_target_pairs={{0,8},{4,12},{8,0},{12,4},{1,9},{5,13},{9,1},{13,5},{2,10},{6,14},... | collective-permute-start | bytes 589832 | tf_op jit(solution)/shard_map/ppermute | solution.py:428
  161.1 17.0 %collective-permute-start.25 = (bf16[48,2048]{1,0:T(8,128)(2,1)S(1)}, bf16[48,2048]{1,0:T(8,128)(2,1)S(1)}, u32[]{:S(2)}, u32[]{:S(2)}) collective-permute-start(bf16[48,2048]{1,0:T(8,128)(2,1)S(1)} %get-tuple-element.100), channel_id=1, source_target_pairs={{0,4},{4,8},{8,12},{12,0},{1,5},{5,9},{9,13},{13,1},{2,6},{6,10},{... | collective-permute-start | bytes 589832 | tf_op jit(solution)/shard_map/ppermute | solution.py:428

commit v5 on v4

--- a/solution.py
+++ b/solution.py
@@ -169,9 +169,8 @@
         moves = [start(rows_in, rows_v, sems.at[0, 0])]
         outs = ((send,), (keep,))
     else:
-        select_ref, p0, p1, p2, p3, down, *sides, rows_out, down_v, out_v, rows_v, arrived, sems = refs
-        moves = pick_start((p0, p1, p2, p3), arrived, sems.at[0])
-        outs = (sides[:2], sides[2:])
+        order_ref, *parts, down, o0, o1, o2, o3, rows_out, down_v, out_v, rows_v, sems = refs
+        outs = ((o0, o1), (o2, o3))
     core, x = ids[0], ids[1]
     block = down_v.shape[1]
     loads = Stream(
@@ -181,7 +180,10 @@
     if near:
         moves[0].wait()
     else:
-        pick_end(moves, select_ref, arrived, rows_v)
+        total = jnp.dot(order_ref[0], parts[0][...], preferred_element_type=F32)
+        for k in range(1, len(parts)):
+            total += jnp.dot(order_ref[k], parts[k][...], preferred_element_type=F32)
+        rows_v[...] = total.astype(BF)
         stores.append(start(rows_v, rows_out, sems.at[0, 0]))
     for i in range(2):
         loads.wait(i)
@@ -196,19 +198,19 @@
 
 def hidden_grads(near, ids, rows, down_weight):
     depth, block = down_weight.shape[1], down_weight.shape[0] // 4
-    count = rows.shape[0] if near else rows[0].shape[0]
+    count = rows.shape[0] if near else rows[0].shape[1]
     args = (rows,) if near else rows
     outs = [((count, block), BF)] * 2 if near else [((count // 2, block), BF)] * 4 + [((count, depth), BF)]
-    arrived = [] if near else [pltpu.VMEM((rows[0].shape[1], depth), BF)]
     return call(
         functools.partial(hidden_kernel, near),
-        [IN_SMEM] + [IN_HBM if near else IN_VMEM] + [IN_HBM] * len(args),
+        [IN_SMEM] + [IN_HBM if near else IN_VMEM] * len(args) + [IN_HBM],
         outs,
         [
             pltpu.VMEM((2, block, depth), BF),
             pltpu.VMEM((2, count, block), BF),
             pltpu.VMEM((count, depth), BF),
-        ] + arrived + [pltpu.SemaphoreType.DMA((4, 4))],
+            pltpu.SemaphoreType.DMA((4, 4)),
+        ],
         HIDDEN_COST,
     )(ids, *args, down_weight)
 
@@ -377,7 +379,29 @@
     final = (spot[:, None] == jnp.arange(sets * piece)[None, :]).astype(BF)
 
     present = all_counts[0] >= 0
-    held = after(grad_out, select, present, *token_parts)
+
+    share = live_rows // n
+    shards = jnp.stack([s, s ^ 2, s ^ 1, s ^ 3])
+    to_share = (index[None, :] == share * s + jnp.arange(share, dtype=jnp.int32)[:, None]).astype(BF)
+    local = shards[slot // shard_rows] * shard_rows + slot % shard_rows
+    from_local = (packing[:, None] == local[None, :]).astype(BF)
+    pick = jnp.dot(to_share, from_local, preferred_element_type=F32).astype(BF)
+    came = (t - jnp.arange(n, dtype=jnp.int32)) % n
+    order_of = (
+        jnp.arange(live_rows, dtype=jnp.int32)[None, :, None]
+        == (share * came[:, None] + jnp.arange(share, dtype=jnp.int32)[None, :])[:, None, :]
+    ).astype(BF)
+
+    def balance(grad_out, far, pick):
+        mine = jnp.concatenate([grad_out, far])
+        whole = jnp.concatenate([mine, lax.ppermute(mine, "seq", sibling)])
+        return jnp.dot(pick, whole, preferred_element_type=F32).astype(BF)
+
+    def no_balance(*_):
+        return jnp.zeros((share, depth), BF)
+
+    held = lax.cond(present, balance, no_balance, grad_out, lax.ppermute(grad_out, "seq", across), pick)
+    held = after(held, select, present, order_of, *token_parts)
     grad_parts = [spread(held, k) for k in range(n)]
 
     def far_side(ids, select, gate_weight, up_weight, *token_parts):
@@ -392,7 +416,7 @@
     across_near = lax.ppermute(pair_far, "seq", across)
 
     send, keep = project(True, ids, picked, gate_weight, up_weight)
-    *outs, picked = hidden_grads(False, ids, (after(select, send), *grad_parts), down_weight)
+    *outs, picked = hidden_grads(False, ids, (after(order_of, send), *grad_parts), down_weight)
     near = keep.astype(F32) + lax.ppermute(after(send, outs[0]), "seq", sibling).astype(F32) + across_near.astype(F32)
     pairs = []
     for m in range(sets):
@@ -423,7 +447,7 @@
         d_both = lax.ppermute(after(ds_far[m], parts[0]), "seq", sibling)
         parts = far_back(ids, place[m].reshape(n * piece, set_rows), ds_far[m], d_both, gate_weight, up_weight, firsts[m])
         total = parts[0].astype(F32)
-        for k in range(1, n):
+        for k in (1, 3, 2):
             shift = [(i, (i + k) % n) for i in range(n)]
             total += lax.ppermute(parts[k], "tensor", shift).astype(F32)
         pieces.append(total.astype(BF))

time: 180 us -> 171 us (0.950)
  starting transfers between devices: 56 us -> 34.9 us
  blocking collectives: 5.96 us -> 20.8 us
  waiting for transfers between devices: 39.7 us -> 32 us
  matrix products: 2.17 us -> 4.25 us
    ppermute x8, starting transfers between devices: 33.4 us -> 17.8 us  [spread(): return lax.ppermute(value, ('tensor', 'seq'), pairs)]
    unnamed x1, blocking collectives: 5.96 us -> 20.8 us
    ppermute x8, waiting for transfers between devices: 8.6 us -> 0.02 us  [spread(): return lax.ppermute(value, ('tensor', 'seq'), pairs)]
    ppermute x6, waiting for transfers between devices: 16.8 us -> 14 us  [tuned(): total += lax.ppermute(parts[k], 'tensor', shift).astype(F32)]
    ppermute x2, starting transfers between devices: 4.86 us -> 2.17 us  [tuned(): got = lax.ppermute(pairs[m], 'seq', across)]
    ppermute x0 -> x2, waiting for transfers between devices: none -> 2.27 us  [the longest x1 2.26 us: balance(): whole = jnp.concatenate([mine, lax.ppermute(mine, 'seq', sibling)])]
    ppermute x6, starting transfers between devices: 10.1 us -> 8.06 us  [tuned(): total += lax.ppermute(parts[k], 'tensor', shift).astype(F32)]
  transfers between devices with their start and end apart: 28 -> 30, of which waited for: 12 -> 9; matrix products, arithmetic and copies ran while one was open for 8% -> 10% of each run, Pallas kernels for 34% -> 37%
where the time goes in v5:
time: 171 us; the launch traced here: 169 us
  Pallas kernels  62.3 us (36%)
  starting transfers between devices  34.9 us (20%)
  waiting for transfers between devices  32 us (19%)
  blocking collectives  20.8 us (12%)
  other arithmetic  10.5 us (6%)
  matrix products  4.25 us (2%)
  local copies, waits for them, and re-layouts  2.62 us (2%)
    pallas_call x2, Pallas kernels, far_back(): call(far_kernel, [IN_SMEM, IN_VMEM] + [IN_HBM] * 5, [((count // 4, depth)...  20.8 us
    unnamed x1, blocking collectives  20.8 us
    pallas_call x2, Pallas kernels, project(): call(functools.partial(project_kernel, near), [IN_SMEM] + [IN_HBM if near...  19.2 us
    ppermute x8, starting transfers between devices, spread(): return lax.ppermute(value, ('tensor', 'seq'), pairs)  17.8 us
    ppermute x6, waiting for transfers between devices, tuned(): total += lax.ppermute(parts[k], 'tensor', shift).astype(F32)  14 us
    pallas_call x2, Pallas kernels, hidden_grads(): call(functools.partial(hidden_kernel, near), [IN_SMEM] + [IN_HBM if near...  13.3 us
    pallas_call x1, Pallas kernels, near_back(): call(near_kernel, [IN_SMEM] + [IN_HBM] * 6, [((rows, depth), F32)] * 2, [...  8.99 us
    ppermute x6, starting transfers between devices, tuned(): total += lax.ppermute(parts[k], 'tensor', shift).astype(F32)  8.06 us
  transfers between devices with their start and end apart: 30, of which 9 were waited for; matrix products, arithmetic and copies ran while one was open for 10% of the time, Pallas kernels for 37%

profile of v5, /device:TPU:0, one launch (start us, length us, event | category | flops | bytes accessed | tf_op | source)
XLA Modules:
  0.0 168.7 jit_solution(3824372298058929506)
XLA Ops:
  0.0 1.6 collective-permute-start.3
  1.6 3.4 %collective-permute-start.4 = (bf16[96,2048]{1,0:T(8,128)(2,1)}, bf16[96,2048]{1,0:T(8,128)(2,1)S(1)}, u32[]{:S(2)}, u32[]{:S(2)}) collective-permute-start(bf16[96,2048]{1,0:T(8,128)(2,1)} %param.13), channel_id=1, source_target_pairs={{0,4},{1,8},{2,12},{3,0},{4,5},{5,9},{6,13},{7,1},{8,6},{9,10},{10... | collective-permute-start | bytes 1179656 | tf_op jit(solution)/shard_map/ppermute | solution.py:346
  5.0 3.4 %collective-permute-start.5 = (bf16[96,2048]{1,0:T(8,128)(2,1)}, bf16[96,2048]{1,0:T(8,128)(2,1)S(1)}, u32[]{:S(2)}, u32[]{:S(2)}) collective-permute-start(bf16[96,2048]{1,0:T(8,128)(2,1)} %param.13), channel_id=1, source_target_pairs={{0,8},{1,12},{2,0},{3,4},{4,9},{5,13},{6,1},{7,5},{8,10},{9,14},{1... | collective-permute-start | bytes 1179656 | tf_op jit(solution)/shard_map/ppermute | solution.py:346
  8.4 2.6 %collective-permute-start.6 = (bf16[96,2048]{1,0:T(8,128)(2,1)}, bf16[96,2048]{1,0:T(8,128)(2,1)S(1)}, u32[]{:S(2)}, u32[]{:S(2)}) collective-permute-start(bf16[96,2048]{1,0:T(8,128)(2,1)} %param.13), channel_id=1, source_target_pairs={{0,12},{1,0},{2,4},{3,8},{4,13},{5,1},{6,5},{7,9},{8,14},{9,2},{10... | collective-permute-start | bytes 1179656 | tf_op jit(solution)/shard_map/ppermute | solution.py:346
  13.7 20.8 %all-reduce = s32[4]{0:T(128)S(1)} all-reduce(s32[4]{0:T(128)S(1)} %dynamic-update-slice), channel_id=1, replica_groups=mesh['group'=2,'tensor'=4,'seq'=4] {'seq'}, use_global_device_ids=true, to_apply=%add | all-reduce | flops 4 | bytes 32
  36.2 1.8 %convolution_convert_fusion.2 = bf16[288,384]{1,0:T(8,128)(2,1)} fusion(s32[384]{0:T(512)S(1)} %fusion.46, s32[384]{0:T(512)} %param.16, s32[384]{0:T(512)S(1)} %get-tuple-element.124), kind=kOutput, calls=%fused_computation.12 | convolution fusion | flops 85303296 | bytes 225792 | tf_op jit(solution)/shard_map/dot_general | solution.py:361
  39.2 3.9 %conditional.4 = (bf16[72,2048]{1,0:T(8,128)(2,1)S(1)}) conditional(s32[]{:T(128)} %convert_element_type.134, () %tuple.43, (bf16[96,2048]{1,0:T(8,128)(2,1)}, bf16[96,2048]{1,0:T(8,128)(2,1)S(1)}, bf16[72,384]{1,0:T(8,128)(2,1)S(1)}) %tuple.44), branch_computations={%region_7.8_spmd, %region_8.9_spmd} | conditional | flops 119685120 | bytes 8214604 | solution.py:403
  40.4 2.3 %collective-permute-done.2 = bf16[192,2048]{1,0:T(8,128)(2,1)S(1)} collective-permute-done((bf16[192,2048]{1,0:T(8,128)(2,1)S(1)}, bf16[192,2048]{1,0:T(8,128)(2,1)S(1)}, u32[]{:S(2)}, u32[]{:S(2)}) %collective-permute-start.2) | collective-permute-done | bytes 786464 | tf_op jit(solution)/shard_map/cond/branch_1_fun/ppermute | solution.py:397
  43.8 3.1 %collective-permute-start.9 = (bf16[72,2048]{1,0:T(8,128)(2,1)S(1)}, bf16[72,2048]{1,0:T(8,128)(2,1)S(1)}, u32[]{:S(2)}, u32[]{:S(2)}) collective-permute-start(bf16[72,2048]{1,0:T(8,128)(2,1)S(1)} %get-tuple-element.139), channel_id=1, source_target_pairs={{0,4},{1,8},{2,12},{3,0},{4,5},{5,9},{6,13},{7,1},{8,6},{9,10},{10... | collective-permute-start | bytes 884744 | tf_op jit(solution)/shard_map/ppermute | solution.py:346
  46.9 1.9 %collective-permute-start.10 = (bf16[72,2048]{1,0:T(8,128)(2,1)S(1)}, bf16[72,2048]{1,0:T(8,128)(2,1)S(1)}, u32[]{:S(2)}, u32[]{:S(2)}) collective-permute-start(bf16[72,2048]{1,0:T(8,128)(2,1)S(1)} %get-tuple-element.139), channel_id=1, source_target_pairs={{0,8},{1,12},{2,0},{3,4},{4,9},{5,13},{6,1},{7,5},{8,10},{9,14},{1... | collective-permute-start | bytes 884744 | tf_op jit(solution)/shard_map/ppermute | solution.py:346
  50.0 14.5 %conditional.3 = (bf16[2,288,1024]{2,1,0:T(8,128)(2,1)}, bf16[288,2048]{1,0:T(8,128)(2,1)S(1)}) conditional(s32[]{:T(128)} %convert_element_type.134, () %tuple.40, (s32[2]{0:T(128)S(1)}, bf16[288,384]{1,0:T(8,128)(2,1)}, bf16[96,2048]{1,0:T(8,128)(2,1)S(1)}, bf16[96,2048]{1,0:T(8,128)(2,1)S(1)}, bf16[96,2048]{1,0:T(8,128)(2,1)S(1)}, ...), branch_computations={%region_5.6_spmd, %region_6.7_spmd} | conditional | flops 2359296 | bytes 28257592 | solution.py:415
  50.0 10.1 %branch_1_fun.2 = (bf16[2,288,1024]{2,1,0:T(8,128)(2,1)S(1)}, bf16[2,288,1024]{2,1,0:T(8,128)(2,1)S(1)}, bf16[288,2048]{1,0:T(8,128)(2,1)S(1)}) custom-call(s32[2]{0:T(128)S(1)} %get-tuple-element.38.ids, bf16[288,384]{1,0:T(8,128)(2,1)} %get-tuple-element.39.refs_0_, bf16[96,2048]{1,0:T(8,128)(2,1)S(1)} %get-tuple-element.40.refs_1_, ...), custom_call_target="tpu_custom_call" | custom-call | bytes 20000000 | tf_op jit(solution)/shard_map/cond/branch_1_fun/pallas_call | solution.py:154
  60.2 2.8 %collective-permute-done.1 = bf16[2,288,1024]{2,1,0:T(8,128)(2,1)S(1)} collective-permute-done((bf16[2,288,1024]{2,1,0:T(8,128)(2,1)S(1)}, bf16[2,288,1024]{2,1,0:T(8,128)(2,1)S(1)}, u32[]{:S(2)}, u32[]{:S(2)}) %collective-permute-start.1) | collective-permute-done | bytes 1179680 | tf_op jit(solution)/shard_map/cond/branch_1_fun/ppermute | solution.py:409
  63.0 1.5 add_convert_fusion
  65.1 9.1 %shard_map.73 = (bf16[2,288,1024]{2,1,0:T(8,128)(2,1)}, bf16[2,288,1024]{2,1,0:T(8,128)(2,1)S(1)}) custom-call(s32[2]{0:T(128)S(1)} %pad_add_fusion.1.ids, bf16[288,2048]{1,0:T(8,128)(2,1)S(1)} %get-tuple-element.86.refs_0_, bf16[2048,4096]{1,0:T(8,128)(2,1)} %gate_w.5, bf16[2048,4096]{1,0:T(8,128)(2,1)} %up_w.5), custom_call_target="tpu_custom_call" | custom-call | bytes 20000000 | tf_op jit(solution)/shard_map/pallas_call | solution.py:154
  74.3 7.1 %shard_map.74 = (bf16[144,1024]{1,0:T(8,128)(2,1)S(1)}, bf16[144,1024]{1,0:T(8,128)(2,1)S(1)}, bf16[144,1024]{1,0:T(8,128)(2,1)S(1)}, bf16[144,1024]{1,0:T(8,128)(2,1)S(1)}, bf16[288,2048]{1,0:T(8,128)(2,1)S(1)}) custom-call(s32[2]{0:T(128)S(1)} %pad_add_fusion.1.ids, bf16[4,288,72]{2,1,0:T(8,128)(2,1)S(1)} %fusion.15.refs_0_, ...), custom_call_target="tpu_custom_call" | custom-call | bytes 60000000 | tf_op jit(solution)/shard_map/pallas_call | solution.py:204
  82.3 2.2 %collective-permute-done.12 = bf16[144,1024]{1,0:T(8,128)(2,1)S(1)} collective-permute-done((bf16[144,1024]{1,0:T(8,128)(2,1)S(1)}, bf16[144,1024]{1,0:T(8,128)(2,1)S(1)}, u32[]{:S(2)}, u32[]{:S(2)}) %collective-permute-start.12) | collective-permute-done | bytes 294944 | tf_op jit(solution)/shard_map/ppermute | solution.py:423
  86.8 8.6 %conditional.5 = (f32[288,1024]{1,0:T(8,128)S(1)}, f32[288,1024]{1,0:T(8,128)S(1)}) conditional(s32[]{:T(128)} %convert_element_type.134, () %tuple.39, (s32[2]{0:T(128)S(1)}, bf16[288,2048]{1,0:T(8,128)(2,1)S(1)}, bf16[4096,2048]{1,0:T(8,128)(2,1)}) %tuple.48), branch_computations={%region_9.10_spmd, %region_10.11_spmd} | conditional | flops 589824 | bytes 65898296 | solution.py:433
  86.8 6.2 %branch_1_fun.3 = (bf16[288,1024]{1,0:T(8,128)(2,1)S(1)}, bf16[288,1024]{1,0:T(8,128)(2,1)S(1)}) custom-call(s32[2]{0:T(128)S(1)} %get-tuple-element.52.ids, bf16[288,2048]{1,0:T(8,128)(2,1)S(1)} %get-tuple-element.53.refs_0_, bf16[4096,2048]{1,0:T(8,128)(2,1)} %get-tuple-element.54.refs_1_), custom_call_target="tpu_custom_call" | custom-call | bytes 60000000 | tf_op jit(solution)/shard_map/cond/branch_1_fun/pallas_call | solution.py:204
  93.2 1.9 %collective-permute-done = bf16[288,1024]{1,0:T(8,128)(2,1)S(1)} collective-permute-done((bf16[288,1024]{1,0:T(8,128)(2,1)S(1)}, bf16[288,1024]{1,0:T(8,128)(2,1)S(1)}, u32[]{:S(2)}, u32[]{:S(2)}) %collective-permute-start) | collective-permute-done | bytes 589856 | tf_op jit(solution)/shard_map/cond/branch_1_fun/ppermute | solution.py:428
  95.6 2.3 %convert_add_fusion = f32[2,288,1024]{2,1,0:T(8,128)S(1)} fusion(bf16[2,288,1024]{2,1,0:T(8,128)(2,1)} %collective-permute-done.16, bf16[2,288,1024]{2,1,0:T(8,128)(2,1)} %collective-permute-done.15, bf16[2,288,1024]{2,1,0:T(8,128)(2,1)S(1)} %get-tuple-element.99), kind=kLoop, calls=%fused_computation.10 | loop fusion | flops 2949120 | bytes 5898240 | tf_op jit(solution)/shard_map/add | solution.py:420
  97.9 3.3 %collective-permute-done.14 = bf16[144,1024]{1,0:T(8,128)(2,1)S(1)} collective-permute-done((bf16[144,1024]{1,0:T(8,128)(2,1)S(1)}, bf16[144,1024]{1,0:T(8,128)(2,1)S(1)}, u32[]{:S(2)}, u32[]{:S(2)}) %collective-permute-start.14) | collective-permute-done | bytes 294944 | tf_op jit(solution)/shard_map/ppermute | solution.py:437
  101.6 2.5 %collective-permute-start.17 = (bf16[2,144,1024]{2,1,0:T(8,128)(2,1)S(1)}, bf16[2,144,1024]{2,1,0:T(8,128)(2,1)S(1)}, u32[]{:S(2)}, u32[]{:S(2)}) collective-permute-start(bf16[2,144,1024]{2,1,0:T(8,128)(2,1)S(1)} %pad_maximum_fusion.1.mine_a), channel_id=1, source_target_pairs={{0,2},{1,3},{2,0},{3,1},{4,6},{5,7},{6,4},{7,5},{8,10},{9,11},{10,... | collective-permute-start | bytes 1769480 | tf_op jit(solution)/shard_map/ppermute | solution.py:443
  104.2 3.4 %collective-permute-done.19 = bf16[144,1024]{1,0:T(8,128)(2,1)S(1)} collective-permute-done((bf16[144,1024]{1,0:T(8,128)(2,1)S(1)}, bf16[144,1024]{1,0:T(8,128)(2,1)S(1)}, u32[]{:S(2)}, u32[]{:S(2)}) %collective-permute-start.19) | collective-permute-done | bytes 294944 | tf_op jit(solution)/shard_map/ppermute | solution.py:437
  108.3 2.5 %collective-permute-start.25 = (bf16[2,144,1024]{2,1,0:T(8,128)(2,1)S(1)}, bf16[2,144,1024]{2,1,0:T(8,128)(2,1)S(1)}, u32[]{:S(2)}, u32[]{:S(2)}) collective-permute-start(bf16[2,144,1024]{2,1,0:T(8,128)(2,1)S(1)} %pad_maximum_fusion.2.mine_b), channel_id=1, source_target_pairs={{0,2},{1,3},{2,0},{3,1},{4,6},{5,7},{6,4},{7,5},{8,10},{9,11},{10,... | collective-permute-start | bytes 1769480 | tf_op jit(solution)/shard_map/ppermute | solution.py:443
  110.8 9.0 %shard_map.75 = (f32[144,2048]{1,0:T(8,128)S(1)}, f32[144,2048]{1,0:T(8,128)S(1)}) custom-call(s32[2]{0:T(128)S(1)} %pad_add_fusion.1.ids, bf16[2,144,1024]{2,1,0:T(8,128)(2,1)S(1)} %pad_maximum_fusion.1.mine_a, bf16[2,144,1024]{2,1,0:T(8,128)(2,1)S(1)} %collective-permute-done.18.other_a, bf16[2,144,1024]{2,1,0:T(8,128)(2,1)S(1)} %pad_maximum_fusion.2.mine_b, ...), custom_call_target="tpu_custom_call" | custom-call | bytes 40000000 | tf_op jit(solution)/shard_map/pallas_call | solution.py:291
  120.4 1.8 %collective-permute-done.21.other = bf16[2,144,1024]{2,1,0:T(8,128)(2,1)S(1)} collective-permute-done((bf16[2,144,1024]{2,1,0:T(8,128)(2,1)S(1)}, bf16[2,144,1024]{2,1,0:T(8,128)(2,1)S(1)}, u32[]{:S(2)}, u32[]{:S(2)}) %collective-permute-start.21) | collective-permute-done | bytes 589856 | tf_op jit(solution)/shard_map/ppermute | solution.py:447
  122.2 10.4 %shard_map.76 = (bf16[48,2048]{1,0:T(8,128)(2,1)S(1)}, bf16[48,2048]{1,0:T(8,128)(2,1)S(1)}, bf16[48,2048]{1,0:T(8,128)(2,1)S(1)}, bf16[48,2048]{1,0:T(8,128)(2,1)S(1)}) custom-call(s32[2]{0:T(128)S(1)} %pad_add_fusion.1.ids, bf16[192,144]{1,0:T(8,128)(2,1)S(1)} %bitcast.76, bf16[2,144,1024]{2,1,0:T(8,128)(2,1)S(1)} %collective-permute-done.17.mine, ...), custom_call_target="tpu_custom_call" | custom-call | bytes 40000000 | tf_op jit(solution)/shard_map/pallas_call | solution.py:310
  133.6 2.5 %collective-permute-start.24 = (bf16[48,2048]{1,0:T(8,128)(2,1)S(1)}, bf16[48,2048]{1,0:T(8,128)(2,1)S(1)}, u32[]{:S(2)}, u32[]{:S(2)}) collective-permute-start(bf16[48,2048]{1,0:T(8,128)(2,1)S(1)} %get-tuple-element.108), channel_id=1, source_target_pairs={{0,8},{4,12},{8,0},{12,4},{1,9},{5,13},{9,1},{13,5},{2,10},{6,14},... | collective-permute-start | bytes 589832 | tf_op jit(solution)/shard_map/ppermute | solution.py:452
  139.5 10.4 %shard_map.77 = (bf16[48,2048]{1,0:T(8,128)(2,1)S(1)}, bf16[48,2048]{1,0:T(8,128)(2,1)S(1)}, bf16[48,2048]{1,0:T(8,128)(2,1)S(1)}, bf16[48,2048]{1,0:T(8,128)(2,1)S(1)}) custom-call(s32[2]{0:T(128)S(1)} %pad_add_fusion.1.ids, bf16[192,144]{1,0:T(8,128)(2,1)S(1)} %bitcast.75, bf16[2,144,1024]{2,1,0:T(8,128)(2,1)S(1)} %collective-permute-done.25.mine, ...), custom_call_target="tpu_custom_call" | custom-call | bytes 40000000 | tf_op jit(solution)/shard_map/pallas_call | solution.py:310
  150.5 2.9 %collective-permute-start.28 = (bf16[48,2048]{1,0:T(8,128)(2,1)S(1)}, bf16[48,2048]{1,0:T(8,128)(2,1)S(1)}, u32[]{:S(2)}, u32[]{:S(2)}) collective-permute-start(bf16[48,2048]{1,0:T(8,128)(2,1)S(1)} %get-tuple-element.113), channel_id=1, source_target_pairs={{0,12},{4,0},{8,4},{12,8},{1,13},{5,1},{9,5},{13,9},{2,14},{6,2},{... | collective-permute-start | bytes 589832 | tf_op jit(solution)/shard_map/ppermute | solution.py:452
  153.5 13.9 %collective-permute-done.29 = bf16[48,2048]{1,0:T(8,128)(2,1)S(1)} collective-permute-done((bf16[48,2048]{1,0:T(8,128)(2,1)S(1)}, bf16[48,2048]{1,0:T(8,128)(2,1)S(1)}, u32[]{:S(2)}, u32[]{:S(2)}) %collective-permute-start.29) | collective-permute-done | bytes 196640 | tf_op jit(solution)/shard_map/ppermute | solution.py:452
  (88 shorter events, 20.7 us)
Async XLA Ops:
  0.0 43.1 %collective-permute-start.3 = (bf16[96,2048]{1,0:T(8,128)(2,1)}, bf16[96,2048]{1,0:T(8,128)(2,1)S(1)}, u32[]{:S(2)}, u32[]{:S(2)}) collective-permute-start(bf16[96,2048]{1,0:T(8,128)(2,1)} %param.13), channel_id=1, source_target_pairs={{0,0},{1,4},{2,8},{3,12},{4,1},{5,5},{6,9},{7,13},{8,2},{9,6},{10,... | collective-permute-start | bytes 1179656 | tf_op jit(solution)/shard_map/ppermute | solution.py:346
  1.6 41.5 %collective-permute-start.4 = (bf16[96,2048]{1,0:T(8,128)(2,1)}, bf16[96,2048]{1,0:T(8,128)(2,1)S(1)}, u32[]{:S(2)}, u32[]{:S(2)}) collective-permute-start(bf16[96,2048]{1,0:T(8,128)(2,1)} %param.13), channel_id=1, source_target_pairs={{0,4},{1,8},{2,12},{3,0},{4,5},{5,9},{6,13},{7,1},{8,6},{9,10},{10... | collective-permute-start | bytes 1179656 | tf_op jit(solution)/shard_map/ppermute | solution.py:346
  5.0 38.1 %collective-permute-start.5 = (bf16[96,2048]{1,0:T(8,128)(2,1)}, bf16[96,2048]{1,0:T(8,128)(2,1)S(1)}, u32[]{:S(2)}, u32[]{:S(2)}) collective-permute-start(bf16[96,2048]{1,0:T(8,128)(2,1)} %param.13), channel_id=1, source_target_pairs={{0,8},{1,12},{2,0},{3,4},{4,9},{5,13},{6,1},{7,5},{8,10},{9,14},{1... | collective-permute-start | bytes 1179656 | tf_op jit(solution)/shard_map/ppermute | solution.py:346
  8.4 34.8 %collective-permute-start.6 = (bf16[96,2048]{1,0:T(8,128)(2,1)}, bf16[96,2048]{1,0:T(8,128)(2,1)S(1)}, u32[]{:S(2)}, u32[]{:S(2)}) collective-permute-start(bf16[96,2048]{1,0:T(8,128)(2,1)} %param.13), channel_id=1, source_target_pairs={{0,12},{1,0},{2,4},{3,8},{4,13},{5,1},{6,5},{7,9},{8,14},{9,2},{10... | collective-permute-start | bytes 1179656 | tf_op jit(solution)/shard_map/ppermute | solution.py:346
  11.0 28.1 %collective-permute-start.7 = (bf16[96,2048]{1,0:T(8,128)(2,1)}, bf16[96,2048]{1,0:T(8,128)(2,1)S(1)}, u32[]{:S(2)}, u32[]{:S(2)}) collective-permute-start(bf16[96,2048]{1,0:T(8,128)(2,1)} %param.14), channel_id=1, source_target_pairs={{0,2},{1,3},{2,0},{3,1},{4,6},{5,7},{6,4},{7,5},{8,10},{9,11},{10,... | collective-permute-start | bytes 1179656 | tf_op jit(solution)/shard_map/ppermute | solution.py:403
  39.2 3.5 %copy-start = (bf16[96,2048]{1,0:T(8,128)(2,1)S(1)}, bf16[96,2048]{1,0:T(8,128)(2,1)}, u32[]{:S(2)}) copy-start(bf16[96,2048]{1,0:T(8,128)(2,1)} %get-tuple-element.49) | copy-start | bytes 1179652 | tf_op jit(solution)/shard_map/cond
  40.3 2.4 %collective-permute-start.2 = (bf16[192,2048]{1,0:T(8,128)(2,1)S(1)}, bf16[192,2048]{1,0:T(8,128)(2,1)S(1)}, u32[]{:S(2)}, u32[]{:S(2)}) collective-permute-start(bf16[192,2048]{1,0:T(8,128)(2,1)S(1)} %pad_maximum_fusion), channel_id=1, source_target_pairs={{0,1},{1,0},{2,3},{3,2},{4,5},{5,4},{6,7},{7,6},{8,9},{9,8},{10,11... | collective-permute-start | bytes 2359304 | tf_op jit(solution)/shard_map/cond/branch_1_fun/ppermute | solution.py:397
  43.1 31.1 %collective-permute-start.8 = (bf16[72,2048]{1,0:T(8,128)(2,1)S(1)}, bf16[72,2048]{1,0:T(8,128)(2,1)S(1)}, u32[]{:S(2)}, u32[]{:S(2)}) collective-permute-start(bf16[72,2048]{1,0:T(8,128)(2,1)S(1)} %get-tuple-element.139), channel_id=1, source_target_pairs={{0,0},{1,4},{2,8},{3,12},{4,1},{5,5},{6,9},{7,13},{8,2},{9,6},{10,... | collective-permute-start | bytes 884744 | tf_op jit(solution)/shard_map/ppermute | solution.py:346
  43.8 30.4 %collective-permute-start.9 = (bf16[72,2048]{1,0:T(8,128)(2,1)S(1)}, bf16[72,2048]{1,0:T(8,128)(2,1)S(1)}, u32[]{:S(2)}, u32[]{:S(2)}) collective-permute-start(bf16[72,2048]{1,0:T(8,128)(2,1)S(1)} %get-tuple-element.139), channel_id=1, source_target_pairs={{0,4},{1,8},{2,12},{3,0},{4,5},{5,9},{6,13},{7,1},{8,6},{9,10},{10... | collective-permute-start | bytes 884744 | tf_op jit(solution)/shard_map/ppermute | solution.py:346
  46.9 27.4 %collective-permute-start.10 = (bf16[72,2048]{1,0:T(8,128)(2,1)S(1)}, bf16[72,2048]{1,0:T(8,128)(2,1)S(1)}, u32[]{:S(2)}, u32[]{:S(2)}) collective-permute-start(bf16[72,2048]{1,0:T(8,128)(2,1)S(1)} %get-tuple-element.139), channel_id=1, source_target_pairs={{0,8},{1,12},{2,0},{3,4},{4,9},{5,13},{6,1},{7,5},{8,10},{9,14},{1... | collective-permute-start | bytes 884744 | tf_op jit(solution)/shard_map/ppermute | solution.py:346
  48.8 25.5 %collective-permute-start.11 = (bf16[72,2048]{1,0:T(8,128)(2,1)S(1)}, bf16[72,2048]{1,0:T(8,128)(2,1)S(1)}, u32[]{:S(2)}, u32[]{:S(2)}) collective-permute-start(bf16[72,2048]{1,0:T(8,128)(2,1)S(1)} %get-tuple-element.139), channel_id=1, source_target_pairs={{0,12},{1,0},{2,4},{3,8},{4,13},{5,1},{6,5},{7,9},{8,14},{9,2},{10... | collective-permute-start | bytes 884744 | tf_op jit(solution)/shard_map/ppermute | solution.py:346
  60.1 2.9 %collective-permute-start.1 = (bf16[2,288,1024]{2,1,0:T(8,128)(2,1)S(1)}, bf16[2,288,1024]{2,1,0:T(8,128)(2,1)S(1)}, u32[]{:S(2)}, u32[]{:S(2)}) collective-permute-start(bf16[2,288,1024]{2,1,0:T(8,128)(2,1)S(1)} %get-tuple-element.47), channel_id=1, source_target_pairs={{0,1},{1,0},{2,3},{3,2},{4,5},{5,4},{6,7},{7,6},{8,9},{9,8},{10,11... | collective-permute-start | bytes 3538952 | tf_op jit(solution)/shard_map/cond/branch_1_fun/ppermute | solution.py:409
  64.5 31.0 %collective-permute-start.16 = (bf16[2,288,1024]{2,1,0:T(8,128)(2,1)}, bf16[2,288,1024]{2,1,0:T(8,128)(2,1)}, u32[]{:S(2)}, u32[]{:S(2)}) collective-permute-start(bf16[2,288,1024]{2,1,0:T(8,128)(2,1)} %get-tuple-element.101), channel_id=1, source_target_pairs={{0,2},{1,3},{2,0},{3,1},{4,6},{5,7},{6,4},{7,5},{8,10},{9,11},{10,... | collective-permute-start | bytes 3538952 | tf_op jit(solution)/shard_map/ppermute | solution.py:416
  81.4 14.1 %collective-permute-start.15 = (bf16[2,288,1024]{2,1,0:T(8,128)(2,1)}, bf16[2,288,1024]{2,1,0:T(8,128)(2,1)}, u32[]{:S(2)}, u32[]{:S(2)}) collective-permute-start(bf16[2,288,1024]{2,1,0:T(8,128)(2,1)} %get-tuple-element.100), channel_id=1, source_target_pairs={{0,1},{1,0},{2,3},{3,2},{4,5},{5,4},{6,7},{7,6},{8,9},{9,8},{10,11... | collective-permute-start | bytes 3538952 | tf_op jit(solution)/shard_map/ppermute | solution.py:420
  81.5 2.9 %collective-permute-start.12 = (bf16[144,1024]{1,0:T(8,128)(2,1)S(1)}, bf16[144,1024]{1,0:T(8,128)(2,1)S(1)}, u32[]{:S(2)}, u32[]{:S(2)}) collective-permute-start(bf16[144,1024]{1,0:T(8,128)(2,1)S(1)} %get-tuple-element.92), channel_id=1, source_target_pairs={{0,1},{1,0},{2,3},{3,2},{4,5},{5,4},{6,7},{7,6},{8,9},{9,8},{10,11... | collective-permute-start | bytes 884744 | tf_op jit(solution)/shard_map/ppermute | solution.py:423
  82.0 4.0 %collective-permute-start.13 = (bf16[144,1024]{1,0:T(8,128)(2,1)S(1)}, bf16[144,1024]{1,0:T(8,128)(2,1)S(1)}, u32[]{:S(2)}, u32[]{:S(2)}) collective-permute-start(bf16[144,1024]{1,0:T(8,128)(2,1)S(1)} %get-tuple-element.94), channel_id=1, source_target_pairs={{0,1},{1,0},{2,3},{3,2},{4,5},{5,4},{6,7},{7,6},{8,9},{9,8},{10,11... | collective-permute-start | bytes 884744 | tf_op jit(solution)/shard_map/ppermute | solution.py:423
  84.5 16.7 %collective-permute-start.14 = (bf16[144,1024]{1,0:T(8,128)(2,1)S(1)}, bf16[144,1024]{1,0:T(8,128)(2,1)S(1)}, u32[]{:S(2)}, u32[]{:S(2)}) collective-permute-start(bf16[144,1024]{1,0:T(8,128)(2,1)S(1)} %add_convert_fusion.2), channel_id=1, source_target_pairs={{0,2},{1,3},{2,0},{3,1},{4,6},{5,7},{6,4},{7,5},{8,10},{9,11},{10,... | collective-permute-start | bytes 884744 | tf_op jit(solution)/shard_map/ppermute | solution.py:437
  86.1 21.5 %collective-permute-start.19 = (bf16[144,1024]{1,0:T(8,128)(2,1)S(1)}, bf16[144,1024]{1,0:T(8,128)(2,1)S(1)}, u32[]{:S(2)}, u32[]{:S(2)}) collective-permute-start(bf16[144,1024]{1,0:T(8,128)(2,1)S(1)} %add_convert_fusion.1), channel_id=1, source_target_pairs={{0,2},{1,3},{2,0},{3,1},{4,6},{5,7},{6,4},{7,5},{8,10},{9,11},{10,... | collective-permute-start | bytes 884744 | tf_op jit(solution)/shard_map/ppermute | solution.py:437
  93.0 2.1 %collective-permute-start = (bf16[288,1024]{1,0:T(8,128)(2,1)S(1)}, bf16[288,1024]{1,0:T(8,128)(2,1)S(1)}, u32[]{:S(2)}, u32[]{:S(2)}) collective-permute-start(bf16[288,1024]{1,0:T(8,128)(2,1)S(1)} %get-tuple-element.56), channel_id=1, source_target_pairs={{0,1},{1,0},{2,3},{3,2},{4,5},{5,4},{6,7},{7,6},{8,9},{9,8},{10,11... | collective-permute-start | bytes 1769480 | tf_op jit(solution)/shard_map/cond/branch_1_fun/ppermute | solution.py:428
  101.6 18.6 %collective-permute-start.17 = (bf16[2,144,1024]{2,1,0:T(8,128)(2,1)S(1)}, bf16[2,144,1024]{2,1,0:T(8,128)(2,1)S(1)}, u32[]{:S(2)}, u32[]{:S(2)}) collective-permute-start(bf16[2,144,1024]{2,1,0:T(8,128)(2,1)S(1)} %pad_maximum_fusion.1.mine_a), channel_id=1, source_target_pairs={{0,2},{1,3},{2,0},{3,1},{4,6},{5,7},{6,4},{7,5},{8,10},{9,11},{10,... | collective-permute-start | bytes 1769480 | tf_op jit(solution)/shard_map/ppermute | solution.py:443
  104.2 6.7 %collective-permute-start.18 = (bf16[2,144,1024]{2,1,0:T(8,128)(2,1)S(1)}, bf16[2,144,1024]{2,1,0:T(8,128)(2,1)S(1)}, u32[]{:S(2)}, u32[]{:S(2)}) collective-permute-start(bf16[2,144,1024]{2,1,0:T(8,128)(2,1)S(1)} %pad_maximum_fusion.1.mine_a), channel_id=1, source_target_pairs={{0,1},{1,0},{2,3},{3,2},{4,5},{5,4},{6,7},{7,6},{8,9},{9,8},{10,11... | collective-permute-start | bytes 1769480 | tf_op jit(solution)/shard_map/ppermute | solution.py:442
  108.0 2.9 %collective-permute-start.20 = (bf16[2,144,1024]{2,1,0:T(8,128)(2,1)S(1)}, bf16[2,144,1024]{2,1,0:T(8,128)(2,1)S(1)}, u32[]{:S(2)}, u32[]{:S(2)}) collective-permute-start(bf16[2,144,1024]{2,1,0:T(8,128)(2,1)S(1)} %pad_maximum_fusion.2.mine_b), channel_id=1, source_target_pairs={{0,1},{1,0},{2,3},{3,2},{4,5},{5,4},{6,7},{7,6},{8,9},{9,8},{10,11... | collective-permute-start | bytes 1769480 | tf_op jit(solution)/shard_map/ppermute | solution.py:442
  108.3 24.3 %collective-permute-start.25 = (bf16[2,144,1024]{2,1,0:T(8,128)(2,1)S(1)}, bf16[2,144,1024]{2,1,0:T(8,128)(2,1)S(1)}, u32[]{:S(2)}, u32[]{:S(2)}) collective-permute-start(bf16[2,144,1024]{2,1,0:T(8,128)(2,1)S(1)} %pad_maximum_fusion.2.mine_b), channel_id=1, source_target_pairs={{0,2},{1,3},{2,0},{3,1},{4,6},{5,7},{6,4},{7,5},{8,10},{9,11},{10,... | collective-permute-start | bytes 1769480 | tf_op jit(solution)/shard_map/ppermute | solution.py:443
  120.2 2.0 %collective-permute-start.21 = (bf16[2,144,1024]{2,1,0:T(8,128)(2,1)S(1)}, bf16[2,144,1024]{2,1,0:T(8,128)(2,1)S(1)}, u32[]{:S(2)}, u32[]{:S(2)}) collective-permute-start(bf16[2,144,1024]{2,1,0:T(8,128)(2,1)S(1)} %collective-permute-done.17.mine), channel_id=1, source_target_pairs={{0,1},{1,0},{2,3},{3,2},{4,5},{5,4},{6,7},{7,6},{8,9},{9,8},{10,11... | collective-permute-start | bytes 1769480 | tf_op jit(solution)/shard_map/ppermute | solution.py:447
  132.6 6.8 %collective-permute-start.26 = (bf16[2,144,1024]{2,1,0:T(8,128)(2,1)S(1)}, bf16[2,144,1024]{2,1,0:T(8,128)(2,1)S(1)}, u32[]{:S(2)}, u32[]{:S(2)}) collective-permute-start(bf16[2,144,1024]{2,1,0:T(8,128)(2,1)S(1)} %collective-permute-done.25.mine), channel_id=1, source_target_pairs={{0,1},{1,0},{2,3},{3,2},{4,5},{5,4},{6,7},{7,6},{8,9},{9,8},{10,11... | collective-permute-start | bytes 1769480 | tf_op jit(solution)/shard_map/ppermute | solution.py:447
  133.6 19.8 %collective-permute-start.24 = (bf16[48,2048]{1,0:T(8,128)(2,1)S(1)}, bf16[48,2048]{1,0:T(8,128)(2,1)S(1)}, u32[]{:S(2)}, u32[]{:S(2)}) collective-permute-start(bf16[48,2048]{1,0:T(8,128)(2,1)S(1)} %get-tuple-element.108), channel_id=1, source_target_pairs={{0,8},{4,12},{8,0},{12,4},{1,9},{5,13},{9,1},{13,5},{2,10},{6,14},... | collective-permute-start | bytes 589832 | tf_op jit(solution)/shard_map/ppermute | solution.py:452
  136.1 17.3 %collective-permute-start.23 = (bf16[48,2048]{1,0:T(8,128)(2,1)S(1)}, bf16[48,2048]{1,0:T(8,128)(2,1)S(1)}, u32[]{:S(2)}, u32[]{:S(2)}) collective-permute-start(bf16[48,2048]{1,0:T(8,128)(2,1)S(1)} %get-tuple-element.107), channel_id=1, source_target_pairs={{0,12},{4,0},{8,4},{12,8},{1,13},{5,1},{9,5},{13,9},{2,14},{6,2},{... | collective-permute-start | bytes 589832 | tf_op jit(solution)/shard_map/ppermute | solution.py:452
  137.0 16.5 %collective-permute-start.22 = (bf16[48,2048]{1,0:T(8,128)(2,1)S(1)}, bf16[48,2048]{1,0:T(8,128)(2,1)S(1)}, u32[]{:S(2)}, u32[]{:S(2)}) collective-permute-start(bf16[48,2048]{1,0:T(8,128)(2,1)S(1)} %get-tuple-element.106), channel_id=1, source_target_pairs={{0,4},{4,8},{8,12},{12,0},{1,5},{5,9},{9,13},{13,1},{2,6},{6,10},{... | collective-permute-start | bytes 589832 | tf_op jit(solution)/shard_map/ppermute | solution.py:452
  149.9 17.6 %collective-permute-start.29 = (bf16[48,2048]{1,0:T(8,128)(2,1)S(1)}, bf16[48,2048]{1,0:T(8,128)(2,1)S(1)}, u32[]{:S(2)}, u32[]{:S(2)}) collective-permute-start(bf16[48,2048]{1,0:T(8,128)(2,1)S(1)} %get-tuple-element.114), channel_id=1, source_target_pairs={{0,8},{4,12},{8,0},{12,4},{1,9},{5,13},{9,1},{13,5},{2,10},{6,14},... | collective-permute-start | bytes 589832 | tf_op jit(solution)/shard_map/ppermute | solution.py:452
  150.5 17.0 %collective-permute-start.28 = (bf16[48,2048]{1,0:T(8,128)(2,1)S(1)}, bf16[48,2048]{1,0:T(8,128)(2,1)S(1)}, u32[]{:S(2)}, u32[]{:S(2)}) collective-permute-start(bf16[48,2048]{1,0:T(8,128)(2,1)S(1)} %get-tuple-element.113), channel_id=1, source_target_pairs={{0,12},{4,0},{8,4},{12,8},{1,13},{5,1},{9,5},{13,9},{2,14},{6,2},{... | collective-permute-start | bytes 589832 | tf_op jit(solution)/shard_map/ppermute | solution.py:452
  153.4 14.1 %collective-permute-start.27 = (bf16[48,2048]{1,0:T(8,128)(2,1)S(1)}, bf16[48,2048]{1,0:T(8,128)(2,1)S(1)}, u32[]{:S(2)}, u32[]{:S(2)}) collective-permute-start(bf16[48,2048]{1,0:T(8,128)(2,1)S(1)} %get-tuple-element.112), channel_id=1, source_target_pairs={{0,4},{4,8},{8,12},{12,0},{1,5},{5,9},{9,13},{13,1},{2,6},{6,10},{... | collective-permute-start | bytes 589832 | tf_op jit(solution)/shard_map/ppermute | solution.py:452

commit v6 on v5

--- a/solution.py
+++ b/solution.py
@@ -441,6 +441,7 @@
         ds.append(jnp.stack(derive(near[0, part], near[1, part], hidden[part] + got.astype(F32))))
         ds_core.append(lax.ppermute(ds[m], "seq", sibling))
         ds_far.append(lax.ppermute(ds[m], "seq", across))
+    ids, final = lax.optimization_barrier((ids, final))
     firsts = near_back(ids, ds, ds_core, gate_weight, up_weight)
     pieces, parts = [], firsts
     for m in range(sets):

time: 171 us -> 171 us (level)
    ppermute x2, waiting for transfers between devices: 6.72 us -> 4.47 us  [tuned(): got = lax.ppermute(pairs[m], 'seq', across)]
  transfers between devices with their start and end apart: 30 -> 30, of which waited for: 9 -> 8; matrix products, arithmetic and copies ran while one was open for 10% -> 10% of each run, Pallas kernels for 37% -> 37%
where the time goes in v6:
time: 171 us; the launch traced here: 169 us
  Pallas kernels  62.5 us (37%)
  starting transfers between devices  35.3 us (21%)
  waiting for transfers between devices  30.7 us (18%)
  blocking collectives  20.8 us (12%)
  other arithmetic  10.2 us (6%)
  matrix products  4.93 us (3%)
  local copies, waits for them, and re-layouts  3.35 us (2%)
    pallas_call x2, Pallas kernels, far_back(): call(far_kernel, [IN_SMEM, IN_VMEM] + [IN_HBM] * 5, [((count // 4, depth)...  20.8 us
    unnamed x1, blocking collectives  20.8 us
    pallas_call x2, Pallas kernels, project(): call(functools.partial(project_kernel, near), [IN_SMEM] + [IN_HBM if near...  19 us
    ppermute x8, starting transfers between devices, spread(): return lax.ppermute(value, ('tensor', 'seq'), pairs)  18.2 us
    ppermute x6, waiting for transfers between devices, tuned(): total += lax.ppermute(parts[k], 'tensor', shift).astype(F32)  15.5 us
    pallas_call x2, Pallas kernels, hidden_grads(): call(functools.partial(hidden_kernel, near), [IN_SMEM] + [IN_HBM if near...  13.7 us
    pallas_call x1, Pallas kernels, near_back(): call(near_kernel, [IN_SMEM] + [IN_HBM] * 6, [((rows, depth), F32)] * 2, [...  8.99 us
    ppermute x6, starting transfers between devices, tuned(): total += lax.ppermute(parts[k], 'tensor', shift).astype(F32)  7.59 us
  transfers between devices with their start and end apart: 30, of which 8 were waited for; matrix products, arithmetic and copies ran while one was open for 10% of the time, Pallas kernels for 37%

profile of v6, /device:TPU:0, one launch (start us, length us, event | category | flops | bytes accessed | tf_op | source)
XLA Modules:
  0.0 169.1 jit_solution(13884308383961776379)
XLA Ops:
  0.0 1.8 %collective-permute-start.3 = (bf16[96,2048]{1,0:T(8,128)(2,1)}, bf16[96,2048]{1,0:T(8,128)(2,1)S(1)}, u32[]{:S(2)}, u32[]{:S(2)}) collective-permute-start(bf16[96,2048]{1,0:T(8,128)(2,1)} %param.13), channel_id=1, source_target_pairs={{0,0},{1,4},{2,8},{3,12},{4,1},{5,5},{6,9},{7,13},{8,2},{9,6},{10,... | collective-permute-start | bytes 1179656 | tf_op jit(solution)/shard_map/ppermute | solution.py:346
  1.8 3.4 %collective-permute-start.4 = (bf16[96,2048]{1,0:T(8,128)(2,1)}, bf16[96,2048]{1,0:T(8,128)(2,1)S(1)}, u32[]{:S(2)}, u32[]{:S(2)}) collective-permute-start(bf16[96,2048]{1,0:T(8,128)(2,1)} %param.13), channel_id=1, source_target_pairs={{0,4},{1,8},{2,12},{3,0},{4,5},{5,9},{6,13},{7,1},{8,6},{9,10},{10... | collective-permute-start | bytes 1179656 | tf_op jit(solution)/shard_map/ppermute | solution.py:346
  5.1 3.4 %collective-permute-start.5 = (bf16[96,2048]{1,0:T(8,128)(2,1)}, bf16[96,2048]{1,0:T(8,128)(2,1)}, u32[]{:S(2)}, u32[]{:S(2)}) collective-permute-start(bf16[96,2048]{1,0:T(8,128)(2,1)} %param.13), channel_id=1, source_target_pairs={{0,8},{1,12},{2,0},{3,4},{4,9},{5,13},{6,1},{7,5},{8,10},{9,14},{1... | collective-permute-start | bytes 1179656 | tf_op jit(solution)/shard_map/ppermute | solution.py:346
  8.5 2.6 %collective-permute-start.6 = (bf16[96,2048]{1,0:T(8,128)(2,1)}, bf16[96,2048]{1,0:T(8,128)(2,1)S(1)}, u32[]{:S(2)}, u32[]{:S(2)}) collective-permute-start(bf16[96,2048]{1,0:T(8,128)(2,1)} %param.13), channel_id=1, source_target_pairs={{0,12},{1,0},{2,4},{3,8},{4,13},{5,1},{6,5},{7,9},{8,14},{9,2},{10... | collective-permute-start | bytes 1179656 | tf_op jit(solution)/shard_map/ppermute | solution.py:346
  13.8 20.8 %all-reduce = s32[4]{0:T(128)S(1)} all-reduce(s32[4]{0:T(128)S(1)} %dynamic-update-slice), channel_id=1, replica_groups=mesh['group'=2,'tensor'=4,'seq'=4] {'seq'}, use_global_device_ids=true, to_apply=%add | all-reduce | flops 4 | bytes 32
  36.4 1.8 %convolution_convert_fusion.2 = bf16[288,384]{1,0:T(8,128)(2,1)} fusion(s32[384]{0:T(512)S(1)} %fusion.46, s32[384]{0:T(512)} %param.16, s32[384]{0:T(512)S(1)} %get-tuple-element.127), kind=kOutput, calls=%fused_computation.12 | convolution fusion | flops 85303296 | bytes 225792 | tf_op jit(solution)/shard_map/dot_general | solution.py:361
  39.3 3.6 %conditional.4 = (bf16[72,2048]{1,0:T(8,128)(2,1)}) conditional(s32[]{:T(128)} %convert_element_type.137, () %tuple.45, (bf16[96,2048]{1,0:T(8,128)(2,1)S(1)}, bf16[96,2048]{1,0:T(8,128)(2,1)S(1)}, bf16[72,384]{1,0:T(8,128)(2,1)S(1)}) %tuple.70), branch_computations={%region_7.8_spmd, %region_8.9_spmd} | conditional | flops 119685120 | bytes 6641712 | solution.py:403
  39.5 2.3 %collective-permute-done.2 = bf16[192,2048]{1,0:T(8,128)(2,1)S(1)} collective-permute-done((bf16[192,2048]{1,0:T(8,128)(2,1)S(1)}, bf16[192,2048]{1,0:T(8,128)(2,1)S(1)}, u32[]{:S(2)}, u32[]{:S(2)}) %collective-permute-start.2) | collective-permute-done | bytes 786464 | tf_op jit(solution)/shard_map/cond/branch_1_fun/ppermute | solution.py:397
  42.9 1.6 collective-permute-start.8
  44.6 2.1 %collective-permute-start.9 = (bf16[72,2048]{1,0:T(8,128)(2,1)}, bf16[72,2048]{1,0:T(8,128)(2,1)S(1)}, u32[]{:S(2)}, u32[]{:S(2)}) collective-permute-start(bf16[72,2048]{1,0:T(8,128)(2,1)} %get-tuple-element.143), channel_id=1, source_target_pairs={{0,4},{1,8},{2,12},{3,0},{4,5},{5,9},{6,13},{7,1},{8,6},{9,10},{10... | collective-permute-start | bytes 884744 | tf_op jit(solution)/shard_map/ppermute | solution.py:346
  46.7 2.2 %collective-permute-start.10 = (bf16[72,2048]{1,0:T(8,128)(2,1)}, bf16[72,2048]{1,0:T(8,128)(2,1)S(1)}, u32[]{:S(2)}, u32[]{:S(2)}) collective-permute-start(bf16[72,2048]{1,0:T(8,128)(2,1)} %get-tuple-element.143), channel_id=1, source_target_pairs={{0,8},{1,12},{2,0},{3,4},{4,9},{5,13},{6,1},{7,5},{8,10},{9,14},{1... | collective-permute-start | bytes 884744 | tf_op jit(solution)/shard_map/ppermute | solution.py:346
  50.2 15.1 %conditional.3 = (bf16[2,288,1024]{2,1,0:T(8,128)(2,1)}, bf16[288,2048]{1,0:T(8,128)(2,1)S(1)}) conditional(s32[]{:T(128)} %convert_element_type.137, () %tuple.42, (s32[2]{0:T(128)S(1)}, bf16[288,384]{1,0:T(8,128)(2,1)}, bf16[96,2048]{1,0:T(8,128)(2,1)S(1)}, bf16[96,2048]{1,0:T(8,128)(2,1)S(1)}, bf16[96,2048]{1,0:T(8,128)(2,1)}, ...), branch_computations={%region_5.6_spmd, %region_6.7_spmd} | conditional | flops 2359296 | bytes 29830484 | solution.py:415
  50.9 10.0 %branch_1_fun.2 = (bf16[2,288,1024]{2,1,0:T(8,128)(2,1)S(1)}, bf16[2,288,1024]{2,1,0:T(8,128)(2,1)S(1)}, bf16[288,2048]{1,0:T(8,128)(2,1)S(1)}) custom-call(s32[2]{0:T(128)S(1)} %get-tuple-element.38.ids, bf16[288,384]{1,0:T(8,128)(2,1)} %get-tuple-element.39.refs_0_, bf16[96,2048]{1,0:T(8,128)(2,1)S(1)} %get-tuple-element.40.refs_1_, ...), custom_call_target="tpu_custom_call" | custom-call | bytes 20000000 | tf_op jit(solution)/shard_map/cond/branch_1_fun/pallas_call | solution.py:154
  61.1 2.7 %collective-permute-done.1 = bf16[2,288,1024]{2,1,0:T(8,128)(2,1)S(1)} collective-permute-done((bf16[2,288,1024]{2,1,0:T(8,128)(2,1)S(1)}, bf16[2,288,1024]{2,1,0:T(8,128)(2,1)S(1)}, u32[]{:S(2)}, u32[]{:S(2)}) %collective-permute-start.1) | collective-permute-done | bytes 1179680 | tf_op jit(solution)/shard_map/cond/branch_1_fun/ppermute | solution.py:409
  66.0 9.1 %shard_map.73 = (bf16[2,288,1024]{2,1,0:T(8,128)(2,1)}, bf16[2,288,1024]{2,1,0:T(8,128)(2,1)S(1)}) custom-call(s32[2]{0:T(128)S(1)} %pad_add_fusion.1.ids, bf16[288,2048]{1,0:T(8,128)(2,1)S(1)} %get-tuple-element.90.refs_0_, bf16[2048,4096]{1,0:T(8,128)(2,1)} %gate_w.5, bf16[2048,4096]{1,0:T(8,128)(2,1)} %up_w.5), custom_call_target="tpu_custom_call" | custom-call | bytes 20000000 | tf_op jit(solution)/shard_map/pallas_call | solution.py:154
  75.1 7.5 %shard_map.74 = (bf16[144,1024]{1,0:T(8,128)(2,1)}, bf16[144,1024]{1,0:T(8,128)(2,1)S(1)}, bf16[144,1024]{1,0:T(8,128)(2,1)S(1)}, bf16[144,1024]{1,0:T(8,128)(2,1)S(1)}, bf16[288,2048]{1,0:T(8,128)(2,1)}) custom-call(s32[2]{0:T(128)S(1)} %pad_add_fusion.1.ids, bf16[4,288,72]{2,1,0:T(8,128)(2,1)S(1)} %fusion.15.refs_0_, ...), custom_call_target="tpu_custom_call" | custom-call | bytes 60000000 | tf_op jit(solution)/shard_map/pallas_call | solution.py:204
  84.3 2.3 %collective-permute-done.12 = bf16[144,1024]{1,0:T(8,128)(2,1)S(1)} collective-permute-done((bf16[144,1024]{1,0:T(8,128)(2,1)}, bf16[144,1024]{1,0:T(8,128)(2,1)S(1)}, u32[]{:S(2)}, u32[]{:S(2)}) %collective-permute-start.12) | collective-permute-done | bytes 294944 | tf_op jit(solution)/shard_map/ppermute | solution.py:423
  89.6 8.6 %conditional.5 = (f32[288,1024]{1,0:T(8,128)S(1)}, f32[288,1024]{1,0:T(8,128)S(1)}) conditional(s32[]{:T(128)} %convert_element_type.137, () %tuple.41, (s32[2]{0:T(128)S(1)}, bf16[288,2048]{1,0:T(8,128)(2,1)S(1)}, bf16[4096,2048]{1,0:T(8,128)(2,1)}) %tuple.69), branch_computations={%region_9.10_spmd, %region_10.11_spmd} | conditional | flops 589824 | bytes 65898296 | solution.py:433
  89.6 6.2 %branch_1_fun.3 = (bf16[288,1024]{1,0:T(8,128)(2,1)S(1)}, bf16[288,1024]{1,0:T(8,128)(2,1)S(1)}) custom-call(s32[2]{0:T(128)S(1)} %get-tuple-element.52.ids, bf16[288,2048]{1,0:T(8,128)(2,1)S(1)} %get-tuple-element.53.refs_0_, bf16[4096,2048]{1,0:T(8,128)(2,1)} %get-tuple-element.54.refs_1_), custom_call_target="tpu_custom_call" | custom-call | bytes 60000000 | tf_op jit(solution)/shard_map/cond/branch_1_fun/pallas_call | solution.py:204
  96.0 1.9 %collective-permute-done = bf16[288,1024]{1,0:T(8,128)(2,1)S(1)} collective-permute-done((bf16[288,1024]{1,0:T(8,128)(2,1)S(1)}, bf16[288,1024]{1,0:T(8,128)(2,1)S(1)}, u32[]{:S(2)}, u32[]{:S(2)}) %collective-permute-start) | collective-permute-done | bytes 589856 | tf_op jit(solution)/shard_map/cond/branch_1_fun/ppermute | solution.py:428
  98.4 2.3 %convert_add_fusion = f32[2,288,1024]{2,1,0:T(8,128)S(1)} fusion(bf16[2,288,1024]{2,1,0:T(8,128)(2,1)} %collective-permute-done.16, bf16[2,288,1024]{2,1,0:T(8,128)(2,1)} %collective-permute-done.15, bf16[2,288,1024]{2,1,0:T(8,128)(2,1)S(1)} %get-tuple-element.103), kind=kLoop, calls=%fused_computation.10 | loop fusion | flops 2949120 | bytes 5898240 | tf_op jit(solution)/shard_map/add | solution.py:420
  102.2 2.4 %collective-permute-start.17 = (bf16[2,144,1024]{2,1,0:T(8,128)(2,1)S(1)}, bf16[2,144,1024]{2,1,0:T(8,128)(2,1)S(1)}, u32[]{:S(2)}, u32[]{:S(2)}) collective-permute-start(bf16[2,144,1024]{2,1,0:T(8,128)(2,1)S(1)} %pad_maximum_fusion.1.mine_a), channel_id=1, source_target_pairs={{0,2},{1,3},{2,0},{3,1},{4,6},{5,7},{6,4},{7,5},{8,10},{9,11},{10,... | collective-permute-start | bytes 1769480 | tf_op jit(solution)/shard_map/ppermute | solution.py:443
  104.7 3.4 %collective-permute-done.19 = bf16[144,1024]{1,0:T(8,128)(2,1)S(1)} collective-permute-done((bf16[144,1024]{1,0:T(8,128)(2,1)S(1)}, bf16[144,1024]{1,0:T(8,128)(2,1)S(1)}, u32[]{:S(2)}, u32[]{:S(2)}) %collective-permute-start.19) | collective-permute-done | bytes 294944 | tf_op jit(solution)/shard_map/ppermute | solution.py:437
  110.1 2.5 %collective-permute-start.25 = (bf16[2,144,1024]{2,1,0:T(8,128)(2,1)S(1)}, bf16[2,144,1024]{2,1,0:T(8,128)(2,1)S(1)}, u32[]{:S(2)}, u32[]{:S(2)}) collective-permute-start(bf16[2,144,1024]{2,1,0:T(8,128)(2,1)S(1)} %pad_maximum_fusion.2.mine_b), channel_id=1, source_target_pairs={{0,2},{1,3},{2,0},{3,1},{4,6},{5,7},{6,4},{7,5},{8,10},{9,11},{10,... | collective-permute-start | bytes 1769480 | tf_op jit(solution)/shard_map/ppermute | solution.py:443
  112.6 9.0 %shard_map.75 = (f32[144,2048]{1,0:T(8,128)S(1)}, f32[144,2048]{1,0:T(8,128)S(1)}) custom-call(s32[2]{0:T(128)S(1)} %pad_add_fusion.1.ids, bf16[2,144,1024]{2,1,0:T(8,128)(2,1)S(1)} %pad_maximum_fusion.1.mine_a, bf16[2,144,1024]{2,1,0:T(8,128)(2,1)S(1)} %collective-permute-done.18.other_a, bf16[2,144,1024]{2,1,0:T(8,128)(2,1)S(1)} %pad_maximum_fusion.2.mine_b, ...), custom_call_target="tpu_custom_call" | custom-call | bytes 40000000 | tf_op jit(solution)/shard_map/pallas_call | solution.py:291
  122.1 1.6 collective-permute-done.21.other
  123.7 10.4 %shard_map.76 = (bf16[48,2048]{1,0:T(8,128)(2,1)S(1)}, bf16[48,2048]{1,0:T(8,128)(2,1)S(1)}, bf16[48,2048]{1,0:T(8,128)(2,1)S(1)}, bf16[48,2048]{1,0:T(8,128)(2,1)S(1)}) custom-call(s32[2]{0:T(128)S(1)} %pad_add_fusion.1.ids, bf16[192,144]{1,0:T(8,128)(2,1)S(1)} %bitcast.77, bf16[2,144,1024]{2,1,0:T(8,128)(2,1)S(1)} %collective-permute-done.17.mine, ...), custom_call_target="tpu_custom_call" | custom-call | bytes 40000000 | tf_op jit(solution)/shard_map/pallas_call | solution.py:310
  135.6 1.9 %collective-permute-start.23 = (bf16[48,2048]{1,0:T(8,128)(2,1)S(1)}, bf16[48,2048]{1,0:T(8,128)(2,1)S(1)}, u32[]{:S(2)}, u32[]{:S(2)}) collective-permute-start(bf16[48,2048]{1,0:T(8,128)(2,1)S(1)} %get-tuple-element.111), channel_id=1, source_target_pairs={{0,12},{4,0},{8,4},{12,8},{1,13},{5,1},{9,5},{13,9},{2,14},{6,2},{... | collective-permute-start | bytes 589832 | tf_op jit(solution)/shard_map/ppermute | solution.py:453
  137.7 10.4 %shard_map.77 = (bf16[48,2048]{1,0:T(8,128)(2,1)S(1)}, bf16[48,2048]{1,0:T(8,128)(2,1)S(1)}, bf16[48,2048]{1,0:T(8,128)(2,1)S(1)}, bf16[48,2048]{1,0:T(8,128)(2,1)S(1)}) custom-call(s32[2]{0:T(128)S(1)} %pad_add_fusion.1.ids, bf16[192,144]{1,0:T(8,128)(2,1)S(1)} %bitcast.76, bf16[2,144,1024]{2,1,0:T(8,128)(2,1)S(1)} %collective-permute-done.25.mine, ...), custom_call_target="tpu_custom_call" | custom-call | bytes 40000000 | tf_op jit(solution)/shard_map/pallas_call | solution.py:310
  148.1 1.7 %collective-permute-start.29 = (bf16[48,2048]{1,0:T(8,128)(2,1)S(1)}, bf16[48,2048]{1,0:T(8,128)(2,1)S(1)}, u32[]{:S(2)}, u32[]{:S(2)}) collective-permute-start(bf16[48,2048]{1,0:T(8,128)(2,1)S(1)} %get-tuple-element.118), channel_id=1, source_target_pairs={{0,8},{4,12},{8,0},{12,4},{1,9},{5,13},{9,1},{13,5},{2,10},{6,14},... | collective-permute-start | bytes 589832 | tf_op jit(solution)/shard_map/ppermute | solution.py:453
  149.8 2.1 %collective-permute-start.28 = (bf16[48,2048]{1,0:T(8,128)(2,1)S(1)}, bf16[48,2048]{1,0:T(8,128)(2,1)S(1)}, u32[]{:S(2)}, u32[]{:S(2)}) collective-permute-start(bf16[48,2048]{1,0:T(8,128)(2,1)S(1)} %get-tuple-element.117), channel_id=1, source_target_pairs={{0,12},{4,0},{8,4},{12,8},{1,13},{5,1},{9,5},{13,9},{2,14},{6,2},{... | collective-permute-start | bytes 589832 | tf_op jit(solution)/shard_map/ppermute | solution.py:453
  152.5 15.5 %collective-permute-done.29 = bf16[48,2048]{1,0:T(8,128)(2,1)S(1)} collective-permute-done((bf16[48,2048]{1,0:T(8,128)(2,1)S(1)}, bf16[48,2048]{1,0:T(8,128)(2,1)S(1)}, u32[]{:S(2)}, u32[]{:S(2)}) %collective-permute-start.29) | collective-permute-done | bytes 196640 | tf_op jit(solution)/shard_map/ppermute | solution.py:453
  (93 shorter events, 23.1 us)
Async XLA Ops:
  0.0 39.3 %copy-start.2 = (bf16[96,2048]{1,0:T(8,128)(2,1)S(1)}, bf16[96,2048]{1,0:T(8,128)(2,1)}, u32[]{:S(2)}) copy-start(bf16[96,2048]{1,0:T(8,128)(2,1)} %param.14) | copy-start | bytes 1179652
  0.0 42.9 %collective-permute-start.3 = (bf16[96,2048]{1,0:T(8,128)(2,1)}, bf16[96,2048]{1,0:T(8,128)(2,1)S(1)}, u32[]{:S(2)}, u32[]{:S(2)}) collective-permute-start(bf16[96,2048]{1,0:T(8,128)(2,1)} %param.13), channel_id=1, source_target_pairs={{0,0},{1,4},{2,8},{3,12},{4,1},{5,5},{6,9},{7,13},{8,2},{9,6},{10,... | collective-permute-start | bytes 1179656 | tf_op jit(solution)/shard_map/ppermute | solution.py:346
  1.8 41.2 %collective-permute-start.4 = (bf16[96,2048]{1,0:T(8,128)(2,1)}, bf16[96,2048]{1,0:T(8,128)(2,1)S(1)}, u32[]{:S(2)}, u32[]{:S(2)}) collective-permute-start(bf16[96,2048]{1,0:T(8,128)(2,1)} %param.13), channel_id=1, source_target_pairs={{0,4},{1,8},{2,12},{3,0},{4,5},{5,9},{6,13},{7,1},{8,6},{9,10},{10... | collective-permute-start | bytes 1179656 | tf_op jit(solution)/shard_map/ppermute | solution.py:346
  5.1 37.8 %collective-permute-start.5 = (bf16[96,2048]{1,0:T(8,128)(2,1)}, bf16[96,2048]{1,0:T(8,128)(2,1)}, u32[]{:S(2)}, u32[]{:S(2)}) collective-permute-start(bf16[96,2048]{1,0:T(8,128)(2,1)} %param.13), channel_id=1, source_target_pairs={{0,8},{1,12},{2,0},{3,4},{4,9},{5,13},{6,1},{7,5},{8,10},{9,14},{1... | collective-permute-start | bytes 1179656 | tf_op jit(solution)/shard_map/ppermute | solution.py:346
  8.5 34.4 %collective-permute-start.6 = (bf16[96,2048]{1,0:T(8,128)(2,1)}, bf16[96,2048]{1,0:T(8,128)(2,1)S(1)}, u32[]{:S(2)}, u32[]{:S(2)}) collective-permute-start(bf16[96,2048]{1,0:T(8,128)(2,1)} %param.13), channel_id=1, source_target_pairs={{0,12},{1,0},{2,4},{3,8},{4,13},{5,1},{6,5},{7,9},{8,14},{9,2},{10... | collective-permute-start | bytes 1179656 | tf_op jit(solution)/shard_map/ppermute | solution.py:346
  11.1 28.2 %collective-permute-start.7 = (bf16[96,2048]{1,0:T(8,128)(2,1)}, bf16[96,2048]{1,0:T(8,128)(2,1)S(1)}, u32[]{:S(2)}, u32[]{:S(2)}) collective-permute-start(bf16[96,2048]{1,0:T(8,128)(2,1)} %param.14), channel_id=1, source_target_pairs={{0,2},{1,3},{2,0},{3,1},{4,6},{5,7},{6,4},{7,5},{8,10},{9,11},{10,... | collective-permute-start | bytes 1179656 | tf_op jit(solution)/shard_map/ppermute | solution.py:403
  39.4 2.4 %collective-permute-start.2 = (bf16[192,2048]{1,0:T(8,128)(2,1)S(1)}, bf16[192,2048]{1,0:T(8,128)(2,1)S(1)}, u32[]{:S(2)}, u32[]{:S(2)}) collective-permute-start(bf16[192,2048]{1,0:T(8,128)(2,1)S(1)} %pad_maximum_fusion), channel_id=1, source_target_pairs={{0,1},{1,0},{2,3},{3,2},{4,5},{5,4},{6,7},{7,6},{8,9},{9,8},{10,11... | collective-permute-start | bytes 2359304 | tf_op jit(solution)/shard_map/cond/branch_1_fun/ppermute | solution.py:397
  42.9 32.2 %collective-permute-start.8 = (bf16[72,2048]{1,0:T(8,128)(2,1)}, bf16[72,2048]{1,0:T(8,128)(2,1)S(1)}, u32[]{:S(2)}, u32[]{:S(2)}) collective-permute-start(bf16[72,2048]{1,0:T(8,128)(2,1)} %get-tuple-element.143), channel_id=1, source_target_pairs={{0,0},{1,4},{2,8},{3,12},{4,1},{5,5},{6,9},{7,13},{8,2},{9,6},{10,... | collective-permute-start | bytes 884744 | tf_op jit(solution)/shard_map/ppermute | solution.py:346
  44.6 30.5 %collective-permute-start.9 = (bf16[72,2048]{1,0:T(8,128)(2,1)}, bf16[72,2048]{1,0:T(8,128)(2,1)S(1)}, u32[]{:S(2)}, u32[]{:S(2)}) collective-permute-start(bf16[72,2048]{1,0:T(8,128)(2,1)} %get-tuple-element.143), channel_id=1, source_target_pairs={{0,4},{1,8},{2,12},{3,0},{4,5},{5,9},{6,13},{7,1},{8,6},{9,10},{10... | collective-permute-start | bytes 884744 | tf_op jit(solution)/shard_map/ppermute | solution.py:346
  46.7 28.4 %collective-permute-start.10 = (bf16[72,2048]{1,0:T(8,128)(2,1)}, bf16[72,2048]{1,0:T(8,128)(2,1)S(1)}, u32[]{:S(2)}, u32[]{:S(2)}) collective-permute-start(bf16[72,2048]{1,0:T(8,128)(2,1)} %get-tuple-element.143), channel_id=1, source_target_pairs={{0,8},{1,12},{2,0},{3,4},{4,9},{5,13},{6,1},{7,5},{8,10},{9,14},{1... | collective-permute-start | bytes 884744 | tf_op jit(solution)/shard_map/ppermute | solution.py:346
  48.9 26.2 %collective-permute-start.11 = (bf16[72,2048]{1,0:T(8,128)(2,1)}, bf16[72,2048]{1,0:T(8,128)(2,1)S(1)}, u32[]{:S(2)}, u32[]{:S(2)}) collective-permute-start(bf16[72,2048]{1,0:T(8,128)(2,1)} %get-tuple-element.143), channel_id=1, source_target_pairs={{0,12},{1,0},{2,4},{3,8},{4,13},{5,1},{6,5},{7,9},{8,14},{9,2},{10... | collective-permute-start | bytes 884744 | tf_op jit(solution)/shard_map/ppermute | solution.py:346
  60.9 2.9 %collective-permute-start.1 = (bf16[2,288,1024]{2,1,0:T(8,128)(2,1)S(1)}, bf16[2,288,1024]{2,1,0:T(8,128)(2,1)S(1)}, u32[]{:S(2)}, u32[]{:S(2)}) collective-permute-start(bf16[2,288,1024]{2,1,0:T(8,128)(2,1)S(1)} %get-tuple-element.47), channel_id=1, source_target_pairs={{0,1},{1,0},{2,3},{3,2},{4,5},{5,4},{6,7},{7,6},{8,9},{9,8},{10,11... | collective-permute-start | bytes 3538952 | tf_op jit(solution)/shard_map/cond/branch_1_fun/ppermute | solution.py:409
  65.3 33.1 %collective-permute-start.16 = (bf16[2,288,1024]{2,1,0:T(8,128)(2,1)}, bf16[2,288,1024]{2,1,0:T(8,128)(2,1)}, u32[]{:S(2)}, u32[]{:S(2)}) collective-permute-start(bf16[2,288,1024]{2,1,0:T(8,128)(2,1)} %get-tuple-element.105), channel_id=1, source_target_pairs={{0,2},{1,3},{2,0},{3,1},{4,6},{5,7},{6,4},{7,5},{8,10},{9,11},{10,... | collective-permute-start | bytes 3538952 | tf_op jit(solution)/shard_map/ppermute | solution.py:416
  82.7 15.7 %collective-permute-start.15 = (bf16[2,288,1024]{2,1,0:T(8,128)(2,1)}, bf16[2,288,1024]{2,1,0:T(8,128)(2,1)}, u32[]{:S(2)}, u32[]{:S(2)}) collective-permute-start(bf16[2,288,1024]{2,1,0:T(8,128)(2,1)} %get-tuple-element.104), channel_id=1, source_target_pairs={{0,1},{1,0},{2,3},{3,2},{4,5},{5,4},{6,7},{7,6},{8,9},{9,8},{10,11... | collective-permute-start | bytes 3538952 | tf_op jit(solution)/shard_map/ppermute | solution.py:420
  82.9 3.7 %collective-permute-start.12 = (bf16[144,1024]{1,0:T(8,128)(2,1)}, bf16[144,1024]{1,0:T(8,128)(2,1)S(1)}, u32[]{:S(2)}, u32[]{:S(2)}) collective-permute-start(bf16[144,1024]{1,0:T(8,128)(2,1)} %get-tuple-element.96), channel_id=1, source_target_pairs={{0,1},{1,0},{2,3},{3,2},{4,5},{5,4},{6,7},{7,6},{8,9},{9,8},{10,11... | collective-permute-start | bytes 884744 | tf_op jit(solution)/shard_map/ppermute | solution.py:423
  83.7 5.1 %collective-permute-start.13 = (bf16[144,1024]{1,0:T(8,128)(2,1)S(1)}, bf16[144,1024]{1,0:T(8,128)(2,1)S(1)}, u32[]{:S(2)}, u32[]{:S(2)}) collective-permute-start(bf16[144,1024]{1,0:T(8,128)(2,1)S(1)} %get-tuple-element.98), channel_id=1, source_target_pairs={{0,1},{1,0},{2,3},{3,2},{4,5},{5,4},{6,7},{7,6},{8,9},{9,8},{10,11... | collective-permute-start | bytes 884744 | tf_op jit(solution)/shard_map/ppermute | solution.py:423
  84.3 5.3 %copy-start = (bf16[288,2048]{1,0:T(8,128)(2,1)S(1)}, bf16[288,2048]{1,0:T(8,128)(2,1)}, u32[]{:S(2)}) copy-start(bf16[288,2048]{1,0:T(8,128)(2,1)} %get-tuple-element.100) | copy-start | bytes 3538948
  87.4 14.4 %collective-permute-start.14 = (bf16[144,1024]{1,0:T(8,128)(2,1)}, bf16[144,1024]{1,0:T(8,128)(2,1)S(1)}, u32[]{:S(2)}, u32[]{:S(2)}) collective-permute-start(bf16[144,1024]{1,0:T(8,128)(2,1)} %add_convert_fusion.2), channel_id=1, source_target_pairs={{0,2},{1,3},{2,0},{3,1},{4,6},{5,7},{6,4},{7,5},{8,10},{9,11},{10,... | collective-permute-start | bytes 884744 | tf_op jit(solution)/shard_map/ppermute | solution.py:437
  88.8 19.2 %collective-permute-start.19 = (bf16[144,1024]{1,0:T(8,128)(2,1)S(1)}, bf16[144,1024]{1,0:T(8,128)(2,1)S(1)}, u32[]{:S(2)}, u32[]{:S(2)}) collective-permute-start(bf16[144,1024]{1,0:T(8,128)(2,1)S(1)} %add_convert_fusion.1), channel_id=1, source_target_pairs={{0,2},{1,3},{2,0},{3,1},{4,6},{5,7},{6,4},{7,5},{8,10},{9,11},{10,... | collective-permute-start | bytes 884744 | tf_op jit(solution)/shard_map/ppermute | solution.py:437
  95.8 2.1 %collective-permute-start = (bf16[288,1024]{1,0:T(8,128)(2,1)S(1)}, bf16[288,1024]{1,0:T(8,128)(2,1)S(1)}, u32[]{:S(2)}, u32[]{:S(2)}) collective-permute-start(bf16[288,1024]{1,0:T(8,128)(2,1)S(1)} %get-tuple-element.56), channel_id=1, source_target_pairs={{0,1},{1,0},{2,3},{3,2},{4,5},{5,4},{6,7},{7,6},{8,9},{9,8},{10,11... | collective-permute-start | bytes 1769480 | tf_op jit(solution)/shard_map/cond/branch_1_fun/ppermute | solution.py:428
  102.2 19.4 %collective-permute-start.17 = (bf16[2,144,1024]{2,1,0:T(8,128)(2,1)S(1)}, bf16[2,144,1024]{2,1,0:T(8,128)(2,1)S(1)}, u32[]{:S(2)}, u32[]{:S(2)}) collective-permute-start(bf16[2,144,1024]{2,1,0:T(8,128)(2,1)S(1)} %pad_maximum_fusion.1.mine_a), channel_id=1, source_target_pairs={{0,2},{1,3},{2,0},{3,1},{4,6},{5,7},{6,4},{7,5},{8,10},{9,11},{10,... | collective-permute-start | bytes 1769480 | tf_op jit(solution)/shard_map/ppermute | solution.py:443
  104.7 8.0 %collective-permute-start.18 = (bf16[2,144,1024]{2,1,0:T(8,128)(2,1)S(1)}, bf16[2,144,1024]{2,1,0:T(8,128)(2,1)S(1)}, u32[]{:S(2)}, u32[]{:S(2)}) collective-permute-start(bf16[2,144,1024]{2,1,0:T(8,128)(2,1)S(1)} %pad_maximum_fusion.1.mine_a), channel_id=1, source_target_pairs={{0,1},{1,0},{2,3},{3,2},{4,5},{5,4},{6,7},{7,6},{8,9},{9,8},{10,11... | collective-permute-start | bytes 1769480 | tf_op jit(solution)/shard_map/ppermute | solution.py:442
  108.4 4.2 %collective-permute-start.20 = (bf16[2,144,1024]{2,1,0:T(8,128)(2,1)S(1)}, bf16[2,144,1024]{2,1,0:T(8,128)(2,1)S(1)}, u32[]{:S(2)}, u32[]{:S(2)}) collective-permute-start(bf16[2,144,1024]{2,1,0:T(8,128)(2,1)S(1)} %pad_maximum_fusion.2.mine_b), channel_id=1, source_target_pairs={{0,1},{1,0},{2,3},{3,2},{4,5},{5,4},{6,7},{7,6},{8,9},{9,8},{10,11... | collective-permute-start | bytes 1769480 | tf_op jit(solution)/shard_map/ppermute | solution.py:442
  110.1 24.0 %collective-permute-start.25 = (bf16[2,144,1024]{2,1,0:T(8,128)(2,1)S(1)}, bf16[2,144,1024]{2,1,0:T(8,128)(2,1)S(1)}, u32[]{:S(2)}, u32[]{:S(2)}) collective-permute-start(bf16[2,144,1024]{2,1,0:T(8,128)(2,1)S(1)} %pad_maximum_fusion.2.mine_b), channel_id=1, source_target_pairs={{0,2},{1,3},{2,0},{3,1},{4,6},{5,7},{6,4},{7,5},{8,10},{9,11},{10,... | collective-permute-start | bytes 1769480 | tf_op jit(solution)/shard_map/ppermute | solution.py:443
  121.6 2.1 %collective-permute-start.21 = (bf16[2,144,1024]{2,1,0:T(8,128)(2,1)S(1)}, bf16[2,144,1024]{2,1,0:T(8,128)(2,1)S(1)}, u32[]{:S(2)}, u32[]{:S(2)}) collective-permute-start(bf16[2,144,1024]{2,1,0:T(8,128)(2,1)S(1)} %collective-permute-done.17.mine), channel_id=1, source_target_pairs={{0,1},{1,0},{2,3},{3,2},{4,5},{5,4},{6,7},{7,6},{8,9},{9,8},{10,11... | collective-permute-start | bytes 1769480 | tf_op jit(solution)/shard_map/ppermute | solution.py:448
  134.1 3.6 %collective-permute-start.26 = (bf16[2,144,1024]{2,1,0:T(8,128)(2,1)S(1)}, bf16[2,144,1024]{2,1,0:T(8,128)(2,1)S(1)}, u32[]{:S(2)}, u32[]{:S(2)}) collective-permute-start(bf16[2,144,1024]{2,1,0:T(8,128)(2,1)S(1)} %collective-permute-done.25.mine), channel_id=1, source_target_pairs={{0,1},{1,0},{2,3},{3,2},{4,5},{5,4},{6,7},{7,6},{8,9},{9,8},{10,11... | collective-permute-start | bytes 1769480 | tf_op jit(solution)/shard_map/ppermute | solution.py:448
  134.4 17.5 %collective-permute-start.24 = (bf16[48,2048]{1,0:T(8,128)(2,1)S(1)}, bf16[48,2048]{1,0:T(8,128)(2,1)S(1)}, u32[]{:S(2)}, u32[]{:S(2)}) collective-permute-start(bf16[48,2048]{1,0:T(8,128)(2,1)S(1)} %get-tuple-element.112), channel_id=1, source_target_pairs={{0,8},{4,12},{8,0},{12,4},{1,9},{5,13},{9,1},{13,5},{2,10},{6,14},... | collective-permute-start | bytes 589832 | tf_op jit(solution)/shard_map/ppermute | solution.py:453
  135.6 16.7 %collective-permute-start.23 = (bf16[48,2048]{1,0:T(8,128)(2,1)S(1)}, bf16[48,2048]{1,0:T(8,128)(2,1)S(1)}, u32[]{:S(2)}, u32[]{:S(2)}) collective-permute-start(bf16[48,2048]{1,0:T(8,128)(2,1)S(1)} %get-tuple-element.111), channel_id=1, source_target_pairs={{0,12},{4,0},{8,4},{12,8},{1,13},{5,1},{9,5},{13,9},{2,14},{6,2},{... | collective-permute-start | bytes 589832 | tf_op jit(solution)/shard_map/ppermute | solution.py:453
  137.5 14.9 %collective-permute-start.22 = (bf16[48,2048]{1,0:T(8,128)(2,1)S(1)}, bf16[48,2048]{1,0:T(8,128)(2,1)S(1)}, u32[]{:S(2)}, u32[]{:S(2)}) collective-permute-start(bf16[48,2048]{1,0:T(8,128)(2,1)S(1)} %get-tuple-element.110), channel_id=1, source_target_pairs={{0,4},{4,8},{8,12},{12,0},{1,5},{5,9},{9,13},{13,1},{2,6},{6,10},{... | collective-permute-start | bytes 589832 | tf_op jit(solution)/shard_map/ppermute | solution.py:453
  148.1 19.9 %collective-permute-start.29 = (bf16[48,2048]{1,0:T(8,128)(2,1)S(1)}, bf16[48,2048]{1,0:T(8,128)(2,1)S(1)}, u32[]{:S(2)}, u32[]{:S(2)}) collective-permute-start(bf16[48,2048]{1,0:T(8,128)(2,1)S(1)} %get-tuple-element.118), channel_id=1, source_target_pairs={{0,8},{4,12},{8,0},{12,4},{1,9},{5,13},{9,1},{13,5},{2,10},{6,14},... | collective-permute-start | bytes 589832 | tf_op jit(solution)/shard_map/ppermute | solution.py:453
  149.8 18.2 %collective-permute-start.28 = (bf16[48,2048]{1,0:T(8,128)(2,1)S(1)}, bf16[48,2048]{1,0:T(8,128)(2,1)S(1)}, u32[]{:S(2)}, u32[]{:S(2)}) collective-permute-start(bf16[48,2048]{1,0:T(8,128)(2,1)S(1)} %get-tuple-element.117), channel_id=1, source_target_pairs={{0,12},{4,0},{8,4},{12,8},{1,13},{5,1},{9,5},{13,9},{2,14},{6,2},{... | collective-permute-start | bytes 589832 | tf_op jit(solution)/shard_map/ppermute | solution.py:453
  151.9 16.1 %collective-permute-start.27 = (bf16[48,2048]{1,0:T(8,128)(2,1)S(1)}, bf16[48,2048]{1,0:T(8,128)(2,1)S(1)}, u32[]{:S(2)}, u32[]{:S(2)}) collective-permute-start(bf16[48,2048]{1,0:T(8,128)(2,1)S(1)} %get-tuple-element.116), channel_id=1, source_target_pairs={{0,4},{4,8},{8,12},{12,0},{1,5},{5,9},{9,13},{13,1},{2,6},{6,10},{... | collective-permute-start | bytes 589832 | tf_op jit(solution)/shard_map/ppermute | solution.py:453
  (1 other events, 0.7 us)
